TPU v7x, 512 devices: a whole 4x8x8 slice. The times are simulated.
512 devices in a mesh: member: 4 (over x), shard: 128 (over y, z, core).
Axes of the slice: x: 4, y: 8, z: 8, core: 2. Of those that a mesh axis runs over, the one named last changes fastest.
Arguments:
- teacher_hidden: bfloat16 [4, 2048, 4096], P('member', 'shard'), may hold values from -80 to 80
- teacher_gain: float32 [4, 4096], P('member'), may hold values from 0.1 to 1.9
- teacher_head: bfloat16 [4, 4096, 65536], P('member', None, 'shard'), may hold values from -0.5 to 0.5
- student_hidden: bfloat16 [2048, 2048], P('shard', 'member'), may hold values from -8 to 8
- student_head: bfloat16 [2048, 65536], P('member', 'shard'), may hold values from -0.6 to 0.6
- positions: int32 [128, 4], P('shard'), may hold values from 0 to 15, as said below
- counts: int32 [128], replicated, may hold values from 1 to 4, 256 in all
- targets: int32 [512], replicated, may hold values from 0 to 65535
Outputs:
- mean_loss: float32 [], replicated
- hidden_grad: bfloat16 [2048, 2048], P('shard', 'member')
Inputs may be any that keep to these rules, and one draw needn't show every extreme that they name: Each owner's positions are distinct. The counts sum to exactly 256.
All inputs are finite; a program needn't handle non-finite values.
Results may differ from a plain program's by a relative error of at most 0.0039.
Values may be sent and summed in bfloat16 or wider, within the bound.
No kernel may reach another device: no remote copies, remote signals or barrier semaphores. Data moves between devices by JAX's collectives and lax.ppermute only.
A program may use at most 64 MiB of HBM per device.

v0:
```python
import jax
import jax.numpy as jnp
from jax import lax
from jax.sharding import PartitionSpec as P

LOSS_SCALE = 16.0
BLEND = 0.5
EPS = 1e-05


def vocab_stats(logits):
    local_top = jnp.max(logits, axis=1)
    highest = lax.pmax(local_top, "shard")
    totals = lax.psum(jnp.sum(jnp.exp(logits - highest[:, None]), axis=1), "shard")
    return (highest, totals)


def on_device(
    teacher_hidden,
    teacher_gain,
    teacher_head,
    student_hidden,
    student_head,
    positions,
    counts,
    targets,
):
    owners = lax.axis_size("shard")
    members = lax.axis_size("member")
    owner_rank = lax.axis_index("shard")
    slot_ids = positions[0]
    per_owner = slot_ids.shape[0]
    vocab_part = student_head.shape[1]
    window_rows = student_hidden.shape[0]
    widened = jnp.take(teacher_hidden[0], slot_ids, axis=0).astype(jnp.float32)
    inverse_rms = lax.rsqrt(jnp.mean(widened * widened, axis=1, keepdims=True) + EPS)
    normed = (widened * inverse_rms * teacher_gain[0][None, :]).astype(jnp.bfloat16)
    student_picked = jnp.take(student_hidden, slot_ids, axis=0)
    teacher_rows, student_rows = (
        lax.all_gather(normed, "shard", axis=0, tiled=True),
        lax.all_gather(student_picked, "shard", axis=0, tiled=True),
    )
    padded_rows = per_owner * owners
    padded_ids = jnp.arange(padded_rows, dtype=jnp.int32)
    padded_slot = padded_ids % per_owner
    owner_counts = jnp.repeat(counts, per_owner, total_repeat_length=padded_rows)
    padded_weight = (padded_slot < owner_counts).astype(jnp.float32)
    teacher_logits = jnp.dot(teacher_rows, teacher_head[0], preferred_element_type=jnp.float32)
    highest, totals = vocab_stats(teacher_logits)
    teacher_probs = jnp.exp(teacher_logits - highest[:, None]) / totals[:, None]
    partial_logits = jnp.dot(student_rows, student_head, preferred_element_type=jnp.float32)
    student_logits, prob_sums = lax.psum((partial_logits, teacher_probs), "member")
    mean_probs = prob_sums / members
    highest, totals = vocab_stats(student_logits)
    log_total = highest + jnp.log(totals)
    vocab_ids = owner_rank * vocab_part + jnp.arange(vocab_part, dtype=jnp.int32)
    onehot = (vocab_ids[None, :] == targets[:, None]).astype(jnp.float32)
    mixture = BLEND * onehot + (1.0 - BLEND) * mean_probs
    cross_part = jnp.sum(padded_weight * jnp.sum(mixture * student_logits, axis=1))
    lse_part = jnp.where(owner_rank == 0, jnp.sum(padded_weight * log_total), 0.0)
    loss_term = lse_part - cross_part
    slope_rows = (
        LOSS_SCALE
        * padded_weight[:, None]
        * (jnp.exp(student_logits - log_total[:, None]) - mixture)
    ).astype(jnp.bfloat16)
    loss_total = lax.psum(loss_term, "shard")
    mean_loss = loss_total / jnp.sum(counts).astype(jnp.float32)
    chosen = lax.slice_in_dim(slope_rows, 0, per_owner * lax.axis_size("shard"), axis=0)
    slot_grad = lax.psum_scatter(
        lax.dot_general(
            chosen, student_head, (((1,), (1,)), ((), ())), preferred_element_type=jnp.float32
        ),
        "shard",
        scatter_dimension=0,
        tiled=True,
    )
    placed = (jnp.arange(window_rows, dtype=jnp.int32)[:, None] == slot_ids[None, :]).astype(
        jnp.float32
    )
    hidden_grad = jnp.sum(placed[:, :, None] * slot_grad[None, :, :], axis=1).astype(jnp.bfloat16)
    return (mean_loss, hidden_grad)


def solution(mesh):
    placed = (
        P("member", "shard", None),
        P("member", None),
        P("member", None, "shard"),
        P("shard", "member"),
        P("member", "shard"),
        P("shard", None),
        P(),
        P(),
    )
    return jax.shard_map(
        on_device,
        mesh=mesh,
        in_specs=placed,
        out_specs=(P(), P("shard", "member")),
        check_vma=False,
    )
```

profile of v0, /device:TPU:1, one launch (start us, length us, event | category | flops | bytes accessed | tf_op | source)
XLA Modules:
  0.0 1239.3 jit_solution(6478698741609276838)
XLA Ops:
  8.0 0.0 copy-start
  8.0 0.0 copy-start.3
  8.0 0.0 all-reduce.6.cloned.1.call-start
  8.1 0.7 fusion.23
  8.8 0.7 compare_and_fusion
  9.5 1.3 gather_fusion.1
  10.7 0.1 select_bitcast_fusion
  10.8 58.9 %all-gather = bf16[128,4,512]{2,1,0:T(4,128)(2,1)S(1)} all-gather(bf16[1,4,512]{2,1,0:T(4,128)(2,1)S(1)} %select_bitcast_fusion), channel_id=1, replica_groups=mesh['member'=4,'shard'=128] {'shard'}, dimensions={0}, use_global_device_ids=true | all-gather | bytes 528384 | tf_op jit(solution)/shard_map/all_gather | solution.py:41
  69.8 0.1 reshape.234
  69.9 1.4 fusion.29
  71.3 0.0 all-reduce.6.cloned.1.call-update
  71.3 0.0 all-gather.4.cloned.1.call-start
  71.4 0.6 gather_fusion.2
  72.0 0.2 fusion.12
  72.2 0.7 fusion.15
  72.9 0.0 all-gather.4.cloned.1.call-update
  72.9 0.0 all-reduce.8.cloned.1.call-start
  73.0 48.6 %all-reduce.6.cloned.1.call-done = f32[512,512]{1,0:T(8,128)} async-done(((f32[512,512]{1,0:T(8,128)}), f32[512,512]{1,0:T(8,128)}) %all-reduce.6.cloned.1.call-update) | async-done | bytes 1048592 | tf_op jit(solution)/shard_map/psum | solution.py:52
  121.6 1.4 reduce_max.18
  123.0 32.7 %all-gather.4.cloned.1.call-done = bf16[128,4,4096]{2,1,0:T(4,128)(2,1)} async-done(((bf16[1,4,4096]{2,1,0:T(4,128)(2,1)}), bf16[128,4,4096]{2,1,0:T(4,128)(2,1)}) %all-gather.4.cloned.1.call-update) | async-done | bytes 4194320 | tf_op jit(solution)/shard_map/all_gather | solution.py:40
  155.6 6.9 reshape.236
  162.6 6.8 fusion.28
  169.4 0.0 copy-start.5
  169.4 1.6 copy.13
  171.1 246.4 %all-reduce.1 = (f32[512]{0:T(512)S(1)}, f32[512]{0:T(512)S(1)}) all-reduce(f32[512]{0:T(512)S(1)} %reduce_max.18, f32[512]{0:T(512)S(1)} %get-tuple-element.25), channel_id=1, replica_groups=mesh['member'=4,'shard'=128] {'shard'}, use_global_device_ids=true, to_apply=%region_2.3 | all-reduce | flops 1024 | bytes 8192 | tf_op jit(solution)/shard_map/pmax | solution.py:13
  417.5 0.3 fusion.3
  417.8 249.4 %psum.37 = f32[512]{0:T(512)S(1)} all-reduce(f32[512]{0:T(512)S(1)} %fusion.3), channel_id=1, replica_groups=mesh['member'=4,'shard'=128] {'shard'}, use_global_device_ids=true, to_apply=%region_10.11 | all-reduce | flops 512 | bytes 4096 | tf_op jit(solution)/shard_map/psum | solution.py:14
  667.2 1.3 fusion.2
  668.4 0.0 all-reduce.8.cloned.1.call-update
  668.5 0.0 all-reduce.10.cloned.1.call-start
  668.5 0.1 add_add_fusion.1
  668.6 0.0 copy-start.7
  668.7 3.3 gather_fusion
  672.0 46.3 %all-reduce.8.cloned.1.call-done = f32[512,512]{1,0:T(8,128)} async-done(((f32[512,512]{1,0:T(8,128)}), f32[512,512]{1,0:T(8,128)}) %all-reduce.8.cloned.1.call-update) | async-done | bytes 1048592 | tf_op jit(solution)/shard_map/psum | solution.py:52
  718.4 0.0 copy-done.2
  718.4 1.8 multiply_reduce_fusion
  720.1 249.5 %psum.36 = f32[512]{0:T(512)S(1)} all-reduce(f32[512]{0:T(512)S(1)} %get-tuple-element.15), channel_id=1, replica_groups=mesh['member'=4,'shard'=128] {'shard'}, use_global_device_ids=true, to_apply=%region_4.5 | all-reduce | flops 512 | bytes 4096 | tf_op jit(solution)/shard_map/psum | solution.py:14
  969.6 0.6 broadcast_select_fusion.1
  970.2 0.6 select_reduce_fusion.1
  970.9 2.8 fusion.4
  973.7 0.0 all-reduce.10.cloned.1.call-update
  973.7 0.6 reduce_sum.78
  975.0 1.3 dynamic-slice.6
  976.3 0.1 fusion.22
  978.3 250.4 %psum.39 = f32[]{:T(128)} all-reduce(f32[]{:T(128)S(6)} %sub.51), channel_id=1, replica_groups=mesh['member'=4,'shard'=128] {'shard'}, use_global_device_ids=true, to_apply=%region_14.15 | all-reduce | flops 1 | bytes 8 | tf_op jit(solution)/shard_map/psum | solution.py:67
  1229.3 0.0 all-reduce.10.cloned.1.call-done
  1229.4 0.7 constant_dynamic-slice_fusion
  1230.1 0.7 multiply_reduce_fusion.1
  (17 shorter events, 0.1 us)
Async XLA Ops:
  8.0 61.9 %copy-start = (bf16[512,512]{1,0:T(8,128)(2,1)S(1)}, bf16[512,512]{1,0:T(8,128)(2,1)}, u32[]{:S(2)}) copy-start(bf16[512,512]{1,0:T(8,128)(2,1)} %param.14) | copy-start | bytes 1572868
  8.0 63.4 %copy-start.3 = (bf16[1,16,4096]{2,1,0:T(8,128)(2,1)S(1)}, bf16[1,16,4096]{2,1,0:T(8,128)(2,1)}, u32[]{:S(2)}) copy-start(bf16[1,16,4096]{2,1,0:T(8,128)(2,1)} %param.10) | copy-start | bytes 393220
  8.0 64.2 %copy-start.4 = (f32[1,4096]{1,0:T(1,128)S(1)}, f32[1,4096]{1,0:T(1,128)}, u32[]{:S(2)}) copy-start(f32[1,4096]{1,0:T(1,128)} %param.11) | copy-start | bytes 49156
  8.0 113.6 %all-reduce.6.cloned.1.call-start = ((), (), s32[]{:S(2)}) async-start(), calls=%async_computation | async-start | bytes 2097152 | tf_op jit(solution)/shard_map/psum | solution.py:52
  71.3 84.3 %all-gather.4.cloned.1.call-start = ((), (), s32[]{:S(2)}) async-start(), calls=%async_computation.2 | async-start | bytes 4227072 | tf_op jit(solution)/shard_map/all_gather | solution.py:40
  72.9 645.4 %all-reduce.8.cloned.1.call-start = ((), (), s32[]{:S(2)}) async-start(), calls=%async_computation.1 | async-start | bytes 2097152 | tf_op jit(solution)/shard_map/psum | solution.py:52
  169.4 499.2 %copy-start.6 = (s32[4,128]{1,0:T(4,128)S(1)}, s32[4,128]{1,0:T(4,128)}, u32[]{:S(2)}) copy-start(s32[4,128]{1,0:T(4,128)} %constant.159.clone.1) | copy-start | bytes 6148
  169.4 499.3 %copy-start.1 = (s32[128]{0:T(128)S(1)}, s32[128]{0:T(128)}, u32[]{:S(2)}) copy-start(s32[128]{0:T(128)} %param.16) | copy-start | bytes 1540
  169.4 549.0 %copy-start.2 = (f32[512,512]{1,0:T(8,128)S(1)}, f32[512,512]{1,0:T(8,128)}, u32[]{:S(2)}) copy-start(f32[512,512]{1,0:T(8,128)} %all-reduce.6.cloned.1.call-done) | copy-start | bytes 3145732
  169.4 549.0 %copy-start.5 = (s32[512]{0:T(512)S(1)}, s32[512]{0:T(512)}, u32[]{:S(2)}) copy-start(s32[512]{0:T(512)} %param.17) | copy-start | bytes 6148
  668.5 560.9 %all-reduce.10.cloned.1.call-start = ((), (), s32[]{:S(2)}) async-start(), calls=%async_computation.3 | async-start | bytes 2097152
  668.6 307.6 %copy-start.7 = (s32[1,4]{1,0:T(1,128)S(1)}, s32[1,4]{1,0:T(1,128)}, u32[]{:S(2)}) copy-start(s32[1,4]{1,0:T(1,128)} %param.15) | copy-start | bytes 52
Sparse Core Ops, SparseCore 0:
  71.5 50.0 all-reduce.5
  668.6 49.7 all-reduce.7
Sparse Core Ops, SparseCore 1:
  75.4 80.2 all-gather.3
  973.8 190.7 all-reduce.9
where the time goes:
time: 1240 us
  blocking collectives  1050 us (85%)
  waiting for transfers between devices  128 us (10%)
  between operations  20 us (2%)
  local copies, waits for them, and re-layouts  15.9 us (1%)
    psum x2, blocking collectives, vocab_stats(): lax.psum(jnp.sum(jnp.exp(logits - highest[:, None]), axis=1), 'shard')  499 us
    psum x1, blocking collectives, on_device(): loss_total = lax.psum(loss_term, 'shard')  250 us
    pmax x1, blocking collectives, vocab_stats(): highest = lax.pmax(local_top, 'shard')  246 us
    psum x2, waiting for transfers between devices, on_device(): lax.psum((partial_logits, teacher_probs), 'member')  94.9 us
    all_gather x1, blocking collectives, on_device(): lax.all_gather(student_picked, 'shard', axis=0, tiled=True)  58.9 us
    all_gather x1, waiting for transfers between devices, on_device(): lax.all_gather(normed, 'shard', axis=0, tiled=True)  32.7 us
  transfers between devices with their start and end apart: 4, of which 3 were waited for; matrix products, arithmetic and copies ran while one was open for 1% of the time, Pallas kernels for 0%

commit v1 on v0

v1 whole, which is shorter than its diff:
```python
import jax
import jax.numpy as jnp
from jax import lax
from jax.sharding import Mesh
from jax.sharding import PartitionSpec as P

LOSS_SCALE = 16.0
BLEND = 0.5
EPS = 1e-05
CHIPS = ("y", "z")
OWNERS = ("y", "z", "core")
BF16 = jnp.bfloat16
F32 = jnp.float32


def spread(block, axes, size):
    return lax.all_to_all(
        jnp.broadcast_to(block[None], (size,) + block.shape), axes, 0, 0, tiled=True
    )


def softmax_stats(logits):
    top = jnp.max(logits, axis=1)
    shifted = jnp.exp(logits - top[:, None])
    return top, shifted, jnp.sum(shifted, axis=1)


def global_stats(top, total, owners):
    rows = top.shape[0]
    mine = jnp.concatenate([top, total]).reshape(2 * rows // 128, 128)
    every = spread(mine, OWNERS, owners).reshape(owners, 2 * rows)
    tops, totals = every[:, :rows], every[:, rows:]
    highest = jnp.max(tops, axis=0)
    return highest, jnp.sum(totals * jnp.exp(tops - highest[None, :]), axis=0)


def three_parts(value):
    high = value.astype(BF16)
    rest = value - high.astype(F32)
    middle = rest.astype(BF16)
    low = (rest - middle.astype(F32)).astype(BF16)
    return jnp.stack([high, middle, low])


def on_device(
    teacher_hidden,
    teacher_gain,
    teacher_head,
    student_hidden,
    student_head,
    positions,
    counts,
    targets,
):
    members = lax.axis_size("member")
    chips = lax.axis_size("y") * lax.axis_size("z")
    cores = lax.axis_size("core")
    owners = chips * cores
    member = lax.axis_index("member")
    core = lax.axis_index("core")
    owner = lax.axis_index(OWNERS)
    slot_ids = positions[0]
    cap = slot_ids.shape[0]
    window, width = student_hidden.shape
    vocab = student_head.shape[1]
    padded = owners * cap
    live_rows = padded // 2
    chunk = live_rows // members

    widened = jnp.take(teacher_hidden[0], slot_ids, axis=0).astype(F32)
    inverse_rms = lax.rsqrt(jnp.mean(widened * widened, axis=1, keepdims=True) + EPS)
    normed = (widened * inverse_rms * teacher_gain[0][None, :]).astype(BF16)
    picked = jnp.take(student_hidden, slot_ids, axis=0)
    depth = normed.shape[1]
    both = lax.all_gather(jnp.concatenate([normed, picked], axis=1), "core", axis=0, tiled=True)
    teacher_rows = lax.all_gather(both[:, :depth], CHIPS, axis=0, tiled=True)

    earlier = (
        jnp.arange(owners, dtype=jnp.int32)[:, None] < jnp.arange(owners, dtype=jnp.int32)[None, :]
    )
    starts = jnp.sum(jnp.where(earlier, counts[:, None], 0), axis=0)
    slots = jnp.arange(cap, dtype=jnp.int32)
    places = jnp.where(
        slots[None, :] < counts[:, None], starts[:, None] + slots[None, :], -1
    )
    packed_ids = jnp.arange(live_rows, dtype=jnp.int32)
    pack_mask = packed_ids[:, None] == places.reshape(1, padded)
    pack = pack_mask.astype(BF16)
    live_targets = jnp.sum(jnp.where(pack_mask, targets[None, :], 0), axis=1)

    student_rows = spread(both[:, depth:], CHIPS, chips).reshape(padded, width)
    student_live = jnp.dot(pack, student_rows, preferred_element_type=F32).astype(BF16)
    partial_logits = jnp.dot(student_live, student_head, preferred_element_type=F32)
    student_logits = jnp.sum(
        lax.all_to_all(
            partial_logits.reshape(members, chunk, vocab), "member", 0, 0, tiled=True
        ),
        axis=0,
    )
    top, _, total = softmax_stats(student_logits)
    highest, totals = global_stats(top, total, owners)
    log_total = highest + jnp.log(totals)
    student_probs = jnp.exp(student_logits - log_total[:, None])
    chunk_targets = lax.dynamic_slice_in_dim(live_targets, member * chunk, chunk)
    vocab_ids = owner * vocab + jnp.arange(vocab, dtype=jnp.int32)
    onehot = (vocab_ids[None, :] == chunk_targets[:, None]).astype(F32)

    teacher_live = jnp.dot(pack, teacher_rows, preferred_element_type=F32).astype(BF16)
    teacher_logits = jnp.dot(teacher_live, teacher_head[0], preferred_element_type=F32)
    top, shifted, total = softmax_stats(teacher_logits)
    highest, totals = global_stats(top, total, owners)
    factor = jnp.exp(top - highest) / totals
    teacher_probs = (shifted * factor[:, None]).astype(BF16)
    mean_probs = (
        jnp.sum(
            lax.all_to_all(
                teacher_probs.reshape(members, chunk, vocab), "member", 0, 0, tiled=True
            ).astype(F32),
            axis=0,
        )
        / members
    )
    mixture = BLEND * onehot + (1.0 - BLEND) * mean_probs
    loss = jnp.where(owner == 0, jnp.sum(log_total), 0.0) - jnp.sum(mixture * student_logits)
    slope = (LOSS_SCALE * (student_probs - mixture)).astype(BF16)
    tail = jnp.zeros((16, vocab), BF16)
    tail = lax.dynamic_update_slice(tail, three_parts(loss)[None, :], (0, 0))
    slopes = spread(jnp.concatenate([slope, tail], axis=0), "member", members)
    shard_loss = jnp.sum(slopes[:, chunk, :3].astype(F32))
    slope_live = slopes[:, :chunk].reshape(live_rows, vocab)

    halves = 2
    half = width // halves

    def term(which_core):
        chosen = jnp.take(places.reshape(chips, cores, cap), which_core, axis=1)
        result = 0.0
        for part in range(halves):
            here = jnp.arange(halves, dtype=jnp.int32)[None, :, None] == part
            at = jnp.where(here, chosen[:, None, :], -1).reshape(chips * halves * cap, 1)
            unpack = (at == packed_ids[None, :]).astype(BF16)
            rows = jnp.dot(unpack, slope_live, preferred_element_type=F32).astype(BF16)
            result = result + lax.dot_general(
                rows,
                student_head[part * half : (part + 1) * half],
                (((1,), (1,)), ((), ())),
                preferred_element_type=F32,
            )
        return result

    swap = [(0, 1), (1, 0)]
    arrived = lax.ppermute(term(1 - core), "core", swap)
    other_loss = lax.ppermute(jnp.full((8, 128), shard_loss, F32), "core", swap)
    grads = (term(core) + arrived).reshape(chips, halves * cap, half)
    chip_loss = jnp.broadcast_to((shard_loss + other_loss[0, 0])[None, None, None], (chips, 8, half))
    owned = jnp.sum(
        lax.all_to_all(
            jnp.concatenate([grads, chip_loss], axis=1), CHIPS, 0, 0, tiled=True
        ),
        axis=0,
    )
    mean_loss = owned[halves * cap, 0] / jnp.sum(counts).astype(F32)
    slot_grad = jnp.concatenate(
        [owned[part * cap : (part + 1) * cap] for part in range(halves)], axis=1
    )
    live_here = slots < lax.dynamic_index_in_dim(counts, owner, keepdims=False)
    placed = (
        (jnp.arange(window, dtype=jnp.int32)[:, None] == slot_ids[None, :]) & live_here[None, :]
    ).astype(F32)
    hidden_grad = jnp.sum(placed[:, :, None] * slot_grad[None, :, :], axis=1).astype(BF16)
    return (mean_loss, hidden_grad)


def solution(mesh):
    fine = Mesh(mesh.devices.reshape(4, 8, 8, 2), ("member", "y", "z", "core"))
    placed = (
        P("member", OWNERS, None),
        P("member", None),
        P("member", None, OWNERS),
        P(OWNERS, "member"),
        P("member", OWNERS),
        P(OWNERS, None),
        P(),
        P(),
    )
    return jax.shard_map(
        on_device,
        mesh=fine,
        in_specs=placed,
        out_specs=(P(), P(OWNERS, "member")),
        check_vma=False,
    )
```

time: 1240 us -> 258 us (0.21)
  blocking collectives: 1050 us -> 8.39 us
  starting transfers between devices: 0.17 us -> 55.6 us
  waiting for transfers between devices: 128 us -> 142 us
    psum x3 -> x0, blocking collectives: 749 us -> none  [the longest x2 499 us: vocab_stats(): lax.psum(jnp.sum(jnp.exp(logits - highest[:, None]), axis=1), 'shard')]
    pmax x1 -> x0, blocking collectives: 246 us -> none  [vocab_stats(): highest = lax.pmax(local_top, 'shard')]
    psum x2 -> x0, waiting for transfers between devices: 94.9 us -> none  [on_device(): lax.psum((partial_logits, teacher_probs), 'member')]
    all_to_all x0 -> x7, waiting for transfers between devices: none -> 66.6 us  [the longest x4 30 us: spread(): lax.all_to_all(jnp.broadcast_to(block[None], (size,) + block.shape), axes...]
    all_gather x1, blocking collectives: 58.9 us -> 8.39 us  [on_device(): lax.all_gather(jnp.concatenate([normed, picked], axis=1), 'core', axis=0,...]
    all_to_all x0 -> x7, starting transfers between devices: none -> 50 us  [the longest x4 38 us: spread(): lax.all_to_all(jnp.broadcast_to(block[None], (size,) + block.shape), axes...]
    all_gather x1, waiting for transfers between devices: 32.7 us -> 75.1 us  [on_device(): teacher_rows = lax.all_gather(both[:, :depth], CHIPS, axis=0, tiled=True)]
  transfers between devices with their start and end apart: 4 -> 10, of which waited for: 3 -> 8; matrix products, arithmetic and copies ran while one was open for 1% -> 7% of each run, Pallas kernels for 0% -> 0%
where the time goes in v1:
time: 258 us; the launch traced here: 255 us
  waiting for transfers between devices  142 us (55%)
  starting transfers between devices  55.6 us (22%)
  between operations  19.4 us (8%)
  other arithmetic  10.4 us (4%)
  local copies, waits for them, and re-layouts  10 us (4%)
  matrix products  9.14 us (4%)
  blocking collectives  8.39 us (3%)
    all_gather x1, waiting for transfers between devices, on_device(): teacher_rows = lax.all_gather(both[:, :depth], CHIPS, axis=0, tiled=True)  75.1 us
    all_to_all x4, starting transfers between devices, spread(): lax.all_to_all(jnp.broadcast_to(block[None], (size,) + block.shape), axes...  38 us
    all_to_all x4, waiting for transfers between devices, spread(): lax.all_to_all(jnp.broadcast_to(block[None], (size,) + block.shape), axes...  30 us
    all_to_all x1, waiting for transfers between devices, on_device(): lax.all_to_all(jnp.concatenate([grads, chip_loss], axis=1), CHIPS, 0, 0,...  25.3 us
    all_gather x1, blocking collectives, on_device(): lax.all_gather(jnp.concatenate([normed, picked], axis=1), 'core', axis=0,...  8.39 us
    all_to_all x1, waiting for transfers between devices, on_device(): lax.all_to_all(partial_logits.reshape(members, chunk, vocab), 'member', 0...  6.16 us
    dot_general x1, matrix products, on_device(): jnp.dot(teacher_live, teacher_head[0], preferred_element_type=F32)  5.88 us
  transfers between devices with their start and end apart: 10, of which 8 were waited for; matrix products, arithmetic and copies ran while one was open for 7% of the time, Pallas kernels for 0%

profile of v1, /device:TPU:1, one launch (start us, length us, event | category | flops | bytes accessed | tf_op | source)
XLA Modules:
  0.0 255.3 jit_solution(4876132610921427669)
XLA Ops:
  7.2 0.7 fusion.39
  7.9 0.7 compare_and_fusion
  8.6 0.6 gather_fusion
  9.4 1.3 gather_fusion.1
  10.8 0.8 fusion.35
  11.6 8.4 %all-gather = bf16[2,4,4608]{2,1,0:T(4,128)(2,1)S(1)} all-gather(bf16[1,4,4608]{2,1,0:T(4,128)(2,1)S(1)} %maximum_bitcast_fusion), channel_id=1, replica_groups=mesh['member'=4,'y'=8,'z'=8,'core'=2] {'core'}, dimensions={0}, use_global_device_ids=true | all-gather | bytes 110592 | tf_op jit(solution)/shard_map/all_gather | solution.py:75
  20.0 0.6 slice.74
  20.7 0.8 broadcast_in_dim.183
  21.5 10.9 %all-to-all-start = ((bf16[64,8,512]{2,1,0:T(8,128)(2,1)}), bf16[64,8,512]{2,1,0:T(8,128)(2,1)S(1)}, u32[]{:S(2)}, u32[]{:S(2)}) async-start(bf16[64,8,512]{2,1,0:T(8,128)(2,1)} %broadcast_in_dim.183), calls=%async_computation | async-start | bytes 1048576 | tf_op jit(solution)/shard_map/all_to_all | solution.py:17
  32.5 0.8 select_reduce_fusion.1
  33.2 0.8 add_select_fusion
  34.1 75.1 %all-gather.3.cloned.1.call-done = bf16[512,4096]{1,0:T(8,128)(2,1)} async-done(((bf16[8,4096]{1,0:T(8,128)(2,1)}), bf16[512,4096]{1,0:T(8,128)(2,1)}) %all-gather.3.cloned.1.call-update) | async-done | bytes 4194320 | tf_op jit(solution)/shard_map/all_gather | solution.py:76
  109.2 5.9 %fusion.42 = (f32[256]{0:T(256)S(1)}, f32[256,512]{1,0:T(8,128)S(1)}) fusion(bf16[1,4096,512]{2,1,0:T(8,128)(2,1)} %param.12, bf16[512,4096]{1,0:T(8,128)(2,1)} %all-gather.3.cloned.1.call-done, s32[512]{0:T(512)S(1)} %select_n.112), kind=kOutput, calls=%fused_computation.96 | convolution fusion | flops 2148794112 | bytes 8915968 | tf_op jit(solution)/shard_map/dot_general | solution.py:109
  115.3 0.7 broadcast_in_dim.187
  116.0 13.6 %all-to-all-start.3 = ((f32[128,4,128]{2,1,0:T(4,128)}), f32[128,4,128]{2,1,0:T(4,128)S(1)}, u32[]{:S(2)}, u32[]{:S(2)}) async-start(f32[128,4,128]{2,1,0:T(4,128)} %broadcast_in_dim.187), calls=%async_computation.3 | async-start | bytes 524288 | tf_op jit(solution)/shard_map/all_to_all | solution.py:17
  129.9 1.3 fusion.10
  131.2 12.6 %all-to-all-done.3 = f32[128,4,128]{2,1,0:T(4,128)S(1)} async-done(((f32[128,4,128]{2,1,0:T(4,128)}), f32[128,4,128]{2,1,0:T(4,128)S(1)}, u32[]{:S(2)}, u32[]{:S(2)}) %all-to-all-start.3) | async-done | bytes 262176 | tf_op jit(solution)/shard_map/all_to_all | solution.py:17
  143.9 4.0 %all-to-all-start.1 = ((f32[4,64,512]{2,1,0:T(8,128)}), f32[4,64,512]{2,1,0:T(8,128)S(1)}, u32[]{:S(2)}, u32[]{:S(2)}) async-start(f32[4,64,512]{2,1,0:T(8,128)} %bitcast.8), calls=%async_computation.1 | async-start | bytes 1048576 | tf_op jit(solution)/shard_map/all_to_all | solution.py:95
  147.9 0.9 multiply_convert_fusion
  148.8 6.2 %all-to-all-done.1 = f32[4,64,512]{2,1,0:T(8,128)S(1)} async-done(((f32[4,64,512]{2,1,0:T(8,128)}), f32[4,64,512]{2,1,0:T(8,128)S(1)}, u32[]{:S(2)}, u32[]{:S(2)}) %all-to-all-start.1) | async-done | bytes 524320 | tf_op jit(solution)/shard_map/all_to_all | solution.py:95
  155.0 3.4 %all-to-all-start.4 = ((bf16[4,64,512]{2,1,0:T(8,128)(2,1)}), bf16[4,64,512]{2,1,0:T(8,128)(2,1)S(1)}, u32[]{:S(2)}, u32[]{:S(2)}) async-start(bf16[4,64,512]{2,1,0:T(8,128)(2,1)} %bitcast.13), calls=%async_computation.4 | async-start | bytes 524288 | tf_op jit(solution)/shard_map/all_to_all | solution.py:116
  158.8 5.1 %all-to-all-done.4 = bf16[4,64,512]{2,1,0:T(8,128)(2,1)S(1)} async-done(((bf16[4,64,512]{2,1,0:T(8,128)(2,1)}), bf16[4,64,512]{2,1,0:T(8,128)(2,1)S(1)}, u32[]{:S(2)}, u32[]{:S(2)}) %all-to-all-start.4) | async-done | bytes 262176 | tf_op jit(solution)/shard_map/all_to_all | solution.py:116
  163.9 0.7 multiply_reduce_fusion.1
  164.7 0.7 broadcast_in_dim.184
  165.4 10.0 %all-to-all-start.2 = ((f32[128,1,128]{2,1,0:T(1,128)}), f32[128,1,128]{2,1,0:T(1,128)S(1)}, u32[]{:S(2)}, u32[]{:S(2)}) async-start(f32[128,1,128]{2,1,0:T(1,128)} %broadcast_in_dim.184), calls=%async_computation.2 | async-start | bytes 131072 | tf_op jit(solution)/shard_map/all_to_all | solution.py:17
  175.7 11.2 %all-to-all-done.2 = f32[128,1,128]{2,1,0:T(1,128)S(1)} async-done(((f32[128,1,128]{2,1,0:T(1,128)}), f32[128,1,128]{2,1,0:T(1,128)S(1)}, u32[]{:S(2)}, u32[]{:S(2)}) %all-to-all-start.2) | async-done | bytes 65568 | tf_op jit(solution)/shard_map/all_to_all | solution.py:17
  187.1 0.6 fusion.40
  189.2 0.7 broadcast_in_dim.189
  190.0 3.5 %all-to-all-start.5 = ((bf16[4,80,512]{2,1,0:T(8,128)(2,1)}), bf16[4,80,512]{2,1,0:T(8,128)(2,1)S(1)}, u32[]{:S(2)}, u32[]{:S(2)}) async-start(bf16[4,80,512]{2,1,0:T(8,128)(2,1)} %broadcast_in_dim.189), calls=%async_computation.5 | async-start | bytes 655360 | tf_op jit(solution)/shard_map/all_to_all | solution.py:17
  193.9 6.2 %all-to-all-done.5 = bf16[4,80,512]{2,1,0:T(8,128)(2,1)S(1)} async-done(((bf16[4,80,512]{2,1,0:T(8,128)(2,1)}), bf16[4,80,512]{2,1,0:T(8,128)(2,1)S(1)}, u32[]{:S(2)}, u32[]{:S(2)}) %all-to-all-start.5) | async-done | bytes 327712 | tf_op jit(solution)/shard_map/all_to_all | solution.py:17
  200.0 0.5 fusion.4
  200.5 0.5 fusion.6
  201.0 3.6 %collective-permute-start = (f32[512,256]{1,0:T(8,128)S(1)}, f32[512,256]{1,0:T(8,128)S(1)}, u32[]{:S(2)}, u32[]{:S(2)}) collective-permute-start(f32[512,256]{1,0:T(8,128)S(1)} %fusion.6), channel_id=1, source_target_pairs={{0,1},{1,0},{2,3},{3,2},{4,5},{5,4},{6,7},{7,6},{8,9},{9,8},{10,11... | collective-permute-start | bytes 1572872 | tf_op jit(solution)/shard_map/ppermute | solution.py:152
  205.0 0.6 convert_reduce_fusion.1
  205.7 0.6 broadcast_in_dim.192
  206.3 1.9 collective-permute-start.1
  208.2 0.5 fusion.2
  208.7 0.6 collective-permute-done.1
  209.4 0.5 slice.54
  211.2 0.5 fusion.9
  211.7 1.1 concatenate.29
  212.8 4.7 %all-to-all-start.6 = ((f32[64,16,256]{2,1,0:T(8,128)}), f32[64,16,256]{2,1,0:T(8,128)S(1)}, u32[]{:S(2)}, u32[]{:S(2)}) async-start(f32[64,16,256]{2,1,0:T(8,128)} %concatenate.29), calls=%async_computation.6 | async-start | bytes 2097152 | tf_op jit(solution)/shard_map/all_to_all | solution.py:157
  217.5 0.6 reduce_sum.148
  218.1 0.6 dynamic_slice.8
  219.3 0.7 iota_compare_fusion.21
  220.1 25.3 %all-to-all-done.6 = f32[64,16,256]{2,1,0:T(8,128)S(1)} async-done(((f32[64,16,256]{2,1,0:T(8,128)}), f32[64,16,256]{2,1,0:T(8,128)S(1)}, u32[]{:S(2)}, u32[]{:S(2)}) %all-to-all-start.6) | async-done | bytes 1048608 | tf_op jit(solution)/shard_map/all_to_all | solution.py:157
  245.5 0.5 slice.79
  246.0 0.7 multiply_reduce_fusion
  (57 shorter events, 3.2 us)
Async XLA Ops:
  7.2 1.4 copy-start
  7.2 102.0 %all-gather.3.cloned.1.call-start = ((), (), s32[]{:S(2)}) async-start(), calls=%async_computation.7 | async-start | bytes 4259840 | tf_op jit(solution)/shard_map/all_gather | solution.py:76
  21.5 93.8 %all-to-all-start = ((bf16[64,8,512]{2,1,0:T(8,128)(2,1)}), bf16[64,8,512]{2,1,0:T(8,128)(2,1)S(1)}, u32[]{:S(2)}, u32[]{:S(2)}) async-start(bf16[64,8,512]{2,1,0:T(8,128)(2,1)} %broadcast_in_dim.183), calls=%async_computation | async-start | bytes 1048576 | tf_op jit(solution)/shard_map/all_to_all | solution.py:17
  34.1 95.7 %copy-start.2 = (s32[128]{0:T(128)S(1)}, s32[128]{0:T(128)}, u32[]{:S(2)}) copy-start(s32[128]{0:T(128)} %param.16) | copy-start | bytes 1540
  34.1 95.8 %copy-start.1 = (bf16[512,512]{1,0:T(8,128)(2,1)S(1)}, bf16[512,512]{1,0:T(8,128)(2,1)}, u32[]{:S(2)}) copy-start(bf16[512,512]{1,0:T(8,128)(2,1)} %param.14) | copy-start | bytes 1572868
  115.0 43.3 %copy-start.3 = (s32[512]{0:T(512)S(1)}, s32[512]{0:T(512)}, u32[]{:S(2)}) copy-start(s32[512]{0:T(512)} %param.17) | copy-start | bytes 6148
  116.0 27.8 %all-to-all-start.3 = ((f32[128,4,128]{2,1,0:T(4,128)}), f32[128,4,128]{2,1,0:T(4,128)S(1)}, u32[]{:S(2)}, u32[]{:S(2)}) async-start(f32[128,4,128]{2,1,0:T(4,128)} %broadcast_in_dim.187), calls=%async_computation.3 | async-start | bytes 524288 | tf_op jit(solution)/shard_map/all_to_all | solution.py:17
  143.9 11.1 %all-to-all-start.1 = ((f32[4,64,512]{2,1,0:T(8,128)}), f32[4,64,512]{2,1,0:T(8,128)S(1)}, u32[]{:S(2)}, u32[]{:S(2)}) async-start(f32[4,64,512]{2,1,0:T(8,128)} %bitcast.8), calls=%async_computation.1 | async-start | bytes 1048576 | tf_op jit(solution)/shard_map/all_to_all | solution.py:95
  155.0 8.9 %all-to-all-start.4 = ((bf16[4,64,512]{2,1,0:T(8,128)(2,1)}), bf16[4,64,512]{2,1,0:T(8,128)(2,1)S(1)}, u32[]{:S(2)}, u32[]{:S(2)}) async-start(bf16[4,64,512]{2,1,0:T(8,128)(2,1)} %bitcast.13), calls=%async_computation.4 | async-start | bytes 524288 | tf_op jit(solution)/shard_map/all_to_all | solution.py:116
  165.4 21.6 %all-to-all-start.2 = ((f32[128,1,128]{2,1,0:T(1,128)}), f32[128,1,128]{2,1,0:T(1,128)S(1)}, u32[]{:S(2)}, u32[]{:S(2)}) async-start(f32[128,1,128]{2,1,0:T(1,128)} %broadcast_in_dim.184), calls=%async_computation.2 | async-start | bytes 131072 | tf_op jit(solution)/shard_map/all_to_all | solution.py:17
  190.0 10.1 %all-to-all-start.5 = ((bf16[4,80,512]{2,1,0:T(8,128)(2,1)}), bf16[4,80,512]{2,1,0:T(8,128)(2,1)S(1)}, u32[]{:S(2)}, u32[]{:S(2)}) async-start(bf16[4,80,512]{2,1,0:T(8,128)(2,1)} %broadcast_in_dim.189), calls=%async_computation.5 | async-start | bytes 655360 | tf_op jit(solution)/shard_map/all_to_all | solution.py:17
  200.5 19.5 %copy-start.4 = (s32[1,4]{1,0:T(1,128)S(1)}, s32[1,4]{1,0:T(1,128)}, u32[]{:S(2)}) copy-start(s32[1,4]{1,0:T(1,128)} %param.15) | copy-start | bytes 52
  201.0 10.1 %collective-permute-start = (f32[512,256]{1,0:T(8,128)S(1)}, f32[512,256]{1,0:T(8,128)S(1)}, u32[]{:S(2)}, u32[]{:S(2)}) collective-permute-start(f32[512,256]{1,0:T(8,128)S(1)} %fusion.6), channel_id=1, source_target_pairs={{0,1},{1,0},{2,3},{3,2},{4,5},{5,4},{6,7},{7,6},{8,9},{9,8},{10,11... | collective-permute-start | bytes 1572872 | tf_op jit(solution)/shard_map/ppermute | solution.py:152
  206.3 3.1 %collective-permute-start.1 = (f32[8,128]{1,0:T(8,128)S(1)}, f32[8,128]{1,0:T(8,128)S(1)}, u32[]{:S(2)}, u32[]{:S(2)}) collective-permute-start(f32[8,128]{1,0:T(8,128)S(1)} %broadcast_in_dim.192), channel_id=1, source_target_pairs={{0,1},{1,0},{2,3},{3,2},{4,5},{5,4},{6,7},{7,6},{8,9},{9,8},{10,11... | collective-permute-start | bytes 12296 | tf_op jit(solution)/shard_map/ppermute | solution.py:153
  212.8 32.6 %all-to-all-start.6 = ((f32[64,16,256]{2,1,0:T(8,128)}), f32[64,16,256]{2,1,0:T(8,128)S(1)}, u32[]{:S(2)}, u32[]{:S(2)}) async-start(f32[64,16,256]{2,1,0:T(8,128)} %concatenate.29), calls=%async_computation.6 | async-start | bytes 2097152 | tf_op jit(solution)/shard_map/all_to_all | solution.py:157
Sparse Core Ops, SparseCore 0:
  20.8 88.3 all-gather.2

commit v2 on v1

v2 whole, which is shorter than its diff:
```python
import jax
import jax.numpy as jnp
from jax import lax
from jax.sharding import Mesh
from jax.sharding import PartitionSpec as P

LOSS_SCALE = 16.0
BLEND = 0.5
EPS = 1e-05
CHIPS = ("y", "z")
OWNERS = ("y", "z", "core")
BF16 = jnp.bfloat16
F32 = jnp.float32


def spread(block, axes, size):
    return lax.all_to_all(
        jnp.broadcast_to(block[None], (size,) + block.shape), axes, 0, 0, tiled=True
    )


def softmax_stats(logits):
    top = jnp.max(logits, axis=1)
    shifted = jnp.exp(logits - top[:, None])
    return top, shifted, jnp.sum(shifted, axis=1)


def row_stats(*columns):
    flat = jnp.concatenate(columns)
    return flat.reshape(-1, 128)


def on_device(
    teacher_hidden,
    teacher_gain,
    teacher_head,
    student_hidden,
    student_head,
    positions,
    counts,
    targets,
):
    members = lax.axis_size("member")
    ring = lax.axis_size("z")
    chips = lax.axis_size("y") * ring
    cores = lax.axis_size("core")
    owners = chips * cores
    member = lax.axis_index("member")
    core = lax.axis_index("core")
    owner = lax.axis_index(OWNERS)
    slot_ids = positions[0]
    cap = slot_ids.shape[0]
    window, width = student_hidden.shape
    vocab = student_head.shape[1]
    padded = owners * cap
    live_rows = padded // 2
    chunk = live_rows // members
    swap = [(0, 1), (1, 0)]

    widened = jnp.take(teacher_hidden[0], slot_ids, axis=0).astype(F32)
    inverse_rms = lax.rsqrt(jnp.mean(widened * widened, axis=1, keepdims=True) + EPS)
    normed = (widened * inverse_rms * teacher_gain[0][None, :]).astype(BF16)
    depth = normed.shape[1]
    quarter = depth // (2 * cores)
    units = normed.reshape(cap, cores, 2, quarter).transpose(1, 2, 0, 3).reshape(
        1, cores, 2 * cap, quarter
    )
    sent = jnp.broadcast_to(units, (ring,) + units.shape[1:]).reshape(-1, 2 * cap, quarter)
    group_rows = lax.all_to_all(sent, ("z", "core"), 0, 0, tiled=True).reshape(-1, quarter)
    teacher_rows = lax.all_gather(group_rows, "y", axis=0, tiled=True)

    before = (
        jnp.arange(owners, dtype=jnp.int32)[:, None] < jnp.arange(owners, dtype=jnp.int32)[None, :]
    )
    starts = jnp.sum(jnp.where(before, counts[:, None], 0), axis=0)
    slots = jnp.arange(cap, dtype=jnp.int32)
    places = jnp.where(slots[None, :] < counts[:, None], starts[:, None] + slots[None, :], -1)
    packed_ids = jnp.arange(live_rows, dtype=jnp.int32)
    sides = jnp.arange(2, dtype=jnp.int32)
    pack = [
        (
            packed_ids[:, None]
            == jnp.where(sides[None, :, None] == side, places[:, None, :], -1).reshape(1, -1)
        ).astype(BF16)
        for side in range(2)
    ]
    live_targets = jnp.sum(
        jnp.where(packed_ids[:, None] == places.reshape(1, padded), targets[None, :], 0), axis=1
    )

    def packed(rows):
        return jnp.concatenate(
            [jnp.dot(one, rows, preferred_element_type=F32).astype(BF16) for one in pack], axis=1
        )

    picked = jnp.take(student_hidden, slot_ids, axis=0)
    picked = picked.reshape(cap, 2, width // 2).transpose(1, 0, 2).reshape(2 * cap, width // 2)
    student_rows = spread(picked, OWNERS, owners).reshape(-1, width // 2)
    partial_logits = jnp.dot(packed(student_rows), student_head, preferred_element_type=F32)
    logits_chunk = jnp.sum(
        lax.all_to_all(
            partial_logits.reshape(members, chunk, vocab), "member", 0, 0, tiled=True
        ),
        axis=0,
    )
    student_logits = spread(logits_chunk, "member", members).reshape(live_rows, vocab)
    top, _, total = softmax_stats(logits_chunk)
    vocab_ids = owner * vocab + jnp.arange(vocab, dtype=jnp.int32)
    hit = vocab_ids[None, :] == live_targets[:, None]
    hit_chunk = vocab_ids[None, :] == lax.dynamic_slice_in_dim(
        live_targets, member * chunk, chunk
    )[:, None]
    target_part = jnp.sum(jnp.where(hit_chunk, logits_chunk, 0.0), axis=1)
    every = spread(
        row_stats(top, total, target_part, jnp.zeros_like(top)), OWNERS, owners
    ).reshape(owners, 4 * chunk)
    tops = every[:, :chunk]
    highest = jnp.max(tops, axis=0)
    totals = jnp.sum(every[:, chunk : 2 * chunk] * jnp.exp(tops - highest[None, :]), axis=0)
    log_chunk = highest + jnp.log(totals)
    student_loss = jnp.sum(log_chunk) - BLEND * jnp.sum(every[:, 2 * chunk : 3 * chunk])
    log_total = spread(jnp.pad(log_chunk[None, :], ((0, 7), (0, 128 - chunk))), "member", members)
    log_total = log_total[:, 0, :chunk].reshape(live_rows)
    student_slope = jnp.exp(student_logits - log_total[:, None]) - BLEND * hit.astype(F32)

    teacher_rows, student_logits = lax.optimization_barrier((teacher_rows, student_logits))
    mine = packed(teacher_rows)
    other = lax.ppermute(mine, "core", swap)
    own_half = lax.dynamic_slice_in_dim(teacher_head[0], core * (depth // 2), depth // 2, axis=0)
    other_half = lax.dynamic_slice_in_dim(
        teacher_head[0], (1 - core) * (depth // 2), depth // 2, axis=0
    )
    teacher_logits = jnp.dot(mine, own_half, preferred_element_type=F32) + jnp.dot(
        other, other_half, preferred_element_type=F32
    )
    top, shifted, total = softmax_stats(teacher_logits)
    cross = jnp.sum(shifted * student_logits, axis=1)
    every = spread(row_stats(top, total, cross), OWNERS, owners).reshape(owners, 3 * live_rows)
    tops = every[:, :live_rows]
    highest = jnp.max(tops, axis=0)
    scales = jnp.exp(tops - highest[None, :])
    totals = jnp.sum(every[:, live_rows : 2 * live_rows] * scales, axis=0)
    crosses = jnp.sum(every[:, 2 * live_rows :] * scales, axis=0)
    teacher_probs = (shifted * (jnp.exp(top - highest) / totals)[:, None]).astype(BF16)
    loss = student_loss - (1.0 - BLEND) / members * jnp.sum(crosses / totals)

    probs = teacher_probs.astype(F32)
    for step in range(1, members):
        shift = [(i, (i + step) % members) for i in range(members)]
        probs = probs + lax.ppermute(teacher_probs, "member", shift).astype(F32)
    slope = (LOSS_SCALE * (student_slope - (1.0 - BLEND) / members * probs)).astype(BF16)

    half = width // 2

    def term(which_core):
        chosen = jnp.take(places.reshape(chips, cores, cap), which_core, axis=1)
        result = 0.0
        for side in range(2):
            at = jnp.where(sides[None, :, None] == side, chosen[:, None, :], -1).reshape(-1, 1)
            unpack = (at == packed_ids[None, :]).astype(BF16)
            rows = jnp.dot(unpack, slope, preferred_element_type=F32).astype(BF16)
            result = result + lax.dot_general(
                rows,
                student_head[side * half : (side + 1) * half],
                (((1,), (1,)), ((), ())),
                preferred_element_type=F32,
            )
        return result

    arrived = lax.ppermute(term(1 - core), "core", swap)
    grads = (term(core) + arrived).reshape(chips, 2 * cap, half)
    owned = jnp.sum(lax.all_to_all(grads, CHIPS, 0, 0, tiled=True), axis=0)
    losses = spread(jnp.full((8, 128), loss, F32), "member", members)
    mean_loss = jnp.sum(losses[:, 0, 0]) / jnp.sum(counts).astype(F32)
    slot_grad = jnp.concatenate([owned[:cap], owned[cap:]], axis=1)
    live_here = slots < lax.dynamic_index_in_dim(counts, owner, keepdims=False)
    placed = (
        (jnp.arange(window, dtype=jnp.int32)[:, None] == slot_ids[None, :]) & live_here[None, :]
    ).astype(F32)
    hidden_grad = jnp.sum(placed[:, :, None] * slot_grad[None, :, :], axis=1).astype(BF16)
    return (mean_loss, hidden_grad)


def solution(mesh):
    fine = Mesh(mesh.devices.reshape(4, 8, 8, 2), ("member", "y", "z", "core"))
    placed = (
        P("member", OWNERS, None),
        P("member", None),
        P("member", None, OWNERS),
        P(OWNERS, "member"),
        P("member", OWNERS),
        P(OWNERS, None),
        P(),
        P(),
    )
    return jax.shard_map(
        on_device,
        mesh=fine,
        in_specs=placed,
        out_specs=(P(), P(OWNERS, "member")),
        check_vma=False,
    )
```

time: 258 us -> 228 us (0.88)
  waiting for transfers between devices: 142 us -> 74.4 us
  blocking collectives: 8.39 us -> 45.8 us
  starting transfers between devices: 55.6 us -> 52.5 us
    all_gather x1, waiting for transfers between devices: 75.1 us -> 0.01 us  [on_device(): teacher_rows = lax.all_gather(group_rows, 'y', axis=0, tiled=True)]
    all_to_all x0 -> x3, blocking collectives: none -> 45.8 us  [the longest x1 23.4 us: on_device(): lax.all_to_all(sent, ('z', 'core'), 0, 0, tiled=True).reshape(-1, quarter)]
    all_to_all x3 -> x1, waiting for transfers between devices: 36.6 us -> 12.2 us  [on_device(): owned = jnp.sum(lax.all_to_all(grads, CHIPS, 0, 0, tiled=True), axis=0)]
    all_to_all x4 -> x5, waiting for transfers between devices: 30 us -> 52 us  [spread(): lax.all_to_all(jnp.broadcast_to(block[None], (size,) + block.shape), axes...]
    ppermute x1 -> x4, starting transfers between devices: 1.92 us -> 14.3 us  [the longest x3 9.52 us: on_device(): probs = probs + lax.ppermute(teacher_probs, 'member', shift).astype(F32)]
    ppermute x1 -> x4, waiting for transfers between devices: 0.64 us -> 10.2 us  [the longest x3 10.2 us: on_device(): probs = probs + lax.ppermute(teacher_probs, 'member', shift).astype(F32)]
    all_to_all x4 -> x5, starting transfers between devices: 38 us -> 28.9 us  [spread(): lax.all_to_all(jnp.broadcast_to(block[None], (size,) + block.shape), axes...]
    all_gather x1 -> x0, blocking collectives: 8.39 us -> none  [on_device(): lax.all_gather(jnp.concatenate([normed, picked], axis=1), 'core', axis=0,...]
  transfers between devices with their start and end apart: 10 -> 12, of which waited for: 8 -> 7; matrix products, arithmetic and copies ran while one was open for 7% -> 9% of each run, Pallas kernels for 0% -> 0%
where the time goes in v2:
time: 228 us; the launch traced here: 224 us
  waiting for transfers between devices  74.4 us (33%)
  starting transfers between devices  52.5 us (23%)
  blocking collectives  45.8 us (20%)
  between operations  19 us (8%)
  matrix products  11.5 us (5%)
  other arithmetic  10.6 us (5%)
  local copies, waits for them, and re-layouts  10.1 us (4%)
    all_to_all x5, waiting for transfers between devices, spread(): lax.all_to_all(jnp.broadcast_to(block[None], (size,) + block.shape), axes...  52 us
    all_to_all x5, starting transfers between devices, spread(): lax.all_to_all(jnp.broadcast_to(block[None], (size,) + block.shape), axes...  28.9 us
    all_to_all x1, blocking collectives, on_device(): lax.all_to_all(sent, ('z', 'core'), 0, 0, tiled=True).reshape(-1, quarter)  23.4 us
    all_to_all x1, blocking collectives, on_device(): lax.all_to_all(partial_logits.reshape(members, chunk, vocab), 'member', 0...  12.4 us
    all_to_all x1, waiting for transfers between devices, on_device(): owned = jnp.sum(lax.all_to_all(grads, CHIPS, 0, 0, tiled=True), axis=0)  12.2 us
    ppermute x3, waiting for transfers between devices, on_device(): probs = probs + lax.ppermute(teacher_probs, 'member', shift).astype(F32)  10.2 us
    all_to_all x1, blocking collectives, spread(): lax.all_to_all(jnp.broadcast_to(block[None], (size,) + block.shape), axes...  9.98 us
    ppermute x3, starting transfers between devices, on_device(): probs = probs + lax.ppermute(teacher_probs, 'member', shift).astype(F32)  9.52 us
  transfers between devices with their start and end apart: 12, of which 7 were waited for; matrix products, arithmetic and copies ran while one was open for 9% of the time, Pallas kernels for 0%

profile of v2, /device:TPU:1, one launch (start us, length us, event | category | flops | bytes accessed | tf_op | source)
XLA Modules:
  0.0 224.1 jit_solution(2666308139334711531)
XLA Ops:
  7.2 0.7 fusion.47
  7.9 0.7 compare_and_fusion
  8.6 0.6 gather_fusion.1
  9.4 0.5 broadcast.296
  10.0 1.4 reduce.8
  11.6 23.4 %all_to_all.45 = bf16[16,8,1024]{2,1,0:T(8,128)(2,1)} all-to-all(bf16[16,8,1024]{2,1,0:T(8,128)(2,1)S(1)} %bitcast.61), channel_id=1, replica_groups=mesh['member'=4,'y'=8,'z'=8,'core'=2] {'z','core'}, dimensions={0} | all-to-all | bytes 524288 | tf_op jit(solution)/shard_map/all_to_all | solution.py:69
  35.0 1.3 gather_fusion
  36.4 0.8 broadcast_in_dim.235
  37.3 9.5 %all-to-all-start = ((bf16[128,8,256]{2,1,0:T(8,128)(2,1)}), bf16[128,8,256]{2,1,0:T(8,128)(2,1)S(1)}, u32[]{:S(2)}, u32[]{:S(2)}) async-start(bf16[128,8,256]{2,1,0:T(8,128)(2,1)} %broadcast_in_dim.235), calls=%async_computation | async-start | bytes 1048576 | tf_op jit(solution)/shard_map/all_to_all | solution.py:17
  47.6 24.9 %all-to-all-done = bf16[128,8,256]{2,1,0:T(8,128)(2,1)S(1)} async-done(((bf16[128,8,256]{2,1,0:T(8,128)(2,1)}), bf16[128,8,256]{2,1,0:T(8,128)(2,1)S(1)}, u32[]{:S(2)}, u32[]{:S(2)}) %all-to-all-start) | async-done | bytes 524320 | tf_op jit(solution)/shard_map/all_to_all | solution.py:17
  73.7 12.4 %all_to_all.46 = f32[4,64,512]{2,1,0:T(8,128)S(1)} all-to-all(f32[4,64,512]{2,1,0:T(8,128)S(1)} %bitcast.59), channel_id=1, replica_groups=mesh['member'=4,'y'=8,'z'=8,'core'=2] {'member'}, dimensions={0} | all-to-all | bytes 1048576 | tf_op jit(solution)/shard_map/all_to_all | solution.py:101
  86.1 10.0 %all_to_all.47 = f32[4,64,512]{2,1,0:T(8,128)S(1)} all-to-all(f32[4,64,512]{2,1,0:T(8,128)S(1)} %broadcast_in_dim.249), channel_id=1, replica_groups=mesh['member'=4,'y'=8,'z'=8,'core'=2] {'member'}, dimensions={0} | all-to-all | bytes 1048576 | tf_op jit(solution)/shard_map/all_to_all | solution.py:17
  96.1 2.5 %convolution_convert_fusion.4 = bf16[256,1024]{1,0:T(8,128)(2,1)S(1)} fusion(bf16[1024,1024]{1,0:T(8,128)(2,1)} %all-gather.2.cloned.1.call-done, s32[1024]{0:T(1024)S(1)} %select_n.150), kind=kOutput, calls=%fused_computation.12 | convolution fusion | flops 537395200 | bytes 2625536 | tf_op jit(solution)/shard_map/dot_general | solution.py:93
  98.6 0.7 convolution_convert_fusion.5
  99.4 4.8 %collective-permute-start = (bf16[256,2048]{1,0:T(8,128)(2,1)S(1)}, bf16[256,2048]{1,0:T(8,128)(2,1)}, u32[]{:S(2)}, u32[]{:S(2)}) collective-permute-start(bf16[256,2048]{1,0:T(8,128)(2,1)S(1)} %pad_maximum_fusion), channel_id=1, source_target_pairs={{0,1},{1,0},{2,3},{3,2},{4,5},{5,4},{6,7},{7,6},{8,9},{9,8},{10,11... | collective-permute-start | bytes 3145736 | tf_op jit(solution)/shard_map/ppermute | solution.py:128
  104.3 0.7 add.135
  105.1 0.7 lt.107
  106.4 0.7 broadcast_in_dim.242
  107.1 6.1 %all-to-all-start.2 = ((f32[128,2,128]{2,1,0:T(2,128)}), f32[128,2,128]{2,1,0:T(2,128)S(1)}, u32[]{:S(2)}, u32[]{:S(2)}) async-start(f32[128,2,128]{2,1,0:T(2,128)} %broadcast_in_dim.242), calls=%async_computation.2 | async-start | bytes 262144 | tf_op jit(solution)/shard_map/all_to_all | solution.py:17
  113.2 2.4 %fusion.2 = f32[256,512]{1,0:T(8,128)S(1)} fusion(bf16[1,4096,512]{2,1,0:T(8,128)(2,1)} %param.12, s32[]{:T(128)S(6)} %select_n.157, bf16[256,1024]{1,0:T(8,128)(2,1)S(1)} %convolution_convert_fusion.4, bf16[256,1024]{1,0:T(8,128)(2,1)S(1)} %convolution_convert_fusion.5), kind=kOutput, calls=%fused_computation.4 | convolution fusion | flops 538968064 | bytes 3670020 | tf_op jit(solution)/shard_map/dot_general | solution.py:133
  116.0 2.0 fusion.52
  118.4 7.0 %all-to-all-done.2 = f32[128,2,128]{2,1,0:T(2,128)S(1)} async-done(((f32[128,2,128]{2,1,0:T(2,128)}), f32[128,2,128]{2,1,0:T(2,128)S(1)}, u32[]{:S(2)}, u32[]{:S(2)}) %all-to-all-start.2) | async-done | bytes 131104 | tf_op jit(solution)/shard_map/all_to_all | solution.py:17
  125.4 0.8 broadcast_in_dim.250
  126.3 6.8 %all-to-all-start.5 = ((f32[128,6,128]{2,1,0:T(8,128)}), f32[128,6,128]{2,1,0:T(8,128)S(1)}, u32[]{:S(2)}, u32[]{:S(2)}) async-start(f32[128,6,128]{2,1,0:T(8,128)} %broadcast_in_dim.250), calls=%async_computation.5 | async-start | bytes 1048576 | tf_op jit(solution)/shard_map/all_to_all | solution.py:17
  133.6 0.6 slice_reduce_fusion.1
  134.3 0.7 fusion.49
  135.0 17.6 %all-to-all-done.5 = f32[128,6,128]{2,1,0:T(8,128)S(1)} async-done(((f32[128,6,128]{2,1,0:T(8,128)}), f32[128,6,128]{2,1,0:T(8,128)S(1)}, u32[]{:S(2)}, u32[]{:S(2)}) %all-to-all-start.5) | async-done | bytes 393248 | tf_op jit(solution)/shard_map/all_to_all | solution.py:17
  152.6 0.6 broadcast_in_dim.254
  153.2 3.3 %all-to-all-start.7 = ((f32[4,8,128]{2,1,0:T(8,128)}), f32[4,8,128]{2,1,0:T(8,128)S(1)}, u32[]{:S(2)}, u32[]{:S(2)}) async-start(f32[4,8,128]{2,1,0:T(8,128)} %broadcast_in_dim.254), calls=%async_computation.7 | async-start | bytes 32768 | tf_op jit(solution)/shard_map/all_to_all | solution.py:17
  157.0 0.7 exponential_divide_fusion
  157.8 4.5 %collective-permute-start.3 = (bf16[256,512]{1,0:T(8,128)(2,1)S(1)}, bf16[256,512]{1,0:T(8,128)(2,1)S(1)}, u32[]{:S(2)}, u32[]{:S(2)}) collective-permute-start(bf16[256,512]{1,0:T(8,128)(2,1)S(1)} %multiply_convert_fusion.1), channel_id=1, source_target_pairs={{0,384},{128,0},{256,128},{384,256},{1,385},{129,1},{257,129},{385... | collective-permute-start | bytes 786440 | tf_op jit(solution)/shard_map/ppermute | solution.py:150
  162.4 2.5 %collective-permute-start.2 = (bf16[256,512]{1,0:T(8,128)(2,1)S(1)}, bf16[256,512]{1,0:T(8,128)(2,1)S(1)}, u32[]{:S(2)}, u32[]{:S(2)}) collective-permute-start(bf16[256,512]{1,0:T(8,128)(2,1)S(1)} %multiply_convert_fusion.1), channel_id=1, source_target_pairs={{0,256},{128,384},{256,0},{384,128},{1,257},{129,385},{257,1},{385... | collective-permute-start | bytes 786440 | tf_op jit(solution)/shard_map/ppermute | solution.py:150
  164.9 2.5 %collective-permute-start.1 = (bf16[256,512]{1,0:T(8,128)(2,1)S(1)}, bf16[256,512]{1,0:T(8,128)(2,1)S(1)}, u32[]{:S(2)}, u32[]{:S(2)}) collective-permute-start(bf16[256,512]{1,0:T(8,128)(2,1)S(1)} %multiply_convert_fusion.1), channel_id=1, source_target_pairs={{0,128},{128,256},{256,384},{384,0},{1,129},{129,257},{257,385},{3... | collective-permute-start | bytes 786440 | tf_op jit(solution)/shard_map/ppermute | solution.py:150
  167.9 3.1 %collective-permute-done.2 = bf16[256,512]{1,0:T(8,128)(2,1)S(1)} collective-permute-done((bf16[256,512]{1,0:T(8,128)(2,1)S(1)}, bf16[256,512]{1,0:T(8,128)(2,1)S(1)}, u32[]{:S(2)}, u32[]{:S(2)}) %collective-permute-start.2) | collective-permute-done | bytes 262176 | tf_op jit(solution)/shard_map/ppermute | solution.py:150
  171.1 7.0 %collective-permute-done.1 = bf16[256,512]{1,0:T(8,128)(2,1)S(1)} collective-permute-done((bf16[256,512]{1,0:T(8,128)(2,1)S(1)}, bf16[256,512]{1,0:T(8,128)(2,1)S(1)}, u32[]{:S(2)}, u32[]{:S(2)}) %collective-permute-start.1) | collective-permute-done | bytes 262176 | tf_op jit(solution)/shard_map/ppermute | solution.py:150
  179.0 0.5 fusion.13
  179.5 3.9 %collective-permute-start.4 = (f32[512,256]{1,0:T(8,128)S(1)}, f32[512,256]{1,0:T(8,128)S(1)}, u32[]{:S(2)}, u32[]{:S(2)}) collective-permute-start(f32[512,256]{1,0:T(8,128)S(1)} %fusion.13), channel_id=1, source_target_pairs={{0,1},{1,0},{2,3},{3,2},{4,5},{5,4},{6,7},{7,6},{8,9},{9,8},{10,11... | collective-permute-start | bytes 1572872 | tf_op jit(solution)/shard_map/ppermute | solution.py:170
  185.8 0.6 broadcast_in_dim_broadcast_in_dim_broadcast_in_dim.3
  186.4 3.3 %all-to-all-start.6 = ((f32[4,8,128]{2,1,0:T(8,128)}), f32[4,8,128]{2,1,0:T(8,128)S(1)}, u32[]{:S(2)}, u32[]{:S(2)}) async-start(f32[4,8,128]{2,1,0:T(8,128)} %broadcast_in_dim_broadcast_in_dim_broadcast_in_dim.3), calls=%async_computation.6 | async-start | bytes 32768 | tf_op jit(solution)/shard_map/all_to_all | solution.py:17
  190.2 1.3 fusion.16
  191.4 2.4 %all-to-all-done.6 = f32[4,8,128]{2,1,0:T(8,128)S(1)} async-done(((f32[4,8,128]{2,1,0:T(8,128)}), f32[4,8,128]{2,1,0:T(8,128)S(1)}, u32[]{:S(2)}, u32[]{:S(2)}) %all-to-all-start.6) | async-done | bytes 16416 | tf_op jit(solution)/shard_map/all_to_all | solution.py:17
  193.8 5.4 %all-to-all-start.8 = ((f32[64,8,256]{2,1,0:T(8,128)}), f32[64,8,256]{2,1,0:T(8,128)S(1)}, u32[]{:S(2)}, u32[]{:S(2)}) async-start(f32[64,8,256]{2,1,0:T(8,128)} %fusion.16), calls=%async_computation.8 | async-start | bytes 1048576 | tf_op jit(solution)/shard_map/all_to_all | solution.py:172
  199.2 0.6 reduce_sum.177
  200.5 0.6 dynamic_slice.22
  201.1 0.6 iota_compare_fusion.22
  201.8 0.6 slice_reduce_fusion.4
  203.1 12.2 %all-to-all-done.8 = f32[64,8,256]{2,1,0:T(8,128)S(1)} async-done(((f32[64,8,256]{2,1,0:T(8,128)}), f32[64,8,256]{2,1,0:T(8,128)S(1)}, u32[]{:S(2)}, u32[]{:S(2)}) %all-to-all-start.8) | async-done | bytes 524320 | tf_op jit(solution)/shard_map/all_to_all | solution.py:172
  215.4 0.7 multiply_reduce_fusion.1
  (85 shorter events, 7.6 us)
Async XLA Ops:
  7.2 1.4 copy-start
  7.2 39.6 %copy-start.5 = (s32[128]{0:T(128)S(1)}, s32[128]{0:T(128)}, u32[]{:S(2)}) copy-start(s32[128]{0:T(128)} %param.16) | copy-start | bytes 1540
  7.2 88.9 %all-gather.2.cloned.1.call-start = ((), (), s32[]{:S(2)}) async-start(), calls=%async_computation.9 | async-start | bytes 2359296 | tf_op jit(solution)/shard_map/all_gather | solution.py:70
  36.3 37.0 %copy-start.1 = (bf16[512,512]{1,0:T(8,128)(2,1)S(1)}, bf16[512,512]{1,0:T(8,128)(2,1)}, u32[]{:S(2)}) copy-start(bf16[512,512]{1,0:T(8,128)(2,1)} %param.14) | copy-start | bytes 1572868
  37.3 35.2 %all-to-all-start = ((bf16[128,8,256]{2,1,0:T(8,128)(2,1)}), bf16[128,8,256]{2,1,0:T(8,128)(2,1)S(1)}, u32[]{:S(2)}, u32[]{:S(2)}) async-start(bf16[128,8,256]{2,1,0:T(8,128)(2,1)} %broadcast_in_dim.235), calls=%async_computation | async-start | bytes 1048576 | tf_op jit(solution)/shard_map/all_to_all | solution.py:17
  46.8 39.3 %copy-start.6 = (pred[2]{0:T(512)(128)(4,1)}, pred[2]{0:T(512)(128)(4,1)S(1)}, u32[]{:S(2)}) copy-start(pred[2]{0:T(512)(128)(4,1)S(1)} %get-tuple-element.45) | copy-start | bytes 10
  96.1 2.5 %copy-start.10 = (bf16[1024,1024]{1,0:T(8,128)(2,1)S(1)}, bf16[1024,1024]{1,0:T(8,128)(2,1)}, u32[]{:S(2)}) copy-start(bf16[1024,1024]{1,0:T(8,128)(2,1)} %all-gather.2.cloned.1.call-done) | copy-start | bytes 6291460
  98.6 7.2 %copy-start.8 = (s32[512]{0:T(512)S(1)}, s32[512]{0:T(512)}, u32[]{:S(2)}) copy-start(s32[512]{0:T(512)} %param.17) | copy-start | bytes 6148
  99.4 16.3 %collective-permute-start = (bf16[256,2048]{1,0:T(8,128)(2,1)S(1)}, bf16[256,2048]{1,0:T(8,128)(2,1)}, u32[]{:S(2)}, u32[]{:S(2)}) collective-permute-start(bf16[256,2048]{1,0:T(8,128)(2,1)S(1)} %pad_maximum_fusion), channel_id=1, source_target_pairs={{0,1},{1,0},{2,3},{3,2},{4,5},{5,4},{6,7},{7,6},{8,9},{9,8},{10,11... | collective-permute-start | bytes 3145736 | tf_op jit(solution)/shard_map/ppermute | solution.py:128
  107.1 18.3 %all-to-all-start.2 = ((f32[128,2,128]{2,1,0:T(2,128)}), f32[128,2,128]{2,1,0:T(2,128)S(1)}, u32[]{:S(2)}, u32[]{:S(2)}) async-start(f32[128,2,128]{2,1,0:T(2,128)} %broadcast_in_dim.242), calls=%async_computation.2 | async-start | bytes 262144 | tf_op jit(solution)/shard_map/all_to_all | solution.py:17
  113.2 2.8 %copy-start.2 = (bf16[1,4096,512]{2,1,0:T(8,128)(2,1)S(1)}, bf16[1,4096,512]{2,1,0:T(8,128)(2,1)}, u32[]{:S(2)}) copy-start(bf16[1,4096,512]{2,1,0:T(8,128)(2,1)} %param.12) | copy-start | bytes 12582916
  118.1 15.0 %copy-start.3 = (s32[64,2]{1,0:T(8,128)S(1)}, s32[64,2]{1,0:T(8,128)}, u32[]{:S(2)}) copy-start(s32[64,2]{1,0:T(8,128)} %add.135) | copy-start | bytes 1540
  118.1 15.0 %copy-start.4 = (s32[64,2]{1,0:T(8,128)S(1)}, s32[64,2]{1,0:T(8,128)}, u32[]{:S(2)}) copy-start(s32[64,2]{1,0:T(8,128)} %lt.107) | copy-start | bytes 1540
  126.2 41.1 %copy-start.7 = (pred[2]{0:T(512)(128)(4,1)S(1)}, pred[2]{0:T(512)(128)(4,1)}, u32[]{:S(2)}) copy-start(pred[2]{0:T(512)(128)(4,1)} %copy-done.6) | copy-start | bytes 10
  126.3 26.3 %all-to-all-start.5 = ((f32[128,6,128]{2,1,0:T(8,128)}), f32[128,6,128]{2,1,0:T(8,128)S(1)}, u32[]{:S(2)}, u32[]{:S(2)}) async-start(f32[128,6,128]{2,1,0:T(8,128)} %broadcast_in_dim.250), calls=%async_computation.5 | async-start | bytes 1048576 | tf_op jit(solution)/shard_map/all_to_all | solution.py:17
  153.2 14.6 %all-to-all-start.7 = ((f32[4,8,128]{2,1,0:T(8,128)}), f32[4,8,128]{2,1,0:T(8,128)S(1)}, u32[]{:S(2)}, u32[]{:S(2)}) async-start(f32[4,8,128]{2,1,0:T(8,128)} %broadcast_in_dim.254), calls=%async_computation.7 | async-start | bytes 32768 | tf_op jit(solution)/shard_map/all_to_all | solution.py:17
  157.8 10.1 %collective-permute-start.3 = (bf16[256,512]{1,0:T(8,128)(2,1)S(1)}, bf16[256,512]{1,0:T(8,128)(2,1)S(1)}, u32[]{:S(2)}, u32[]{:S(2)}) collective-permute-start(bf16[256,512]{1,0:T(8,128)(2,1)S(1)} %multiply_convert_fusion.1), channel_id=1, source_target_pairs={{0,384},{128,0},{256,128},{384,256},{1,385},{129,1},{257,129},{385... | collective-permute-start | bytes 786440 | tf_op jit(solution)/shard_map/ppermute | solution.py:150
  162.4 8.7 %collective-permute-start.2 = (bf16[256,512]{1,0:T(8,128)(2,1)S(1)}, bf16[256,512]{1,0:T(8,128)(2,1)S(1)}, u32[]{:S(2)}, u32[]{:S(2)}) collective-permute-start(bf16[256,512]{1,0:T(8,128)(2,1)S(1)} %multiply_convert_fusion.1), channel_id=1, source_target_pairs={{0,256},{128,384},{256,0},{384,128},{1,257},{129,385},{257,1},{385... | collective-permute-start | bytes 786440 | tf_op jit(solution)/shard_map/ppermute | solution.py:150
  164.9 13.2 %collective-permute-start.1 = (bf16[256,512]{1,0:T(8,128)(2,1)S(1)}, bf16[256,512]{1,0:T(8,128)(2,1)S(1)}, u32[]{:S(2)}, u32[]{:S(2)}) collective-permute-start(bf16[256,512]{1,0:T(8,128)(2,1)S(1)} %multiply_convert_fusion.1), channel_id=1, source_target_pairs={{0,128},{128,256},{256,384},{384,0},{1,129},{129,257},{257,385},{3... | collective-permute-start | bytes 786440 | tf_op jit(solution)/shard_map/ppermute | solution.py:150
  179.5 10.6 %collective-permute-start.4 = (f32[512,256]{1,0:T(8,128)S(1)}, f32[512,256]{1,0:T(8,128)S(1)}, u32[]{:S(2)}, u32[]{:S(2)}) collective-permute-start(f32[512,256]{1,0:T(8,128)S(1)} %fusion.13), channel_id=1, source_target_pairs={{0,1},{1,0},{2,3},{3,2},{4,5},{5,4},{6,7},{7,6},{8,9},{9,8},{10,11... | collective-permute-start | bytes 1572872 | tf_op jit(solution)/shard_map/ppermute | solution.py:170
  186.4 7.4 %all-to-all-start.6 = ((f32[4,8,128]{2,1,0:T(8,128)}), f32[4,8,128]{2,1,0:T(8,128)S(1)}, u32[]{:S(2)}, u32[]{:S(2)}) async-start(f32[4,8,128]{2,1,0:T(8,128)} %broadcast_in_dim_broadcast_in_dim_broadcast_in_dim.3), calls=%async_computation.6 | async-start | bytes 32768 | tf_op jit(solution)/shard_map/all_to_all | solution.py:17
  189.6 12.1 %copy-start.9 = (s32[1,4]{1,0:T(1,128)S(1)}, s32[1,4]{1,0:T(1,128)}, u32[]{:S(2)}) copy-start(s32[1,4]{1,0:T(1,128)} %param.15) | copy-start | bytes 52
  193.8 21.5 %all-to-all-start.8 = ((f32[64,8,256]{2,1,0:T(8,128)}), f32[64,8,256]{2,1,0:T(8,128)S(1)}, u32[]{:S(2)}, u32[]{:S(2)}) async-start(f32[64,8,256]{2,1,0:T(8,128)} %fusion.16), calls=%async_computation.8 | async-start | bytes 1048576 | tf_op jit(solution)/shard_map/all_to_all | solution.py:172
Sparse Core Ops, SparseCore 0:
  35.2 46.7 all-gather.1

commit v3 on v2

--- a/solution.py
+++ b/solution.py
@@ -1,6 +1,8 @@
 import jax
 import jax.numpy as jnp
 from jax import lax
+from jax.experimental import pallas as pl
+from jax.experimental.pallas import tpu as pltpu
 from jax.sharding import Mesh
 from jax.sharding import PartitionSpec as P
 
@@ -17,6 +19,81 @@
     return lax.all_to_all(
         jnp.broadcast_to(block[None], (size,) + block.shape), axes, 0, 0, tiled=True
     )
+
+
+def own_rows_kernel(copies, ids_ref, teacher_ref, gain_ref, student_ref, sent_ref):
+    cap = ids_ref.shape[1]
+    window, depth = teacher_ref.shape[1:]
+    width = student_ref.shape[1]
+    rows = 4 * cap
+    row = lax.broadcasted_iota(jnp.int32, (rows, window), 0) % cap
+    column = lax.broadcasted_iota(jnp.int32, (rows, window), 1)
+    wanted = jnp.zeros((rows, window), jnp.int32)
+    for slot in range(cap):
+        wanted = jnp.where(row == slot, ids_ref[0, slot], wanted)
+    select = (column == wanted).astype(BF16)
+    picked = jnp.dot(select, teacher_ref[0], preferred_element_type=F32)
+    inverse_rms = lax.rsqrt(jnp.mean(picked * picked, axis=1, keepdims=True) + EPS)
+    normed = picked * inverse_rms * gain_ref[...]
+    student = jnp.dot(select, student_ref[...], preferred_element_type=F32)
+
+    def quarters(values):
+        part = values.shape[1] // 4
+        group = lax.broadcasted_iota(jnp.int32, (rows, part), 0) // cap
+        result = values[:, :part]
+        for index in range(1, 4):
+            result = jnp.where(group == index, values[:, index * part : (index + 1) * part], result)
+        return result.astype(BF16)
+
+    teacher_part, student_part = quarters(normed), quarters(student)
+    for copy in range(copies):
+        sent_ref[copy * rows : (copy + 1) * rows, : depth // 4] = teacher_part
+        sent_ref[copy * rows : (copy + 1) * rows, depth // 4 :] = student_part
+
+
+def own_rows(copies, slot_ids, teacher_hidden, teacher_gain, student_hidden):
+    cap = slot_ids.shape[1]
+    features = teacher_hidden.shape[2] // 4 + student_hidden.shape[1] // 4
+    return pl.pallas_call(
+        lambda *refs: own_rows_kernel(copies, *refs),
+        out_shape=jax.ShapeDtypeStruct((copies * 4 * cap, features), BF16),
+        in_specs=[pl.BlockSpec(memory_space=pltpu.SMEM)]
+        + [pl.BlockSpec(memory_space=pltpu.VMEM)] * 3,
+        out_specs=pl.BlockSpec(memory_space=pltpu.VMEM),
+        name="own_rows",
+    )(slot_ids, teacher_hidden, teacher_gain, student_hidden)
+
+
+def pack_kernel(places_ref, rows_ref, packed_ref, one_ref):
+    live = packed_ref.shape[1]
+
+    @pl.when(pl.program_id(0) == 0)
+    def _():
+        ids = lax.broadcasted_iota(jnp.int32, (live, places_ref.shape[1]), 0)
+        for side in range(2):
+            one_ref[side] = (ids == places_ref[side : side + 1, :]).astype(BF16)
+
+    for side in range(2):
+        packed_ref[side] = jnp.dot(
+            one_ref[side], rows_ref[...], preferred_element_type=F32
+        ).astype(BF16)
+
+
+def pack_rows(places, rows, live, parts):
+    total, features = rows.shape
+    part = features // parts
+    return pl.pallas_call(
+        pack_kernel,
+        grid=(parts,),
+        out_shape=jax.ShapeDtypeStruct((2, live, features), BF16),
+        in_specs=[
+            pl.BlockSpec((2, total), lambda i: (0, 0)),
+            pl.BlockSpec((total, part), lambda i: (0, i)),
+        ],
+        out_specs=pl.BlockSpec((2, live, part), lambda i: (0, 0, i)),
+        scratch_shapes=[pltpu.VMEM((2, live, total), BF16)],
+        name="pack_rows",
+    )(places, rows)
 
 
 def softmax_stats(logits):
@@ -57,17 +134,13 @@
     chunk = live_rows // members
     swap = [(0, 1), (1, 0)]
 
-    widened = jnp.take(teacher_hidden[0], slot_ids, axis=0).astype(F32)
-    inverse_rms = lax.rsqrt(jnp.mean(widened * widened, axis=1, keepdims=True) + EPS)
-    normed = (widened * inverse_rms * teacher_gain[0][None, :]).astype(BF16)
-    depth = normed.shape[1]
+    sent = own_rows(ring, positions, teacher_hidden, teacher_gain, student_hidden)
+    depth = teacher_hidden.shape[2]
     quarter = depth // (2 * cores)
-    units = normed.reshape(cap, cores, 2, quarter).transpose(1, 2, 0, 3).reshape(
-        1, cores, 2 * cap, quarter
-    )
-    sent = jnp.broadcast_to(units, (ring,) + units.shape[1:]).reshape(-1, 2 * cap, quarter)
-    group_rows = lax.all_to_all(sent, ("z", "core"), 0, 0, tiled=True).reshape(-1, quarter)
-    teacher_rows = lax.all_gather(group_rows, "y", axis=0, tiled=True)
+    sent = sent.reshape(ring * cores, 2 * cap, -1)
+    group_rows = lax.all_to_all(sent, ("z", "core"), 0, 0, tiled=True)
+    group_rows = group_rows.reshape(ring * cores * 2 * cap, -1)
+    teacher_rows = lax.all_gather(group_rows[:, :quarter], "y", axis=0, tiled=True)
 
     before = (
         jnp.arange(owners, dtype=jnp.int32)[:, None] < jnp.arange(owners, dtype=jnp.int32)[None, :]
@@ -77,26 +150,33 @@
     places = jnp.where(slots[None, :] < counts[:, None], starts[:, None] + slots[None, :], -1)
     packed_ids = jnp.arange(live_rows, dtype=jnp.int32)
     sides = jnp.arange(2, dtype=jnp.int32)
-    pack = [
-        (
-            packed_ids[:, None]
-            == jnp.where(sides[None, :, None] == side, places[:, None, :], -1).reshape(1, -1)
-        ).astype(BF16)
-        for side in range(2)
-    ]
+    side_places = jnp.stack(
+        [
+            jnp.where(sides[None, :, None] == side, places[:, None, :], -1).reshape(-1)
+            for side in range(2)
+        ]
+    )
     live_targets = jnp.sum(
         jnp.where(packed_ids[:, None] == places.reshape(1, padded), targets[None, :], 0), axis=1
     )
 
-    def packed(rows):
-        return jnp.concatenate(
-            [jnp.dot(one, rows, preferred_element_type=F32).astype(BF16) for one in pack], axis=1
-        )
-
-    picked = jnp.take(student_hidden, slot_ids, axis=0)
-    picked = picked.reshape(cap, 2, width // 2).transpose(1, 0, 2).reshape(2 * cap, width // 2)
-    student_rows = spread(picked, OWNERS, owners).reshape(-1, width // 2)
-    partial_logits = jnp.dot(packed(student_rows), student_head, preferred_element_type=F32)
+    def both_halves(mine, other, weights):
+        half = weights.shape[0] // cores
+        part = half // 2
+        result = 0.0
+        for values, first in ((mine, core * half), (other, (1 - core) * half)):
+            for side in range(2):
+                result = result + jnp.dot(
+                    values[side],
+                    lax.dynamic_slice_in_dim(weights, first + side * part, part, axis=0),
+                    preferred_element_type=F32,
+                )
+        return result
+
+    student_rows = spread(group_rows[:, quarter:], "y", lax.axis_size("y"))
+    student_rows = student_rows.reshape(2 * padded, -1)
+    mine = pack_rows(side_places, student_rows, live_rows, 1)
+    partial_logits = both_halves(mine, lax.ppermute(mine, "core", swap), student_head)
     logits_chunk = jnp.sum(
         lax.all_to_all(
             partial_logits.reshape(members, chunk, vocab), "member", 0, 0, tiled=True
@@ -119,35 +199,41 @@
     totals = jnp.sum(every[:, chunk : 2 * chunk] * jnp.exp(tops - highest[None, :]), axis=0)
     log_chunk = highest + jnp.log(totals)
     student_loss = jnp.sum(log_chunk) - BLEND * jnp.sum(every[:, 2 * chunk : 3 * chunk])
-    log_total = spread(jnp.pad(log_chunk[None, :], ((0, 7), (0, 128 - chunk))), "member", members)
-    log_total = log_total[:, 0, :chunk].reshape(live_rows)
-    student_slope = jnp.exp(student_logits - log_total[:, None]) - BLEND * hit.astype(F32)
-
-    teacher_rows, student_logits = lax.optimization_barrier((teacher_rows, student_logits))
-    mine = packed(teacher_rows)
-    other = lax.ppermute(mine, "core", swap)
-    own_half = lax.dynamic_slice_in_dim(teacher_head[0], core * (depth // 2), depth // 2, axis=0)
-    other_half = lax.dynamic_slice_in_dim(
-        teacher_head[0], (1 - core) * (depth // 2), depth // 2, axis=0
-    )
-    teacher_logits = jnp.dot(mine, own_half, preferred_element_type=F32) + jnp.dot(
-        other, other_half, preferred_element_type=F32
-    )
+
+    teacher_rows, student_logits, log_chunk = lax.optimization_barrier(
+        (teacher_rows, student_logits, log_chunk)
+    )
+    mine = pack_rows(side_places, teacher_rows, live_rows, 4)
+    teacher_logits = both_halves(mine, lax.ppermute(mine, "core", swap), teacher_head[0])
     top, shifted, total = softmax_stats(teacher_logits)
     cross = jnp.sum(shifted * student_logits, axis=1)
-    every = spread(row_stats(top, total, cross), OWNERS, owners).reshape(owners, 3 * live_rows)
+    shifted = shifted.astype(BF16)
+    arrived = [shifted] + [
+        lax.ppermute(shifted, "member", [(i, (i + step) % members) for i in range(members)])
+        for step in range(1, members)
+    ]
+    every = spread(jnp.concatenate([top, total, cross])[None], OWNERS, owners)
+    every = every.reshape(owners, 3 * live_rows)
     tops = every[:, :live_rows]
     highest = jnp.max(tops, axis=0)
     scales = jnp.exp(tops - highest[None, :])
     totals = jnp.sum(every[:, live_rows : 2 * live_rows] * scales, axis=0)
     crosses = jnp.sum(every[:, 2 * live_rows :] * scales, axis=0)
-    teacher_probs = (shifted * (jnp.exp(top - highest) / totals)[:, None]).astype(BF16)
+    factor = jnp.exp(top - highest) / totals
     loss = student_loss - (1.0 - BLEND) / members * jnp.sum(crosses / totals)
-
-    probs = teacher_probs.astype(F32)
-    for step in range(1, members):
-        shift = [(i, (i + step) % members) for i in range(members)]
-        probs = probs + lax.ppermute(teacher_probs, "member", shift).astype(F32)
+    factors = spread(
+        jnp.concatenate([factor, log_chunk, jnp.full((128 - chunk,), loss)]).reshape(-1, 128), "member", members
+    )
+    mean_loss = jnp.sum(factors[:, -1, chunk]) / jnp.sum(counts).astype(F32)
+    log_total = factors[:, -1, :chunk].reshape(live_rows)
+    factors = factors[:, :-1].reshape(members, live_rows)
+    ranks = jnp.arange(members, dtype=jnp.int32)[:, None]
+    probs = 0.0
+    for step in range(members):
+        source = (member - step) % members
+        scale = jnp.sum(jnp.where(ranks == source, factors, 0.0), axis=0)
+        probs = probs + arrived[step].astype(F32) * scale[:, None]
+    student_slope = jnp.exp(student_logits - log_total[:, None]) - BLEND * hit.astype(F32)
     slope = (LOSS_SCALE * (student_slope - (1.0 - BLEND) / members * probs)).astype(BF16)
 
     half = width // 2
@@ -170,8 +256,6 @@
     arrived = lax.ppermute(term(1 - core), "core", swap)
     grads = (term(core) + arrived).reshape(chips, 2 * cap, half)
     owned = jnp.sum(lax.all_to_all(grads, CHIPS, 0, 0, tiled=True), axis=0)
-    losses = spread(jnp.full((8, 128), loss, F32), "member", members)
-    mean_loss = jnp.sum(losses[:, 0, 0]) / jnp.sum(counts).astype(F32)
     slot_grad = jnp.concatenate([owned[:cap], owned[cap:]], axis=1)
     live_here = slots < lax.dynamic_index_in_dim(counts, owner, keepdims=False)
     placed = (

time: 228 us -> 201 us (0.88)
  waiting for transfers between devices: 74.4 us -> 52.7 us
  Pallas kernels: 0 us -> 8.65 us
  starting transfers between devices: 52.5 us -> 48.6 us
  blocking collectives: 45.8 us -> 42.5 us
  local copies, waits for them, and re-layouts: 10.1 us -> 6.86 us
    all_to_all x5 -> x4, waiting for transfers between devices: 52 us -> 30.2 us  [spread(): lax.all_to_all(jnp.broadcast_to(block[None], (size,) + block.shape), axes...]
    all_to_all x2 -> x1, blocking collectives: 35.8 us -> 24.2 us  [on_device(): group_rows = lax.all_to_all(sent, ('z', 'core'), 0, 0, tiled=True)]
    ppermute x4 -> x5, waiting for transfers between devices: 10.2 us -> 0.01 us  [the longest x3 0.01 us: on_device(): lax.ppermute(shifted, 'member', [(i, (i + step) % members) for i in range...]
    all_to_all x5 -> x4, starting transfers between devices: 28.9 us -> 18.8 us  [spread(): lax.all_to_all(jnp.broadcast_to(block[None], (size,) + block.shape), axes...]
    all_to_all x0 -> x1, waiting for transfers between devices: none -> 8.91 us  [on_device(): lax.all_to_all(partial_logits.reshape(members, chunk, vocab), 'member', 0...]
    pallas_call x0 -> x3, Pallas kernels: none -> 8.65 us  [the longest x2 6.68 us: pack_rows(): pl.pallas_call(pack_kernel, grid=(parts,), out_shape=jax.ShapeDtypeStruct...]
    all_to_all x1, blocking collectives: 9.98 us -> 18.3 us  [spread(): lax.all_to_all(jnp.broadcast_to(block[None], (size,) + block.shape), axes...]
    all_to_all x0 -> x1, starting transfers between devices: none -> 4.06 us  [on_device(): lax.all_to_all(partial_logits.reshape(members, chunk, vocab), 'member', 0...]
  transfers between devices with their start and end apart: 12 -> 13, of which waited for: 7 -> 7; matrix products, arithmetic and copies ran while one was open for 9% -> 10% of each run, Pallas kernels for 0% -> 1%
where the time goes in v3:
time: 201 us; the launch traced here: 198 us
  waiting for transfers between devices  52.7 us (26%)
  starting transfers between devices  48.6 us (24%)
  blocking collectives  42.5 us (21%)
  between operations  18.9 us (9%)
  matrix products  10.9 us (5%)
  other arithmetic  8.98 us (4%)
  Pallas kernels  8.65 us (4%)
  local copies, waits for them, and re-layouts  6.86 us (3%)
    all_to_all x4, waiting for transfers between devices, spread(): lax.all_to_all(jnp.broadcast_to(block[None], (size,) + block.shape), axes...  30.2 us
    all_to_all x1, blocking collectives, on_device(): group_rows = lax.all_to_all(sent, ('z', 'core'), 0, 0, tiled=True)  24.2 us
    all_to_all x4, starting transfers between devices, spread(): lax.all_to_all(jnp.broadcast_to(block[None], (size,) + block.shape), axes...  18.8 us
    all_to_all x1, blocking collectives, spread(): lax.all_to_all(jnp.broadcast_to(block[None], (size,) + block.shape), axes...  18.3 us
    all_to_all x1, waiting for transfers between devices, on_device(): owned = jnp.sum(lax.all_to_all(grads, CHIPS, 0, 0, tiled=True), axis=0)  12.8 us
    all_to_all x1, waiting for transfers between devices, on_device(): lax.all_to_all(partial_logits.reshape(members, chunk, vocab), 'member', 0...  8.91 us
    ppermute x3, starting transfers between devices, on_device(): lax.ppermute(shifted, 'member', [(i, (i + step) % members) for i in range...  8.42 us
    dot_general x8, matrix products, both_halves(): jnp.dot(values[side], lax.dynamic_slice_in_dim(weights, first + side * pa...  8.2 us
  transfers between devices with their start and end apart: 13, of which 7 were waited for; matrix products, arithmetic and copies ran while one was open for 10% of the time, Pallas kernels for 1%

profile of v3, /device:TPU:1, one launch (start us, length us, event | category | flops | bytes accessed | tf_op | source)
XLA Modules:
  0.0 198.1 jit_solution(9144028901011738655)
XLA Ops:
  7.2 2.0 own_rows.1
  9.2 24.2 %all_to_all.40 = bf16[16,8,1152]{2,1,0:T(8,128)(2,1)S(1)} all-to-all(bf16[16,8,1152]{2,1,0:T(8,128)(2,1)} %bitcast.73), channel_id=1, replica_groups=mesh['member'=4,'y'=8,'z'=8,'core'=2] {'z','core'}, dimensions={0} | all-to-all | bytes 589824 | tf_op jit(solution)/shard_map/all_to_all | solution.py:141
  33.4 0.7 slice.103
  34.1 0.8 select_reduce_fusion.2
  34.9 0.8 broadcast_in_dim.235
  35.7 6.8 %all-to-all-start.1 = ((bf16[8,128,128]{2,1,0:T(8,128)(2,1)}), bf16[8,128,128]{2,1,0:T(8,128)(2,1)S(1)}, u32[]{:S(2)}, u32[]{:S(2)}) async-start(bf16[8,128,128]{2,1,0:T(8,128)(2,1)} %broadcast_in_dim.235), calls=%async_computation.1 | async-start | bytes 524288 | tf_op jit(solution)/shard_map/all_to_all | solution.py:19
  42.5 0.8 add_select_fusion
  43.8 0.6 pad_add_fusion.places_ref
  44.4 12.7 %all-to-all-done.1 = bf16[8,128,128]{2,1,0:T(8,128)(2,1)S(1)} async-done(((bf16[8,128,128]{2,1,0:T(8,128)(2,1)}), bf16[8,128,128]{2,1,0:T(8,128)(2,1)S(1)}, u32[]{:S(2)}, u32[]{:S(2)}) %all-to-all-start.1) | async-done | bytes 262176 | tf_op jit(solution)/shard_map/all_to_all | solution.py:19
  57.1 0.7 copy-done.2
  57.8 2.0 %pack_rows.2 = bf16[2,256,128]{2,1,0:T(8,128)(2,1)} custom-call(s32[2,1024]{1,0:T(2,128)} %pad_add_fusion.places_ref, bf16[1024,128]{1,0:T(8,128)(2,1)} %bitcast.74), custom_call_target="tpu_custom_call" | custom-call | tf_op jit(solution)/shard_map/pack_rows/pallas_call | solution.py:85
  59.9 2.4 %collective-permute-start = (bf16[2,256,128]{2,1,0:T(8,128)(2,1)}, bf16[2,256,128]{2,1,0:T(8,128)(2,1)S(1)}, u32[]{:S(2)}, u32[]{:S(2)}) collective-permute-start(bf16[2,256,128]{2,1,0:T(8,128)(2,1)} %pack_rows.2), channel_id=1, source_target_pairs={{0,1},{1,0},{2,3},{3,2},{4,5},{5,4},{6,7},{7,6},{8,9},{9,8},{10,11... | collective-permute-start | bytes 393224 | tf_op jit(solution)/shard_map/ppermute | solution.py:179
  62.2 1.2 fusion.40
  63.4 1.1 convolution_add_fusion.3
  64.7 1.0 fusion.5
  65.7 4.1 %all-to-all-start.2 = ((f32[4,64,512]{2,1,0:T(8,128)}), f32[4,64,512]{2,1,0:T(8,128)S(1)}, u32[]{:S(2)}, u32[]{:S(2)}) async-start(f32[4,64,512]{2,1,0:T(8,128)} %bitcast.7), calls=%async_computation.2 | async-start | bytes 1048576 | tf_op jit(solution)/shard_map/all_to_all | solution.py:181
  70.1 8.9 %all-to-all-done.2 = f32[4,64,512]{2,1,0:T(8,128)S(1)} async-done(((f32[4,64,512]{2,1,0:T(8,128)}), f32[4,64,512]{2,1,0:T(8,128)S(1)}, u32[]{:S(2)}, u32[]{:S(2)}) %all-to-all-start.2) | async-done | bytes 524320 | tf_op jit(solution)/shard_map/all_to_all | solution.py:181
  79.5 18.3 %all_to_all.41 = f32[128,2,128]{2,1,0:T(2,128)S(1)} all-to-all(f32[128,2,128]{2,1,0:T(2,128)S(1)} %broadcast_in_dim.242), channel_id=1, replica_groups=mesh['member'=4,'y'=8,'z'=8,'core'=2] {'y','z','core'}, dimensions={0} | all-to-all | bytes 262144 | tf_op jit(solution)/shard_map/all_to_all | solution.py:19
  97.8 0.9 broadcast_in_dim.236
  98.7 3.5 %all-to-all-start.3 = ((f32[4,64,512]{2,1,0:T(8,128)}), f32[4,64,512]{2,1,0:T(8,128)S(1)}, u32[]{:S(2)}, u32[]{:S(2)}) async-start(f32[4,64,512]{2,1,0:T(8,128)} %broadcast_in_dim.236), calls=%async_computation.3 | async-start | bytes 1048576 | tf_op jit(solution)/shard_map/all_to_all | solution.py:19
  102.4 0.6 slice_reduce_fusion.1
  103.0 0.6 fusion.53
  103.6 7.4 %all-to-all-done.3 = f32[4,64,512]{2,1,0:T(8,128)S(1)} async-done(((f32[4,64,512]{2,1,0:T(8,128)}), f32[4,64,512]{2,1,0:T(8,128)S(1)}, u32[]{:S(2)}, u32[]{:S(2)}) %all-to-all-start.3) | async-done | bytes 524320 | tf_op jit(solution)/shard_map/all_to_all | solution.py:19
  111.0 4.6 %pack_rows.3 = bf16[2,256,1024]{2,1,0:T(8,128)(2,1)} custom-call(s32[2,1024]{1,0:T(2,128)} %pad_add_fusion.places_ref, bf16[1024,1024]{1,0:T(8,128)(2,1)} %all-gather.2.cloned.1.call-done.rows_ref), custom_call_target="tpu_custom_call" | custom-call | tf_op jit(solution)/shard_map/pack_rows/pallas_call | solution.py:85
  115.6 3.5 %collective-permute-start.1 = (bf16[2,256,1024]{2,1,0:T(8,128)(2,1)}, bf16[2,256,1024]{2,1,0:T(8,128)(2,1)S(1)}, u32[]{:S(2)}, u32[]{:S(2)}) collective-permute-start(bf16[2,256,1024]{2,1,0:T(8,128)(2,1)} %pack_rows.3), channel_id=1, source_target_pairs={{0,1},{1,0},{2,3},{3,2},{4,5},{5,4},{6,7},{7,6},{8,9},{9,8},{10,11... | collective-permute-start | bytes 3145736 | tf_op jit(solution)/shard_map/ppermute | solution.py:207
  119.1 2.0 fusion.14
  121.1 1.8 convolution_add_fusion.1
  123.4 0.5 fusion.55
  124.2 0.9 broadcast_in_dim.243
  125.2 5.3 %all-to-all-start.5 = ((f32[128,1,768]{2,1,0:T(1,128)}), f32[128,1,768]{2,1,0:T(1,128)S(1)}, u32[]{:S(2)}, u32[]{:S(2)}) async-start(f32[128,1,768]{2,1,0:T(1,128)} %broadcast_in_dim.243), calls=%async_computation.5 | async-start | bytes 786432 | tf_op jit(solution)/shard_map/all_to_all | solution.py:19
  132.5 2.2 %collective-permute-start.2 = (bf16[256,512]{1,0:T(8,128)(2,1)S(1)}, bf16[256,512]{1,0:T(8,128)(2,1)S(1)}, u32[]{:S(2)}, u32[]{:S(2)}) collective-permute-start(bf16[256,512]{1,0:T(8,128)(2,1)S(1)} %get-tuple-element.34), channel_id=1, source_target_pairs={{0,128},{128,256},{256,384},{384,0},{1,129},{129,257},{257,385},{3... | collective-permute-start | bytes 786440 | tf_op jit(solution)/shard_map/ppermute | solution.py:212
  134.7 3.7 %collective-permute-start.3 = (bf16[256,512]{1,0:T(8,128)(2,1)S(1)}, bf16[256,512]{1,0:T(8,128)(2,1)S(1)}, u32[]{:S(2)}, u32[]{:S(2)}) collective-permute-start(bf16[256,512]{1,0:T(8,128)(2,1)S(1)} %get-tuple-element.34), channel_id=1, source_target_pairs={{0,256},{128,384},{256,0},{384,128},{1,257},{129,385},{257,1},{385... | collective-permute-start | bytes 786440 | tf_op jit(solution)/shard_map/ppermute | solution.py:212
  138.4 2.5 %collective-permute-start.4 = (bf16[256,512]{1,0:T(8,128)(2,1)S(1)}, bf16[256,512]{1,0:T(8,128)(2,1)S(1)}, u32[]{:S(2)}, u32[]{:S(2)}) collective-permute-start(bf16[256,512]{1,0:T(8,128)(2,1)S(1)} %get-tuple-element.34), channel_id=1, source_target_pairs={{0,384},{128,0},{256,128},{384,256},{1,385},{129,1},{257,129},{385... | collective-permute-start | bytes 786440 | tf_op jit(solution)/shard_map/ppermute | solution.py:212
  141.0 6.3 %all-to-all-done.5 = f32[128,1,768]{2,1,0:T(1,128)S(1)} async-done(((f32[128,1,768]{2,1,0:T(1,128)}), f32[128,1,768]{2,1,0:T(1,128)S(1)}, u32[]{:S(2)}, u32[]{:S(2)}) %all-to-all-start.5) | async-done | bytes 393248 | tf_op jit(solution)/shard_map/all_to_all | solution.py:19
  147.4 0.6 exponential_divide_fusion
  148.8 0.6 broadcast_in_dim.246
  149.4 3.2 %all-to-all-start.6 = ((f32[4,3,128]{2,1,0:T(4,128)}), f32[4,3,128]{2,1,0:T(4,128)S(1)}, u32[]{:S(2)}, u32[]{:S(2)}) async-start(f32[4,3,128]{2,1,0:T(4,128)} %broadcast_in_dim.246), calls=%async_computation.6 | async-start | bytes 16384 | tf_op jit(solution)/shard_map/all_to_all | solution.py:19
  152.9 3.9 %all-to-all-done.6 = f32[4,3,128]{2,1,0:T(4,128)S(1)} async-done(((f32[4,3,128]{2,1,0:T(4,128)}), f32[4,3,128]{2,1,0:T(4,128)S(1)}, u32[]{:S(2)}, u32[]{:S(2)}) %all-to-all-start.6) | async-done | bytes 6176 | tf_op jit(solution)/shard_map/all_to_all | solution.py:19
  158.4 5.0 %collective-permute-start.5 = (f32[512,256]{1,0:T(8,128)S(1)}, f32[512,256]{1,0:T(8,128)S(1)}, u32[]{:S(2)}, u32[]{:S(2)}) collective-permute-start(f32[512,256]{1,0:T(8,128)S(1)} %fusion.6), channel_id=1, source_target_pairs={{0,1},{1,0},{2,3},{3,2},{4,5},{5,4},{6,7},{7,6},{8,9},{9,8},{10,11... | collective-permute-start | bytes 1572872 | tf_op jit(solution)/shard_map/ppermute | solution.py:256
  164.2 0.8 collective-permute-done.5
  165.0 1.3 fusion.9
  166.2 6.4 %all-to-all-start.7 = ((f32[64,8,256]{2,1,0:T(8,128)}), f32[64,8,256]{2,1,0:T(8,128)S(1)}, u32[]{:S(2)}, u32[]{:S(2)}) async-start(f32[64,8,256]{2,1,0:T(8,128)} %fusion.9), calls=%async_computation.7 | async-start | bytes 1048576 | tf_op jit(solution)/shard_map/all_to_all | solution.py:258
  172.6 0.6 reduce_sum.203
  173.3 0.6 dynamic_slice.52
  174.5 0.7 iota_compare_fusion.20
  175.2 0.7 slice_reduce_fusion.4
  176.6 12.8 %all-to-all-done.7 = f32[64,8,256]{2,1,0:T(8,128)S(1)} async-done(((f32[64,8,256]{2,1,0:T(8,128)}), f32[64,8,256]{2,1,0:T(8,128)S(1)}, u32[]{:S(2)}, u32[]{:S(2)}) %all-to-all-start.7) | async-done | bytes 524320 | tf_op jit(solution)/shard_map/all_to_all | solution.py:258
  189.4 0.7 multiply_reduce_fusion.1
  (67 shorter events, 6.2 us)
Async XLA Ops:
  7.2 56.2 %copy-start.1 = (bf16[512,512]{1,0:T(8,128)(2,1)S(1)}, bf16[512,512]{1,0:T(8,128)(2,1)}, u32[]{:S(2)}) copy-start(bf16[512,512]{1,0:T(8,128)(2,1)} %param.14) | copy-start | bytes 1572868
  7.2 103.8 %all-gather.2.cloned.1.call-start = ((), (), s32[]{:S(2)}) async-start(), calls=%async_computation.8 | async-start | bytes 2359296 | tf_op jit(solution)/shard_map/all_gather | solution.py:143
  33.4 36.5 %copy-start.4 = (s32[512]{0:T(512)S(1)}, s32[512]{0:T(512)}, u32[]{:S(2)}) copy-start(s32[512]{0:T(512)} %param.17) | copy-start | bytes 6148
  35.7 21.4 %all-to-all-start.1 = ((bf16[8,128,128]{2,1,0:T(8,128)(2,1)}), bf16[8,128,128]{2,1,0:T(8,128)(2,1)S(1)}, u32[]{:S(2)}, u32[]{:S(2)}) async-start(bf16[8,128,128]{2,1,0:T(8,128)(2,1)} %broadcast_in_dim.235), calls=%async_computation.1 | async-start | bytes 524288 | tf_op jit(solution)/shard_map/all_to_all | solution.py:19
  57.1 0.7 copy-start.2
  59.9 4.6 %collective-permute-start = (bf16[2,256,128]{2,1,0:T(8,128)(2,1)}, bf16[2,256,128]{2,1,0:T(8,128)(2,1)S(1)}, u32[]{:S(2)}, u32[]{:S(2)}) collective-permute-start(bf16[2,256,128]{2,1,0:T(8,128)(2,1)} %pack_rows.2), channel_id=1, source_target_pairs={{0,1},{1,0},{2,3},{3,2},{4,5},{5,4},{6,7},{7,6},{8,9},{9,8},{10,11... | collective-permute-start | bytes 393224 | tf_op jit(solution)/shard_map/ppermute | solution.py:179
  65.7 13.3 %all-to-all-start.2 = ((f32[4,64,512]{2,1,0:T(8,128)}), f32[4,64,512]{2,1,0:T(8,128)S(1)}, u32[]{:S(2)}, u32[]{:S(2)}) async-start(f32[4,64,512]{2,1,0:T(8,128)} %bitcast.7), calls=%async_computation.2 | async-start | bytes 1048576 | tf_op jit(solution)/shard_map/all_to_all | solution.py:181
  98.7 12.3 %all-to-all-start.3 = ((f32[4,64,512]{2,1,0:T(8,128)}), f32[4,64,512]{2,1,0:T(8,128)S(1)}, u32[]{:S(2)}, u32[]{:S(2)}) async-start(f32[4,64,512]{2,1,0:T(8,128)} %broadcast_in_dim.236), calls=%async_computation.3 | async-start | bytes 1048576 | tf_op jit(solution)/shard_map/all_to_all | solution.py:19
  115.6 7.4 %collective-permute-start.1 = (bf16[2,256,1024]{2,1,0:T(8,128)(2,1)}, bf16[2,256,1024]{2,1,0:T(8,128)(2,1)S(1)}, u32[]{:S(2)}, u32[]{:S(2)}) collective-permute-start(bf16[2,256,1024]{2,1,0:T(8,128)(2,1)} %pack_rows.3), channel_id=1, source_target_pairs={{0,1},{1,0},{2,3},{3,2},{4,5},{5,4},{6,7},{7,6},{8,9},{9,8},{10,11... | collective-permute-start | bytes 3145736 | tf_op jit(solution)/shard_map/ppermute | solution.py:207
  119.1 3.8 %copy-start = (bf16[1,4096,512]{2,1,0:T(8,128)(2,1)S(1)}, bf16[1,4096,512]{2,1,0:T(8,128)(2,1)}, u32[]{:S(2)}) copy-start(bf16[1,4096,512]{2,1,0:T(8,128)(2,1)} %param.12) | copy-start | bytes 12582916
  122.9 7.7 %copy-start.3 = (s32[128]{0:T(128)S(1)}, s32[128]{0:T(128)}, u32[]{:S(2)}) copy-start(s32[128]{0:T(128)} %param.16) | copy-start | bytes 1540
  125.2 22.1 %all-to-all-start.5 = ((f32[128,1,768]{2,1,0:T(1,128)}), f32[128,1,768]{2,1,0:T(1,128)S(1)}, u32[]{:S(2)}, u32[]{:S(2)}) async-start(f32[128,1,768]{2,1,0:T(1,128)} %broadcast_in_dim.243), calls=%async_computation.5 | async-start | bytes 786432 | tf_op jit(solution)/shard_map/all_to_all | solution.py:19
  132.5 24.4 %collective-permute-start.2 = (bf16[256,512]{1,0:T(8,128)(2,1)S(1)}, bf16[256,512]{1,0:T(8,128)(2,1)S(1)}, u32[]{:S(2)}, u32[]{:S(2)}) collective-permute-start(bf16[256,512]{1,0:T(8,128)(2,1)S(1)} %get-tuple-element.34), channel_id=1, source_target_pairs={{0,128},{128,256},{256,384},{384,0},{1,129},{129,257},{257,385},{3... | collective-permute-start | bytes 786440 | tf_op jit(solution)/shard_map/ppermute | solution.py:212
  134.7 22.2 %collective-permute-start.3 = (bf16[256,512]{1,0:T(8,128)(2,1)S(1)}, bf16[256,512]{1,0:T(8,128)(2,1)S(1)}, u32[]{:S(2)}, u32[]{:S(2)}) collective-permute-start(bf16[256,512]{1,0:T(8,128)(2,1)S(1)} %get-tuple-element.34), channel_id=1, source_target_pairs={{0,256},{128,384},{256,0},{384,128},{1,257},{129,385},{257,1},{385... | collective-permute-start | bytes 786440 | tf_op jit(solution)/shard_map/ppermute | solution.py:212
  138.4 18.6 %collective-permute-start.4 = (bf16[256,512]{1,0:T(8,128)(2,1)S(1)}, bf16[256,512]{1,0:T(8,128)(2,1)S(1)}, u32[]{:S(2)}, u32[]{:S(2)}) collective-permute-start(bf16[256,512]{1,0:T(8,128)(2,1)S(1)} %get-tuple-element.34), channel_id=1, source_target_pairs={{0,384},{128,0},{256,128},{384,256},{1,385},{129,1},{257,129},{385... | collective-permute-start | bytes 786440 | tf_op jit(solution)/shard_map/ppermute | solution.py:212
  149.4 7.4 %all-to-all-start.6 = ((f32[4,3,128]{2,1,0:T(4,128)}), f32[4,3,128]{2,1,0:T(4,128)S(1)}, u32[]{:S(2)}, u32[]{:S(2)}) async-start(f32[4,3,128]{2,1,0:T(4,128)} %broadcast_in_dim.246), calls=%async_computation.6 | async-start | bytes 16384 | tf_op jit(solution)/shard_map/all_to_all | solution.py:19
  157.0 18.2 %copy-start.5 = (s32[1,4]{1,0:T(1,128)S(1)}, s32[1,4]{1,0:T(1,128)}, u32[]{:S(2)}) copy-start(s32[1,4]{1,0:T(1,128)} %refs_0_.1) | copy-start | bytes 52
  158.4 6.5 %collective-permute-start.5 = (f32[512,256]{1,0:T(8,128)S(1)}, f32[512,256]{1,0:T(8,128)S(1)}, u32[]{:S(2)}, u32[]{:S(2)}) collective-permute-start(f32[512,256]{1,0:T(8,128)S(1)} %fusion.6), channel_id=1, source_target_pairs={{0,1},{1,0},{2,3},{3,2},{4,5},{5,4},{6,7},{7,6},{8,9},{9,8},{10,11... | collective-permute-start | bytes 1572872 | tf_op jit(solution)/shard_map/ppermute | solution.py:256
  166.2 23.1 %all-to-all-start.7 = ((f32[64,8,256]{2,1,0:T(8,128)}), f32[64,8,256]{2,1,0:T(8,128)S(1)}, u32[]{:S(2)}, u32[]{:S(2)}) async-start(f32[64,8,256]{2,1,0:T(8,128)} %fusion.9), calls=%async_computation.7 | async-start | bytes 1048576 | tf_op jit(solution)/shard_map/all_to_all | solution.py:258
Sparse Core Ops, SparseCore 0:
  34.3 40.4 all-gather.1

commit v4 on v3

--- a/solution.py
+++ b/solution.py
@@ -64,47 +64,56 @@
     )(slot_ids, teacher_hidden, teacher_gain, student_hidden)
 
 
-def pack_kernel(places_ref, rows_ref, packed_ref, one_ref):
+def one_hot_kernel(places_ref, rows_ref, packed_ref, one_ref):
     live = packed_ref.shape[1]
-
-    @pl.when(pl.program_id(0) == 0)
-    def _():
-        ids = lax.broadcasted_iota(jnp.int32, (live, places_ref.shape[1]), 0)
-        for side in range(2):
-            one_ref[side] = (ids == places_ref[side : side + 1, :]).astype(BF16)
-
+    ids = lax.broadcasted_iota(jnp.int32, (live, places_ref.shape[1]), 0)
+    for side in range(2):
+        one_ref[side] = (ids == places_ref[side : side + 1, :]).astype(BF16)
+        packed_ref[side] = jnp.dot(
+            one_ref[side], rows_ref[...], preferred_element_type=F32
+        ).astype(BF16)
+
+
+def pack_with_places(places, rows, live):
+    total, features = rows.shape
+    return pl.pallas_call(
+        one_hot_kernel,
+        out_shape=(
+            jax.ShapeDtypeStruct((2, live, features), BF16),
+            jax.ShapeDtypeStruct((2, live, total), BF16),
+        ),
+        name="pack_student",
+    )(places, rows)
+
+
+def pack_kernel(one_ref, rows_ref, packed_ref):
     for side in range(2):
         packed_ref[side] = jnp.dot(
             one_ref[side], rows_ref[...], preferred_element_type=F32
         ).astype(BF16)
 
 
-def pack_rows(places, rows, live, parts):
+def pack_rows(one, rows, parts):
     total, features = rows.shape
+    live = one.shape[1]
     part = features // parts
     return pl.pallas_call(
         pack_kernel,
         grid=(parts,),
         out_shape=jax.ShapeDtypeStruct((2, live, features), BF16),
         in_specs=[
-            pl.BlockSpec((2, total), lambda i: (0, 0)),
+            pl.BlockSpec((2, live, total), lambda i: (0, 0, 0)),
             pl.BlockSpec((total, part), lambda i: (0, i)),
         ],
         out_specs=pl.BlockSpec((2, live, part), lambda i: (0, 0, i)),
-        scratch_shapes=[pltpu.VMEM((2, live, total), BF16)],
-        name="pack_rows",
-    )(places, rows)
+        name="pack_teacher",
+    )(one, rows)
 
 
 def softmax_stats(logits):
     top = jnp.max(logits, axis=1)
     shifted = jnp.exp(logits - top[:, None])
     return top, shifted, jnp.sum(shifted, axis=1)
-
-
-def row_stats(*columns):
-    flat = jnp.concatenate(columns)
-    return flat.reshape(-1, 128)
 
 
 def on_device(
@@ -175,7 +184,7 @@
 
     student_rows = spread(group_rows[:, quarter:], "y", lax.axis_size("y"))
     student_rows = student_rows.reshape(2 * padded, -1)
-    mine = pack_rows(side_places, student_rows, live_rows, 1)
+    mine, one = pack_with_places(side_places, student_rows, live_rows)
     partial_logits = both_halves(mine, lax.ppermute(mine, "core", swap), student_head)
     logits_chunk = jnp.sum(
         lax.all_to_all(
@@ -191,19 +200,10 @@
         live_targets, member * chunk, chunk
     )[:, None]
     target_part = jnp.sum(jnp.where(hit_chunk, logits_chunk, 0.0), axis=1)
-    every = spread(
-        row_stats(top, total, target_part, jnp.zeros_like(top)), OWNERS, owners
-    ).reshape(owners, 4 * chunk)
-    tops = every[:, :chunk]
-    highest = jnp.max(tops, axis=0)
-    totals = jnp.sum(every[:, chunk : 2 * chunk] * jnp.exp(tops - highest[None, :]), axis=0)
-    log_chunk = highest + jnp.log(totals)
-    student_loss = jnp.sum(log_chunk) - BLEND * jnp.sum(every[:, 2 * chunk : 3 * chunk])
-
-    teacher_rows, student_logits, log_chunk = lax.optimization_barrier(
-        (teacher_rows, student_logits, log_chunk)
-    )
-    mine = pack_rows(side_places, teacher_rows, live_rows, 4)
+    student_stats = jnp.concatenate([top, total, target_part, jnp.zeros_like(top)])
+
+    teacher_rows, student_stats = lax.optimization_barrier((teacher_rows, student_stats))
+    mine = pack_rows(one, teacher_rows, 2)
     teacher_logits = both_halves(mine, lax.ppermute(mine, "core", swap), teacher_head[0])
     top, shifted, total = softmax_stats(teacher_logits)
     cross = jnp.sum(shifted * student_logits, axis=1)
@@ -212,13 +212,23 @@
         lax.ppermute(shifted, "member", [(i, (i + step) % members) for i in range(members)])
         for step in range(1, members)
     ]
-    every = spread(jnp.concatenate([top, total, cross])[None], OWNERS, owners)
-    every = every.reshape(owners, 3 * live_rows)
+    every = spread(jnp.concatenate([top, total, cross, student_stats])[None], OWNERS, owners)
+    every = every.reshape(owners, -1)
+    student_every = every[:, 3 * live_rows :]
+    student_tops = student_every[:, :chunk]
+    highest = jnp.max(student_tops, axis=0)
+    totals = jnp.sum(
+        student_every[:, chunk : 2 * chunk] * jnp.exp(student_tops - highest[None, :]), axis=0
+    )
+    log_chunk = highest + jnp.log(totals)
+    student_loss = jnp.sum(log_chunk) - BLEND * jnp.sum(
+        student_every[:, 2 * chunk : 3 * chunk]
+    )
     tops = every[:, :live_rows]
     highest = jnp.max(tops, axis=0)
     scales = jnp.exp(tops - highest[None, :])
     totals = jnp.sum(every[:, live_rows : 2 * live_rows] * scales, axis=0)
-    crosses = jnp.sum(every[:, 2 * live_rows :] * scales, axis=0)
+    crosses = jnp.sum(every[:, 2 * live_rows : 3 * live_rows] * scales, axis=0)
     factor = jnp.exp(top - highest) / totals
     loss = student_loss - (1.0 - BLEND) / members * jnp.sum(crosses / totals)
     factors = spread(
@@ -254,8 +264,8 @@
         return result
 
     arrived = lax.ppermute(term(1 - core), "core", swap)
-    grads = (term(core) + arrived).reshape(chips, 2 * cap, half)
-    owned = jnp.sum(lax.all_to_all(grads, CHIPS, 0, 0, tiled=True), axis=0)
+    grads = (term(core) + arrived).astype(BF16).reshape(chips, 2 * cap, half)
+    owned = jnp.sum(lax.all_to_all(grads, CHIPS, 0, 0, tiled=True).astype(F32), axis=0)
     slot_grad = jnp.concatenate([owned[:cap], owned[cap:]], axis=1)
     live_here = slots < lax.dynamic_index_in_dim(counts, owner, keepdims=False)
     placed = (

time: 201 us -> 178 us (0.89)
  blocking collectives: 42.5 us -> 24.2 us
    all_to_all x1 -> x0, blocking collectives: 18.3 us -> none  [spread(): lax.all_to_all(jnp.broadcast_to(block[None], (size,) + block.shape), axes...]
    all_to_all x1, waiting for transfers between devices: 12.8 us -> 9.49 us  [on_device(): lax.all_to_all(grads, CHIPS, 0, 0, tiled=True).astype(F32)]
    pallas_call x2 -> x1, Pallas kernels: 6.68 us -> 3.81 us  [pack_rows(): pl.pallas_call(pack_kernel, grid=(parts,), out_shape=jax.ShapeDtypeStruct...]
    pallas_call x0 -> x1, Pallas kernels: none -> 2.41 us  [pack_with_places(): pl.pallas_call(one_hot_kernel, out_shape=(jax.ShapeDtypeStruct((2, live,...]
  transfers between devices with their start and end apart: 13 -> 13, of which waited for: 7 -> 7; matrix products, arithmetic and copies ran while one was open for 10% -> 12% of each run, Pallas kernels for 1% -> 1%
where the time goes in v4:
time: 178 us; the launch traced here: 177 us
  waiting for transfers between devices  50.7 us (28%)
  starting transfers between devices  48.1 us (27%)
  blocking collectives  24.2 us (14%)
  between operations  19 us (11%)
  matrix products  10.8 us (6%)
  other arithmetic  9 us (5%)
  Pallas kernels  8.19 us (5%)
  local copies, waits for them, and re-layouts  6.89 us (4%)
    all_to_all x4, waiting for transfers between devices, spread(): lax.all_to_all(jnp.broadcast_to(block[None], (size,) + block.shape), axes...  31.5 us
    all_to_all x1, blocking collectives, on_device(): group_rows = lax.all_to_all(sent, ('z', 'core'), 0, 0, tiled=True)  24.2 us
    all_to_all x4, starting transfers between devices, spread(): lax.all_to_all(jnp.broadcast_to(block[None], (size,) + block.shape), axes...  20.4 us
    all_to_all x1, waiting for transfers between devices, on_device(): lax.all_to_all(grads, CHIPS, 0, 0, tiled=True).astype(F32)  9.49 us
    all_to_all x1, waiting for transfers between devices, on_device(): lax.all_to_all(partial_logits.reshape(members, chunk, vocab), 'member', 0...  8.93 us
    ppermute x3, starting transfers between devices, on_device(): lax.ppermute(shifted, 'member', [(i, (i + step) % members) for i in range...  8.41 us
    dot_general x8, matrix products, both_halves(): jnp.dot(values[side], lax.dynamic_slice_in_dim(weights, first + side * pa...  8.19 us
    ppermute x2, starting transfers between devices, on_device(): lax.ppermute(mine, 'core', swap)  5.41 us
  transfers between devices with their start and end apart: 13, of which 7 were waited for; matrix products, arithmetic and copies ran while one was open for 12% of the time, Pallas kernels for 1%

profile of v4, /device:TPU:1, one launch (start us, length us, event | category | flops | bytes accessed | tf_op | source)
XLA Modules:
  0.0 176.9 jit_solution(8998105006596712866)
XLA Ops:
  7.2 2.0 %own_rows.1 = bf16[128,1152]{1,0:T(8,128)(2,1)} custom-call(s32[1,4]{1,0:T(1,128)} %refs_0_.1, bf16[1,16,4096]{2,1,0:T(8,128)(2,1)} %refs_1_.1, f32[1,4096]{1,0:T(1,128)} %refs_2_.1, bf16[16,512]{1,0:T(8,128)(2,1)} %refs_3_.1), custom_call_target="tpu_custom_call" | custom-call | tf_op jit(solution)/shard_map/own_rows/pallas_call | solution.py:57
  9.2 24.2 %all_to_all.35 = bf16[16,8,1152]{2,1,0:T(8,128)(2,1)S(1)} all-to-all(bf16[16,8,1152]{2,1,0:T(8,128)(2,1)} %bitcast.84), channel_id=1, replica_groups=mesh['member'=4,'y'=8,'z'=8,'core'=2] {'z','core'}, dimensions={0} | all-to-all | bytes 589824 | tf_op jit(solution)/shard_map/all_to_all | solution.py:150
  33.4 0.7 slice.108
  34.1 0.8 select_reduce_fusion.2
  34.9 0.8 broadcast_in_dim.228
  35.7 6.8 %all-to-all-start.1 = ((bf16[8,128,128]{2,1,0:T(8,128)(2,1)}), bf16[8,128,128]{2,1,0:T(8,128)(2,1)S(1)}, u32[]{:S(2)}, u32[]{:S(2)}) async-start(bf16[8,128,128]{2,1,0:T(8,128)(2,1)} %broadcast_in_dim.228), calls=%async_computation.1 | async-start | bytes 524288 | tf_op jit(solution)/shard_map/all_to_all | solution.py:19
  42.5 0.8 add_select_fusion
  43.8 0.6 pad_add_fusion.places_ref
  44.4 12.7 %all-to-all-done.1 = bf16[8,128,128]{2,1,0:T(8,128)(2,1)S(1)} async-done(((bf16[8,128,128]{2,1,0:T(8,128)(2,1)}), bf16[8,128,128]{2,1,0:T(8,128)(2,1)S(1)}, u32[]{:S(2)}, u32[]{:S(2)}) %all-to-all-start.1) | async-done | bytes 262176 | tf_op jit(solution)/shard_map/all_to_all | solution.py:19
  57.1 0.7 copy-done.2
  57.8 2.4 %pack_student.1 = (bf16[2,256,128]{2,1,0:T(8,128)(2,1)}, bf16[2,256,1024]{2,1,0:T(8,128)(2,1)}) custom-call(s32[2,1024]{1,0:T(2,128)} %pad_add_fusion.places_ref, bf16[1024,128]{1,0:T(8,128)(2,1)} %bitcast.85), custom_call_target="tpu_custom_call" | custom-call | tf_op jit(solution)/shard_map/pack_student/pallas_call | solution.py:79
  60.2 2.4 %collective-permute-start = (bf16[2,256,128]{2,1,0:T(8,128)(2,1)}, bf16[2,256,128]{2,1,0:T(8,128)(2,1)S(1)}, u32[]{:S(2)}, u32[]{:S(2)}) collective-permute-start(bf16[2,256,128]{2,1,0:T(8,128)(2,1)} %get-tuple-element.8), channel_id=1, source_target_pairs={{0,1},{1,0},{2,3},{3,2},{4,5},{5,4},{6,7},{7,6},{8,9},{9,8},{10,11... | collective-permute-start | bytes 393224 | tf_op jit(solution)/shard_map/ppermute | solution.py:188
  62.6 1.2 fusion.47
  63.8 1.1 convolution_add_fusion.3
  65.1 1.0 fusion.5
  66.1 4.1 %all-to-all-start.2 = ((f32[4,64,512]{2,1,0:T(8,128)}), f32[4,64,512]{2,1,0:T(8,128)S(1)}, u32[]{:S(2)}, u32[]{:S(2)}) async-start(f32[4,64,512]{2,1,0:T(8,128)} %bitcast.7), calls=%async_computation.2 | async-start | bytes 1048576 | tf_op jit(solution)/shard_map/all_to_all | solution.py:190
  70.5 8.9 %all-to-all-done.2 = f32[4,64,512]{2,1,0:T(8,128)S(1)} async-done(((f32[4,64,512]{2,1,0:T(8,128)}), f32[4,64,512]{2,1,0:T(8,128)S(1)}, u32[]{:S(2)}, u32[]{:S(2)}) %all-to-all-start.2) | async-done | bytes 524320 | tf_op jit(solution)/shard_map/all_to_all | solution.py:190
  79.9 3.8 %pack_teacher.1 = bf16[2,256,1024]{2,1,0:T(8,128)(2,1)} custom-call(bf16[2,256,1024]{2,1,0:T(8,128)(2,1)} %get-tuple-element.7.one_ref, bf16[1024,1024]{1,0:T(8,128)(2,1)} %all-gather.2.cloned.1.call-done.rows_ref), custom_call_target="tpu_custom_call" | custom-call | tf_op jit(solution)/shard_map/pack_teacher/pallas_call | solution.py:100
  83.7 3.1 %collective-permute-start.1 = (bf16[2,256,1024]{2,1,0:T(8,128)(2,1)}, bf16[2,256,1024]{2,1,0:T(8,128)(2,1)S(1)}, u32[]{:S(2)}, u32[]{:S(2)}) collective-permute-start(bf16[2,256,1024]{2,1,0:T(8,128)(2,1)} %pack_teacher.1), channel_id=1, source_target_pairs={{0,1},{1,0},{2,3},{3,2},{4,5},{5,4},{6,7},{7,6},{8,9},{9,8},{10,11... | collective-permute-start | bytes 3145736 | tf_op jit(solution)/shard_map/ppermute | solution.py:207
  86.7 0.8 broadcast_in_dim.233
  87.6 3.5 %all-to-all-start.3 = ((f32[4,64,512]{2,1,0:T(8,128)}), f32[4,64,512]{2,1,0:T(8,128)S(1)}, u32[]{:S(2)}, u32[]{:S(2)}) async-start(f32[4,64,512]{2,1,0:T(8,128)} %broadcast_in_dim.233), calls=%async_computation.3 | async-start | bytes 1048576 | tf_op jit(solution)/shard_map/all_to_all | solution.py:19
  91.1 2.0 %fusion.15 = f32[256,512]{1,0:T(8,128)S(1)} fusion(bf16[1,4096,512]{2,1,0:T(8,128)(2,1)} %param.12, s32[]{:T(128)S(6)} %select_n.185, bf16[2,256,1024]{2,1,0:T(8,128)(2,1)} %pack_teacher.1), kind=kOutput, calls=%fused_computation.23 | convolution fusion | flops 268435456 | bytes 2097156 | tf_op jit(solution)/shard_map/dot_general | solution.py:178
  93.1 1.8 %convolution_add_fusion.1 = f32[256,512]{1,0:T(8,128)S(1)} fusion(f32[256,512]{1,0:T(8,128)S(1)} %fusion.15, bf16[1,4096,512]{2,1,0:T(8,128)(2,1)} %param.12, s32[]{:T(128)S(6)} %select_n.186, bf16[2,256,1024]{2,1,0:T(8,128)(2,1)} %pack_teacher.1), kind=kOutput, calls=%fused_computation.5 | convolution fusion | flops 268566528 | bytes 2621444 | tf_op jit(solution)/shard_map/dot_general | solution.py:178
  95.4 0.5 fusion.66
  95.9 4.8 %all-to-all-done.3 = f32[4,64,512]{2,1,0:T(8,128)S(1)} async-done(((f32[4,64,512]{2,1,0:T(8,128)}), f32[4,64,512]{2,1,0:T(8,128)S(1)}, u32[]{:S(2)}, u32[]{:S(2)}) %all-to-all-start.3) | async-done | bytes 524320 | tf_op jit(solution)/shard_map/all_to_all | solution.py:19
  101.0 1.1 broadcast_in_dim.234
  102.0 6.9 %all-to-all-start.4 = ((f32[128,1,1024]{2,1,0:T(1,128)}), f32[128,1,1024]{2,1,0:T(1,128)S(1)}, u32[]{:S(2)}, u32[]{:S(2)}) async-start(f32[128,1,1024]{2,1,0:T(1,128)} %broadcast_in_dim.234), calls=%async_computation.4 | async-start | bytes 1048576 | tf_op jit(solution)/shard_map/all_to_all | solution.py:19
  109.8 2.2 %collective-permute-start.2 = (bf16[256,512]{1,0:T(8,128)(2,1)S(1)}, bf16[256,512]{1,0:T(8,128)(2,1)S(1)}, u32[]{:S(2)}, u32[]{:S(2)}) collective-permute-start(bf16[256,512]{1,0:T(8,128)(2,1)S(1)} %get-tuple-element.36), channel_id=1, source_target_pairs={{0,128},{128,256},{256,384},{384,0},{1,129},{129,257},{257,385},{3... | collective-permute-start | bytes 786440 | tf_op jit(solution)/shard_map/ppermute | solution.py:212
  112.0 3.7 %collective-permute-start.3 = (bf16[256,512]{1,0:T(8,128)(2,1)S(1)}, bf16[256,512]{1,0:T(8,128)(2,1)S(1)}, u32[]{:S(2)}, u32[]{:S(2)}) collective-permute-start(bf16[256,512]{1,0:T(8,128)(2,1)S(1)} %get-tuple-element.36), channel_id=1, source_target_pairs={{0,256},{128,384},{256,0},{384,128},{1,257},{129,385},{257,1},{385... | collective-permute-start | bytes 786440 | tf_op jit(solution)/shard_map/ppermute | solution.py:212
  115.7 2.5 %collective-permute-start.4 = (bf16[256,512]{1,0:T(8,128)(2,1)S(1)}, bf16[256,512]{1,0:T(8,128)(2,1)S(1)}, u32[]{:S(2)}, u32[]{:S(2)}) collective-permute-start(bf16[256,512]{1,0:T(8,128)(2,1)S(1)} %get-tuple-element.36), channel_id=1, source_target_pairs={{0,384},{128,0},{256,128},{384,256},{1,385},{129,1},{257,129},{385... | collective-permute-start | bytes 786440 | tf_op jit(solution)/shard_map/ppermute | solution.py:212
  118.2 10.2 %all-to-all-done.4 = f32[128,1,1024]{2,1,0:T(1,128)S(1)} async-done(((f32[128,1,1024]{2,1,0:T(1,128)}), f32[128,1,1024]{2,1,0:T(1,128)S(1)}, u32[]{:S(2)}, u32[]{:S(2)}) %all-to-all-start.4) | async-done | bytes 524320 | tf_op jit(solution)/shard_map/all_to_all | solution.py:19
  128.6 0.6 slice_reduce_fusion.1
  129.2 0.6 fusion.64
  129.8 0.7 exponential_divide_fusion
  132.6 0.6 broadcast_in_dim.237
  133.2 3.2 %all-to-all-start.5 = ((f32[4,3,128]{2,1,0:T(4,128)}), f32[4,3,128]{2,1,0:T(4,128)S(1)}, u32[]{:S(2)}, u32[]{:S(2)}) async-start(f32[4,3,128]{2,1,0:T(4,128)} %broadcast_in_dim.237), calls=%async_computation.5 | async-start | bytes 16384 | tf_op jit(solution)/shard_map/all_to_all | solution.py:19
  136.7 3.9 %all-to-all-done.5 = f32[4,3,128]{2,1,0:T(4,128)S(1)} async-done(((f32[4,3,128]{2,1,0:T(4,128)}), f32[4,3,128]{2,1,0:T(4,128)S(1)}, u32[]{:S(2)}, u32[]{:S(2)}) %all-to-all-start.5) | async-done | bytes 6176 | tf_op jit(solution)/shard_map/all_to_all | solution.py:19
  142.3 5.1 %collective-permute-start.5 = (f32[512,256]{1,0:T(8,128)S(1)}, f32[512,256]{1,0:T(8,128)S(1)}, u32[]{:S(2)}, u32[]{:S(2)}) collective-permute-start(f32[512,256]{1,0:T(8,128)S(1)} %fusion.6), channel_id=1, source_target_pairs={{0,1},{1,0},{2,3},{3,2},{4,5},{5,4},{6,7},{7,6},{8,9},{9,8},{10,11... | collective-permute-start | bytes 1572872 | tf_op jit(solution)/shard_map/ppermute | solution.py:266
  147.6 0.5 fusion.1
  148.1 0.8 collective-permute-done.5
  148.9 1.2 fusion.10
  150.1 4.6 %all-to-all-start.6 = ((bf16[64,8,256]{2,1,0:T(8,128)(2,1)}), bf16[64,8,256]{2,1,0:T(8,128)(2,1)S(1)}, u32[]{:S(2)}, u32[]{:S(2)}) async-start(bf16[64,8,256]{2,1,0:T(8,128)(2,1)} %fusion.10), calls=%async_computation.6 | async-start | bytes 524288 | tf_op jit(solution)/shard_map/all_to_all | solution.py:268
  154.7 0.6 reduce_sum.203
  155.3 0.6 dynamic_slice.52
  156.6 0.7 iota_compare_fusion.20
  157.3 0.7 slice_reduce_fusion.4
  158.7 9.5 %all-to-all-done.6 = bf16[64,8,256]{2,1,0:T(8,128)(2,1)S(1)} async-done(((bf16[64,8,256]{2,1,0:T(8,128)(2,1)}), bf16[64,8,256]{2,1,0:T(8,128)(2,1)S(1)}, u32[]{:S(2)}, u32[]{:S(2)}) %all-to-all-start.6) | async-done | bytes 262176 | tf_op jit(solution)/shard_map/all_to_all | solution.py:268
  168.2 0.7 multiply_reduce_fusion
  (64 shorter events, 5.6 us)
Async XLA Ops:
  7.2 56.6 %copy-start.1 = (bf16[512,512]{1,0:T(8,128)(2,1)S(1)}, bf16[512,512]{1,0:T(8,128)(2,1)}, u32[]{:S(2)}) copy-start(bf16[512,512]{1,0:T(8,128)(2,1)} %param.14) | copy-start | bytes 1572868
  7.2 72.7 %all-gather.2.cloned.1.call-start = ((), (), s32[]{:S(2)}) async-start(), calls=%async_computation.7 | async-start | bytes 2359296 | tf_op jit(solution)/shard_map/all_gather | solution.py:152
  33.4 36.9 %copy-start.4 = (s32[512]{0:T(512)S(1)}, s32[512]{0:T(512)}, u32[]{:S(2)}) copy-start(s32[512]{0:T(512)} %param.17) | copy-start | bytes 6148
  35.7 21.4 %all-to-all-start.1 = ((bf16[8,128,128]{2,1,0:T(8,128)(2,1)}), bf16[8,128,128]{2,1,0:T(8,128)(2,1)S(1)}, u32[]{:S(2)}, u32[]{:S(2)}) async-start(bf16[8,128,128]{2,1,0:T(8,128)(2,1)} %broadcast_in_dim.228), calls=%async_computation.1 | async-start | bytes 524288 | tf_op jit(solution)/shard_map/all_to_all | solution.py:19
  57.1 0.7 copy-start.2
  60.2 4.6 %collective-permute-start = (bf16[2,256,128]{2,1,0:T(8,128)(2,1)}, bf16[2,256,128]{2,1,0:T(8,128)(2,1)S(1)}, u32[]{:S(2)}, u32[]{:S(2)}) collective-permute-start(bf16[2,256,128]{2,1,0:T(8,128)(2,1)} %get-tuple-element.8), channel_id=1, source_target_pairs={{0,1},{1,0},{2,3},{3,2},{4,5},{5,4},{6,7},{7,6},{8,9},{9,8},{10,11... | collective-permute-start | bytes 393224 | tf_op jit(solution)/shard_map/ppermute | solution.py:188
  66.1 13.3 %all-to-all-start.2 = ((f32[4,64,512]{2,1,0:T(8,128)}), f32[4,64,512]{2,1,0:T(8,128)S(1)}, u32[]{:S(2)}, u32[]{:S(2)}) async-start(f32[4,64,512]{2,1,0:T(8,128)} %bitcast.7), calls=%async_computation.2 | async-start | bytes 1048576 | tf_op jit(solution)/shard_map/all_to_all | solution.py:190
  83.7 11.2 %collective-permute-start.1 = (bf16[2,256,1024]{2,1,0:T(8,128)(2,1)}, bf16[2,256,1024]{2,1,0:T(8,128)(2,1)S(1)}, u32[]{:S(2)}, u32[]{:S(2)}) collective-permute-start(bf16[2,256,1024]{2,1,0:T(8,128)(2,1)} %pack_teacher.1), channel_id=1, source_target_pairs={{0,1},{1,0},{2,3},{3,2},{4,5},{5,4},{6,7},{7,6},{8,9},{9,8},{10,11... | collective-permute-start | bytes 3145736 | tf_op jit(solution)/shard_map/ppermute | solution.py:207
  87.6 13.1 %all-to-all-start.3 = ((f32[4,64,512]{2,1,0:T(8,128)}), f32[4,64,512]{2,1,0:T(8,128)S(1)}, u32[]{:S(2)}, u32[]{:S(2)}) async-start(f32[4,64,512]{2,1,0:T(8,128)} %broadcast_in_dim.233), calls=%async_computation.3 | async-start | bytes 1048576 | tf_op jit(solution)/shard_map/all_to_all | solution.py:19
  91.1 3.9 %copy-start = (bf16[1,4096,512]{2,1,0:T(8,128)(2,1)S(1)}, bf16[1,4096,512]{2,1,0:T(8,128)(2,1)}, u32[]{:S(2)}) copy-start(bf16[1,4096,512]{2,1,0:T(8,128)(2,1)} %param.12) | copy-start | bytes 12582916
  94.9 14.2 %copy-start.3 = (s32[128]{0:T(128)S(1)}, s32[128]{0:T(128)}, u32[]{:S(2)}) copy-start(s32[128]{0:T(128)} %param.16) | copy-start | bytes 1540
  102.0 26.4 %all-to-all-start.4 = ((f32[128,1,1024]{2,1,0:T(1,128)}), f32[128,1,1024]{2,1,0:T(1,128)S(1)}, u32[]{:S(2)}, u32[]{:S(2)}) async-start(f32[128,1,1024]{2,1,0:T(1,128)} %broadcast_in_dim.234), calls=%async_computation.4 | async-start | bytes 1048576 | tf_op jit(solution)/shard_map/all_to_all | solution.py:19
  109.8 31.0 %collective-permute-start.2 = (bf16[256,512]{1,0:T(8,128)(2,1)S(1)}, bf16[256,512]{1,0:T(8,128)(2,1)S(1)}, u32[]{:S(2)}, u32[]{:S(2)}) collective-permute-start(bf16[256,512]{1,0:T(8,128)(2,1)S(1)} %get-tuple-element.36), channel_id=1, source_target_pairs={{0,128},{128,256},{256,384},{384,0},{1,129},{129,257},{257,385},{3... | collective-permute-start | bytes 786440 | tf_op jit(solution)/shard_map/ppermute | solution.py:212
  112.0 28.8 %collective-permute-start.3 = (bf16[256,512]{1,0:T(8,128)(2,1)S(1)}, bf16[256,512]{1,0:T(8,128)(2,1)S(1)}, u32[]{:S(2)}, u32[]{:S(2)}) collective-permute-start(bf16[256,512]{1,0:T(8,128)(2,1)S(1)} %get-tuple-element.36), channel_id=1, source_target_pairs={{0,256},{128,384},{256,0},{384,128},{1,257},{129,385},{257,1},{385... | collective-permute-start | bytes 786440 | tf_op jit(solution)/shard_map/ppermute | solution.py:212
  115.7 25.1 %collective-permute-start.4 = (bf16[256,512]{1,0:T(8,128)(2,1)S(1)}, bf16[256,512]{1,0:T(8,128)(2,1)S(1)}, u32[]{:S(2)}, u32[]{:S(2)}) collective-permute-start(bf16[256,512]{1,0:T(8,128)(2,1)S(1)} %get-tuple-element.36), channel_id=1, source_target_pairs={{0,384},{128,0},{256,128},{384,256},{1,385},{129,1},{257,129},{385... | collective-permute-start | bytes 786440 | tf_op jit(solution)/shard_map/ppermute | solution.py:212
  133.2 7.4 %all-to-all-start.5 = ((f32[4,3,128]{2,1,0:T(4,128)}), f32[4,3,128]{2,1,0:T(4,128)S(1)}, u32[]{:S(2)}, u32[]{:S(2)}) async-start(f32[4,3,128]{2,1,0:T(4,128)} %broadcast_in_dim.237), calls=%async_computation.5 | async-start | bytes 16384 | tf_op jit(solution)/shard_map/all_to_all | solution.py:19
  140.8 16.4 %copy-start.5 = (s32[1,4]{1,0:T(1,128)S(1)}, s32[1,4]{1,0:T(1,128)}, u32[]{:S(2)}) copy-start(s32[1,4]{1,0:T(1,128)} %refs_0_.1) | copy-start | bytes 52
  142.3 6.6 %collective-permute-start.5 = (f32[512,256]{1,0:T(8,128)S(1)}, f32[512,256]{1,0:T(8,128)S(1)}, u32[]{:S(2)}, u32[]{:S(2)}) collective-permute-start(f32[512,256]{1,0:T(8,128)S(1)} %fusion.6), channel_id=1, source_target_pairs={{0,1},{1,0},{2,3},{3,2},{4,5},{5,4},{6,7},{7,6},{8,9},{9,8},{10,11... | collective-permute-start | bytes 1572872 | tf_op jit(solution)/shard_map/ppermute | solution.py:266
  150.1 18.1 %all-to-all-start.6 = ((bf16[64,8,256]{2,1,0:T(8,128)(2,1)}), bf16[64,8,256]{2,1,0:T(8,128)(2,1)S(1)}, u32[]{:S(2)}, u32[]{:S(2)}) async-start(bf16[64,8,256]{2,1,0:T(8,128)(2,1)} %fusion.10), calls=%async_computation.6 | async-start | bytes 524288 | tf_op jit(solution)/shard_map/all_to_all | solution.py:268
Sparse Core Ops, SparseCore 0:
  34.3 40.4 all-gather.1

commit v5 on v4

--- a/solution.py
+++ b/solution.py
@@ -108,6 +108,42 @@
         out_specs=pl.BlockSpec((2, live, part), lambda i: (0, 0, i)),
         name="pack_teacher",
     )(one, rows)
+
+
+def combine_kernel(every_ref, top_ref, sent_ref):
+    live = top_ref.shape[1]
+    chunk = (every_ref.shape[2] - 2 * live) // 2
+    copies = sent_ref.shape[0]
+
+    def totals(first, count):
+        tops = every_ref[:, :, first : first + count]
+        highest = jnp.max(tops, axis=0)
+        sums = every_ref[:, :, first + count : first + 2 * count]
+        return highest, jnp.sum(sums * jnp.exp(tops - highest[None]), axis=0)
+
+    highest, total = totals(0, live)
+    factor = jnp.exp(top_ref[...] - highest) / total
+    highest, total = totals(2 * live, chunk)
+    log_total = highest + jnp.log(total)
+    for copy in range(copies):
+        sent_ref[copy, :, :live] = factor
+        sent_ref[copy, :, live:] = jnp.concatenate([log_total, log_total], axis=1)
+
+
+def combine(every, top, copies):
+    live = top.shape[0]
+    return pl.pallas_call(
+        combine_kernel,
+        out_shape=jax.ShapeDtypeStruct((copies, 1, live + 128), F32),
+        name="combine",
+    )(every, top[None])
+
+
+def three_parts(values):
+    high = lax.reduce_precision(values, 8, 7)
+    rest = values - high
+    middle = lax.reduce_precision(rest, 8, 7)
+    return [part.astype(BF16) for part in (high, middle, rest - middle)]
 
 
 def softmax_stats(logits):
@@ -192,81 +228,65 @@
         ),
         axis=0,
     )
-    student_logits = spread(logits_chunk, "member", members).reshape(live_rows, vocab)
-    top, _, total = softmax_stats(logits_chunk)
+    student_top, _, student_total = softmax_stats(logits_chunk)
     vocab_ids = owner * vocab + jnp.arange(vocab, dtype=jnp.int32)
     hit = vocab_ids[None, :] == live_targets[:, None]
-    hit_chunk = vocab_ids[None, :] == lax.dynamic_slice_in_dim(
-        live_targets, member * chunk, chunk
-    )[:, None]
-    target_part = jnp.sum(jnp.where(hit_chunk, logits_chunk, 0.0), axis=1)
-    student_stats = jnp.concatenate([top, total, target_part, jnp.zeros_like(top)])
-
-    teacher_rows, student_stats = lax.optimization_barrier((teacher_rows, student_stats))
+    teacher_rows, student_top, student_total = lax.optimization_barrier(
+        (teacher_rows, student_top, student_total)
+    )
     mine = pack_rows(one, teacher_rows, 2)
     teacher_logits = both_halves(mine, lax.ppermute(mine, "core", swap), teacher_head[0])
     top, shifted, total = softmax_stats(teacher_logits)
-    cross = jnp.sum(shifted * student_logits, axis=1)
-    shifted = shifted.astype(BF16)
-    arrived = [shifted] + [
-        lax.ppermute(shifted, "member", [(i, (i + step) % members) for i in range(members)])
+    every = spread(
+        jnp.concatenate([top, total, student_top, student_total])[None], OWNERS, owners
+    )
+    shared = jnp.concatenate([shifted.astype(BF16)] + three_parts(logits_chunk), axis=0)
+    arrived = [shared] + [
+        lax.ppermute(shared, "member", [(i, (i + step) % members) for i in range(members)])
         for step in range(1, members)
     ]
-    every = spread(jnp.concatenate([top, total, cross, student_stats])[None], OWNERS, owners)
-    every = every.reshape(owners, -1)
-    student_every = every[:, 3 * live_rows :]
-    student_tops = student_every[:, :chunk]
-    highest = jnp.max(student_tops, axis=0)
-    totals = jnp.sum(
-        student_every[:, chunk : 2 * chunk] * jnp.exp(student_tops - highest[None, :]), axis=0
-    )
-    log_chunk = highest + jnp.log(totals)
-    student_loss = jnp.sum(log_chunk) - BLEND * jnp.sum(
-        student_every[:, 2 * chunk : 3 * chunk]
-    )
-    tops = every[:, :live_rows]
-    highest = jnp.max(tops, axis=0)
-    scales = jnp.exp(tops - highest[None, :])
-    totals = jnp.sum(every[:, live_rows : 2 * live_rows] * scales, axis=0)
-    crosses = jnp.sum(every[:, 2 * live_rows : 3 * live_rows] * scales, axis=0)
-    factor = jnp.exp(top - highest) / totals
-    loss = student_loss - (1.0 - BLEND) / members * jnp.sum(crosses / totals)
-    factors = spread(
-        jnp.concatenate([factor, log_chunk, jnp.full((128 - chunk,), loss)]).reshape(-1, 128), "member", members
-    )
-    mean_loss = jnp.sum(factors[:, -1, chunk]) / jnp.sum(counts).astype(F32)
-    log_total = factors[:, -1, :chunk].reshape(live_rows)
-    factors = factors[:, :-1].reshape(members, live_rows)
+    every, *arrived = lax.optimization_barrier((every, *arrived))
+    sent = combine(every, top, members)
+    factors = lax.all_to_all(sent, "member", 0, 0, tiled=True).reshape(members, -1)
+    log_total = factors[:, live_rows : live_rows + chunk].reshape(live_rows)
+    factors = factors[:, :live_rows]
     ranks = jnp.arange(members, dtype=jnp.int32)[:, None]
-    probs = 0.0
+    probs = []
     for step in range(members):
         source = (member - step) % members
         scale = jnp.sum(jnp.where(ranks == source, factors, 0.0), axis=0)
-        probs = probs + arrived[step].astype(F32) * scale[:, None]
-    student_slope = jnp.exp(student_logits - log_total[:, None]) - BLEND * hit.astype(F32)
-    slope = (LOSS_SCALE * (student_slope - (1.0 - BLEND) / members * probs)).astype(BF16)
-
-    half = width // 2
+        probs.append(arrived[step][:live_rows].astype(F32) * scale[:, None])
+    mean_probs = ((probs[0] + probs[2]) + (probs[1] + probs[3])) / members
+    chunks = []
+    for index in range(members):
+        parts = arrived[0][live_rows:]
+        for step in range(1, members):
+            parts = jnp.where((member - step) % members == index, arrived[step][live_rows:], parts)
+        parts = parts.astype(F32).reshape(3, chunk, vocab)
+        chunks.append((parts[0] + parts[1]) + parts[2])
+    student_logits = jnp.concatenate(chunks, axis=0)
+    mixture = BLEND * hit.astype(F32) + (1.0 - BLEND) * mean_probs
+    loss = jnp.where(owner == 0, jnp.sum(log_total), 0.0) - jnp.sum(mixture * student_logits)
+    slope = (LOSS_SCALE * (jnp.exp(student_logits - log_total[:, None]) - mixture)).astype(BF16)
 
     def term(which_core):
-        chosen = jnp.take(places.reshape(chips, cores, cap), which_core, axis=1)
-        result = 0.0
-        for side in range(2):
-            at = jnp.where(sides[None, :, None] == side, chosen[:, None, :], -1).reshape(-1, 1)
-            unpack = (at == packed_ids[None, :]).astype(BF16)
-            rows = jnp.dot(unpack, slope, preferred_element_type=F32).astype(BF16)
-            result = result + lax.dot_general(
-                rows,
-                student_head[side * half : (side + 1) * half],
-                (((1,), (1,)), ((), ())),
-                preferred_element_type=F32,
-            )
-        return result
+        chosen = jnp.take(places.reshape(chips, cores, cap), which_core, axis=1).reshape(-1, 1)
+        unpack = (chosen == packed_ids[None, :]).astype(BF16)
+        rows = jnp.dot(unpack, slope, preferred_element_type=F32).astype(BF16)
+        return lax.dot_general(
+            rows, student_head, (((1,), (1,)), ((), ())), preferred_element_type=F32
+        )
 
     arrived = lax.ppermute(term(1 - core), "core", swap)
-    grads = (term(core) + arrived).astype(BF16).reshape(chips, 2 * cap, half)
-    owned = jnp.sum(lax.all_to_all(grads, CHIPS, 0, 0, tiled=True).astype(F32), axis=0)
-    slot_grad = jnp.concatenate([owned[:cap], owned[cap:]], axis=1)
+    other_loss = lax.ppermute(jnp.full((8, 128), loss, F32), "core", swap)
+    grads = (term(core) + arrived).reshape(chips, cap, width)
+    chip_loss = jnp.broadcast_to(loss + other_loss[0, 0], (chips, cap, 128))
+    owned = jnp.sum(
+        lax.all_to_all(jnp.concatenate([grads, chip_loss], axis=2), CHIPS, 0, 0, tiled=True),
+        axis=0,
+    )
+    slot_grad = owned[:, :width]
+    mean_loss = owned[0, width] / jnp.sum(counts).astype(F32)
     live_here = slots < lax.dynamic_index_in_dim(counts, owner, keepdims=False)
     placed = (
         (jnp.arange(window, dtype=jnp.int32)[:, None] == slot_ids[None, :]) & live_here[None, :]

time: 178 us -> 197 us (1.11); the launches traced: 177 us -> 194 us
  blocking collectives: 24.2 us -> 37.3 us
  starting transfers between devices: 48.1 us -> 53.1 us
  matrix products: 10.8 us -> 8.22 us
  Pallas kernels: 8.19 us -> 10.2 us
    all_to_all x4 -> x2, waiting for transfers between devices: 31.5 us -> 12.7 us  [spread(): lax.all_to_all(jnp.broadcast_to(block[None], (size,) + block.shape), axes...]
    ppermute x3 -> x4, waiting for transfers between devices: 0.01 us -> 17.2 us  [the longest x3 16.1 us: on_device(): lax.ppermute(shared, 'member', [(i, (i + step) % members) for i in range(...]
    all_to_all x0 -> x1, blocking collectives: none -> 13.1 us  [on_device(): lax.all_to_all(partial_logits.reshape(members, chunk, vocab), 'member', 0...]
    all_to_all x2, starting transfers between devices: 8.68 us -> 17.4 us  [the longest x1 12.8 us: on_device(): lax.all_to_all(jnp.concatenate([grads, chip_loss], axis=2), CHIPS, 0, 0,...]
    all_to_all x4 -> x2, starting transfers between devices: 20.4 us -> 13.7 us  [spread(): lax.all_to_all(jnp.broadcast_to(block[None], (size,) + block.shape), axes...]
    ppermute x3 -> x4, starting transfers between devices: 8.41 us -> 12.4 us  [the longest x3 10.5 us: on_device(): lax.ppermute(shared, 'member', [(i, (i + step) % members) for i in range(...]
    all_to_all x2, waiting for transfers between devices: 18.4 us -> 20.6 us  [the longest x1 16.7 us: on_device(): lax.all_to_all(jnp.concatenate([grads, chip_loss], axis=2), CHIPS, 0, 0,...]
    pallas_call x0 -> x1, Pallas kernels: none -> 2.04 us  [combine(): pl.pallas_call(combine_kernel, out_shape=jax.ShapeDtypeStruct((copies, 1,...]
  transfers between devices with their start and end apart: 13 -> 12, of which waited for: 7 -> 7; matrix products, arithmetic and copies ran while one was open for 12% -> 7% of each run, Pallas kernels for 1% -> 1%
where the time goes in v5:
time: 197 us; the launch traced here: 194 us
  starting transfers between devices  53.1 us (27%)
  waiting for transfers between devices  50.4 us (26%)
  blocking collectives  37.3 us (19%)
  between operations  19 us (10%)
  Pallas kernels  10.2 us (5%)
  matrix products  8.22 us (4%)
  local copies, waits for them, and re-layouts  7.73 us (4%)
  other arithmetic  7.61 us (4%)
    all_to_all x1, blocking collectives, on_device(): group_rows = lax.all_to_all(sent, ('z', 'core'), 0, 0, tiled=True)  24.2 us
    all_to_all x1, waiting for transfers between devices, on_device(): lax.all_to_all(jnp.concatenate([grads, chip_loss], axis=2), CHIPS, 0, 0,...  16.7 us
    ppermute x3, waiting for transfers between devices, on_device(): lax.ppermute(shared, 'member', [(i, (i + step) % members) for i in range(...  16.1 us
    all_to_all x2, starting transfers between devices, spread(): lax.all_to_all(jnp.broadcast_to(block[None], (size,) + block.shape), axes...  13.7 us
    all_to_all x1, blocking collectives, on_device(): lax.all_to_all(partial_logits.reshape(members, chunk, vocab), 'member', 0...  13.1 us
    all_to_all x1, starting transfers between devices, on_device(): lax.all_to_all(jnp.concatenate([grads, chip_loss], axis=2), CHIPS, 0, 0,...  12.8 us
    all_to_all x2, waiting for transfers between devices, spread(): lax.all_to_all(jnp.broadcast_to(block[None], (size,) + block.shape), axes...  12.7 us
    ppermute x3, starting transfers between devices, on_device(): lax.ppermute(shared, 'member', [(i, (i + step) % members) for i in range(...  10.5 us
  transfers between devices with their start and end apart: 12, of which 7 were waited for; matrix products, arithmetic and copies ran while one was open for 7% of the time, Pallas kernels for 1%

profile of v5, /device:TPU:1, one launch (start us, length us, event | category | flops | bytes accessed | tf_op | source)
XLA Modules:
  0.0 193.7 jit_solution(1777538732030748400)
XLA Ops:
  7.2 2.0 %own_rows.1 = bf16[128,1152]{1,0:T(8,128)(2,1)} custom-call(s32[1,4]{1,0:T(1,128)} %refs_0_.1, bf16[1,16,4096]{2,1,0:T(8,128)(2,1)} %refs_1_.1, f32[1,4096]{1,0:T(1,128)} %refs_2_.1, bf16[16,512]{1,0:T(8,128)(2,1)} %refs_3_.1), custom_call_target="tpu_custom_call" | custom-call | tf_op jit(solution)/shard_map/own_rows/pallas_call | solution.py:57
  9.2 24.2 %all_to_all.30 = bf16[16,8,1152]{2,1,0:T(8,128)(2,1)S(1)} all-to-all(bf16[16,8,1152]{2,1,0:T(8,128)(2,1)} %bitcast.63), channel_id=1, replica_groups=mesh['member'=4,'y'=8,'z'=8,'core'=2] {'z','core'}, dimensions={0} | all-to-all | bytes 589824 | tf_op jit(solution)/shard_map/all_to_all | solution.py:186
  33.4 0.7 slice.174
  34.2 0.8 select_reduce_fusion.1
  34.9 0.8 broadcast_in_dim.152
  35.7 6.8 %all-to-all-start.1 = ((bf16[8,128,128]{2,1,0:T(8,128)(2,1)}), bf16[8,128,128]{2,1,0:T(8,128)(2,1)S(1)}, u32[]{:S(2)}, u32[]{:S(2)}) async-start(bf16[8,128,128]{2,1,0:T(8,128)(2,1)} %broadcast_in_dim.152), calls=%async_computation.1 | async-start | bytes 524288 | tf_op jit(solution)/shard_map/all_to_all | solution.py:19
  42.5 0.8 add_select_fusion
  43.8 0.6 pad_add_fusion.places_ref
  44.5 12.7 %all-to-all-done.1 = bf16[8,128,128]{2,1,0:T(8,128)(2,1)S(1)} async-done(((bf16[8,128,128]{2,1,0:T(8,128)(2,1)}), bf16[8,128,128]{2,1,0:T(8,128)(2,1)S(1)}, u32[]{:S(2)}, u32[]{:S(2)}) %all-to-all-start.1) | async-done | bytes 262176 | tf_op jit(solution)/shard_map/all_to_all | solution.py:19
  57.1 0.7 copy-done.3
  57.8 2.4 %pack_student.1 = (bf16[2,256,128]{2,1,0:T(8,128)(2,1)}, bf16[2,256,1024]{2,1,0:T(8,128)(2,1)}) custom-call(s32[2,1024]{1,0:T(2,128)} %pad_add_fusion.places_ref, bf16[1024,128]{1,0:T(8,128)(2,1)} %bitcast.64), custom_call_target="tpu_custom_call" | custom-call | tf_op jit(solution)/shard_map/pack_student/pallas_call | solution.py:79
  60.2 2.4 %collective-permute-start = (bf16[2,256,128]{2,1,0:T(8,128)(2,1)}, bf16[2,256,128]{2,1,0:T(8,128)(2,1)S(1)}, u32[]{:S(2)}, u32[]{:S(2)}) collective-permute-start(bf16[2,256,128]{2,1,0:T(8,128)(2,1)} %get-tuple-element.14), channel_id=1, source_target_pairs={{0,1},{1,0},{2,3},{3,2},{4,5},{5,4},{6,7},{7,6},{8,9},{9,8},{10,11... | collective-permute-start | bytes 393224 | tf_op jit(solution)/shard_map/ppermute | solution.py:224
  62.6 1.0 fusion.22
  63.7 1.1 convolution_add_fusion.3
  65.2 13.1 %all_to_all.31 = f32[4,64,512]{2,1,0:T(8,128)S(1)} all-to-all(f32[4,64,512]{2,1,0:T(8,128)S(1)} %bitcast.60), channel_id=1, replica_groups=mesh['member'=4,'y'=8,'z'=8,'core'=2] {'member'}, dimensions={0} | all-to-all | bytes 1048576 | tf_op jit(solution)/shard_map/all_to_all | solution.py:226
  78.7 3.8 %pack_teacher.1 = bf16[2,256,1024]{2,1,0:T(8,128)(2,1)} custom-call(bf16[2,256,1024]{2,1,0:T(8,128)(2,1)} %get-tuple-element.13.one_ref, bf16[1024,1024]{1,0:T(8,128)(2,1)} %all-gather.2.cloned.1.call-done.rows_ref), custom_call_target="tpu_custom_call" | custom-call | tf_op jit(solution)/shard_map/pack_teacher/pallas_call | solution.py:100
  82.5 3.1 %collective-permute-start.1 = (bf16[2,256,1024]{2,1,0:T(8,128)(2,1)}, bf16[2,256,1024]{2,1,0:T(8,128)(2,1)S(1)}, u32[]{:S(2)}, u32[]{:S(2)}) collective-permute-start(bf16[2,256,1024]{2,1,0:T(8,128)(2,1)} %pack_teacher.1), channel_id=1, source_target_pairs={{0,1},{1,0},{2,3},{3,2},{4,5},{5,4},{6,7},{7,6},{8,9},{9,8},{10,11... | collective-permute-start | bytes 3145736 | tf_op jit(solution)/shard_map/ppermute | solution.py:238
  86.4 2.0 %fusion.7 = f32[256,512]{1,0:T(8,128)S(1)} fusion(bf16[1,4096,512]{2,1,0:T(8,128)(2,1)} %param.12, s32[]{:T(128)S(6)} %select_n.234, bf16[2,256,1024]{2,1,0:T(8,128)(2,1)} %pack_teacher.1), kind=kOutput, calls=%fused_computation.14 | convolution fusion | flops 268435456 | bytes 2097156 | tf_op jit(solution)/shard_map/dot_general | solution.py:214
  88.3 1.8 convolution_add_fusion.1
  90.7 0.5 fusion.40
  91.5 0.9 broadcast_in_dim.153
  92.4 6.8 %all-to-all-start.3 = ((f32[128,1,640]{2,1,0:T(1,128)}), f32[128,1,640]{2,1,0:T(1,128)S(1)}, u32[]{:S(2)}, u32[]{:S(2)}) async-start(f32[128,1,640]{2,1,0:T(1,128)} %broadcast_in_dim.153), calls=%async_computation.3 | async-start | bytes 655360 | tf_op jit(solution)/shard_map/all_to_all | solution.py:19
  99.4 3.1 %collective-permute-start.2 = (bf16[448,512]{1,0:T(8,128)(2,1)S(1)}, bf16[448,512]{1,0:T(8,128)(2,1)S(1)}, u32[]{:S(2)}, u32[]{:S(2)}) collective-permute-start(bf16[448,512]{1,0:T(8,128)(2,1)S(1)} %pad_maximum_fusion.1), channel_id=1, source_target_pairs={{0,128},{128,256},{256,384},{384,0},{1,129},{129,257},{257,385},{3... | collective-permute-start | bytes 1376264 | tf_op jit(solution)/shard_map/ppermute | solution.py:245
  102.5 4.3 %collective-permute-start.3 = (bf16[448,512]{1,0:T(8,128)(2,1)S(1)}, bf16[448,512]{1,0:T(8,128)(2,1)S(1)}, u32[]{:S(2)}, u32[]{:S(2)}) collective-permute-start(bf16[448,512]{1,0:T(8,128)(2,1)S(1)} %pad_maximum_fusion.1), channel_id=1, source_target_pairs={{0,256},{128,384},{256,0},{384,128},{1,257},{129,385},{257,1},{385... | collective-permute-start | bytes 1376264 | tf_op jit(solution)/shard_map/ppermute | solution.py:245
  106.8 3.1 %collective-permute-start.4 = (bf16[448,512]{1,0:T(8,128)(2,1)S(1)}, bf16[448,512]{1,0:T(8,128)(2,1)S(1)}, u32[]{:S(2)}, u32[]{:S(2)}) collective-permute-start(bf16[448,512]{1,0:T(8,128)(2,1)S(1)} %pad_maximum_fusion.1), channel_id=1, source_target_pairs={{0,384},{128,0},{256,128},{384,256},{1,385},{129,1},{257,129},{385... | collective-permute-start | bytes 1376264 | tf_op jit(solution)/shard_map/ppermute | solution.py:245
  110.1 3.5 %collective-permute-done.2 = bf16[448,512]{1,0:T(8,128)(2,1)S(1)} collective-permute-done((bf16[448,512]{1,0:T(8,128)(2,1)S(1)}, bf16[448,512]{1,0:T(8,128)(2,1)S(1)}, u32[]{:S(2)}, u32[]{:S(2)}) %collective-permute-start.2) | collective-permute-done | bytes 458784 | tf_op jit(solution)/shard_map/ppermute | solution.py:245
  113.7 10.7 %collective-permute-done.3 = bf16[448,512]{1,0:T(8,128)(2,1)S(1)} collective-permute-done((bf16[448,512]{1,0:T(8,128)(2,1)S(1)}, bf16[448,512]{1,0:T(8,128)(2,1)S(1)}, u32[]{:S(2)}, u32[]{:S(2)}) %collective-permute-start.3) | collective-permute-done | bytes 458784 | tf_op jit(solution)/shard_map/ppermute | solution.py:245
  124.4 1.9 collective-permute-done.4
  126.3 0.7 copy-done.2
  127.0 2.0 %combine.1 = f32[4,1,384]{2,1,0:T(1,128)} custom-call(f32[128,1,640]{2,1,0:T(1,128)} %copy-done.2, f32[1,256]{1,0:T(1,128)} %bitcast.67), custom_call_target="tpu_custom_call" | custom-call | tf_op jit(solution)/shard_map/combine/pallas_call | solution.py:135
  129.0 4.7 %all-to-all-start.4 = ((f32[4,1,384]{2,1,0:T(1,128)}), f32[4,1,384]{2,1,0:T(1,128)S(1)}, u32[]{:S(2)}, u32[]{:S(2)}) async-start(f32[4,1,384]{2,1,0:T(1,128)} %combine.1), calls=%async_computation.4 | async-start | bytes 12288 | tf_op jit(solution)/shard_map/all_to_all | solution.py:250
  134.0 3.8 %all-to-all-done.4 = f32[4,1,384]{2,1,0:T(1,128)S(1)} async-done(((f32[4,1,384]{2,1,0:T(1,128)}), f32[4,1,384]{2,1,0:T(1,128)S(1)}, u32[]{:S(2)}, u32[]{:S(2)}) %all-to-all-start.4) | async-done | bytes 6176 | tf_op jit(solution)/shard_map/all_to_all | solution.py:250
  137.9 0.6 slice_reduce_fusion
  138.6 1.0 multiply_reduce_fusion
  139.9 0.5 fusion.2
  140.3 4.2 %collective-permute-start.5 = (f32[256,512]{1,0:T(8,128)S(1)}, f32[256,512]{1,0:T(8,128)S(1)}, u32[]{:S(2)}, u32[]{:S(2)}) collective-permute-start(f32[256,512]{1,0:T(8,128)S(1)} %fusion.2), channel_id=1, source_target_pairs={{0,1},{1,0},{2,3},{3,2},{4,5},{5,4},{6,7},{7,6},{8,9},{9,8},{10,11... | collective-permute-start | bytes 1572872 | tf_op jit(solution)/shard_map/ppermute | solution.py:280
  145.8 1.9 collective-permute-start.6
  147.9 1.0 collective-permute-done.6
  148.9 0.5 slice.161
  150.1 0.5 convolution_add_fusion.4
  150.7 0.9 concatenate.15
  151.6 12.8 %all-to-all-start.5 = ((f32[64,4,640]{2,1,0:T(4,128)}), f32[64,4,640]{2,1,0:T(4,128)S(1)}, u32[]{:S(2)}, u32[]{:S(2)}) async-start(f32[64,4,640]{2,1,0:T(4,128)} %concatenate.15), calls=%async_computation.5 | async-start | bytes 1310720 | tf_op jit(solution)/shard_map/all_to_all | solution.py:285
  164.4 0.6 reduce_sum.138
  165.0 0.6 dynamic_slice.48
  166.3 0.7 iota_compare_fusion.11
  167.0 16.7 %all-to-all-done.5 = f32[64,4,640]{2,1,0:T(4,128)S(1)} async-done(((f32[64,4,640]{2,1,0:T(4,128)}), f32[64,4,640]{2,1,0:T(4,128)S(1)}, u32[]{:S(2)}, u32[]{:S(2)}) %all-to-all-start.5) | async-done | bytes 655392 | tf_op jit(solution)/shard_map/all_to_all | solution.py:285
  183.9 0.5 slice.195
  184.4 0.7 multiply_reduce_fusion.1
  (63 shorter events, 4.2 us)
Async XLA Ops:
  7.2 55.4 %copy-start = (bf16[512,512]{1,0:T(8,128)(2,1)S(1)}, bf16[512,512]{1,0:T(8,128)(2,1)}, u32[]{:S(2)}) copy-start(bf16[512,512]{1,0:T(8,128)(2,1)} %param.14) | copy-start | bytes 1572868
  7.2 71.5 %all-gather.2.cloned.1.call-start = ((), (), s32[]{:S(2)}) async-start(), calls=%async_computation.6 | async-start | bytes 2359296 | tf_op jit(solution)/shard_map/all_gather | solution.py:188
  35.7 21.5 %all-to-all-start.1 = ((bf16[8,128,128]{2,1,0:T(8,128)(2,1)}), bf16[8,128,128]{2,1,0:T(8,128)(2,1)S(1)}, u32[]{:S(2)}, u32[]{:S(2)}) async-start(bf16[8,128,128]{2,1,0:T(8,128)(2,1)} %broadcast_in_dim.152), calls=%async_computation.1 | async-start | bytes 524288 | tf_op jit(solution)/shard_map/all_to_all | solution.py:19
  57.1 0.7 copy-start.3
  60.2 4.5 %collective-permute-start = (bf16[2,256,128]{2,1,0:T(8,128)(2,1)}, bf16[2,256,128]{2,1,0:T(8,128)(2,1)S(1)}, u32[]{:S(2)}, u32[]{:S(2)}) collective-permute-start(bf16[2,256,128]{2,1,0:T(8,128)(2,1)} %get-tuple-element.14), channel_id=1, source_target_pairs={{0,1},{1,0},{2,3},{3,2},{4,5},{5,4},{6,7},{7,6},{8,9},{9,8},{10,11... | collective-permute-start | bytes 393224 | tf_op jit(solution)/shard_map/ppermute | solution.py:224
  65.0 21.0 %copy-start.5 = (s32[128]{0:T(128)S(1)}, s32[128]{0:T(128)}, u32[]{:S(2)}) copy-start(s32[128]{0:T(128)} %param.16) | copy-start | bytes 1540
  82.5 7.7 %collective-permute-start.1 = (bf16[2,256,1024]{2,1,0:T(8,128)(2,1)}, bf16[2,256,1024]{2,1,0:T(8,128)(2,1)S(1)}, u32[]{:S(2)}, u32[]{:S(2)}) collective-permute-start(bf16[2,256,1024]{2,1,0:T(8,128)(2,1)} %pack_teacher.1), channel_id=1, source_target_pairs={{0,1},{1,0},{2,3},{3,2},{4,5},{5,4},{6,7},{7,6},{8,9},{9,8},{10,11... | collective-permute-start | bytes 3145736 | tf_op jit(solution)/shard_map/ppermute | solution.py:238
  86.2 4.0 %copy-start.1 = (bf16[1,4096,512]{2,1,0:T(8,128)(2,1)S(1)}, bf16[1,4096,512]{2,1,0:T(8,128)(2,1)}, u32[]{:S(2)}) copy-start(bf16[1,4096,512]{2,1,0:T(8,128)(2,1)} %param.12) | copy-start | bytes 12582916
  90.2 19.8 %copy-start.6 = (s32[512]{0:T(512)S(1)}, s32[512]{0:T(512)}, u32[]{:S(2)}) copy-start(s32[512]{0:T(512)} %param.17) | copy-start | bytes 6148
  91.2 35.1 %copy-start.4 = (f32[256]{0:T(256)}, f32[256]{0:T(256)S(1)}, u32[]{:S(2)}) copy-start(f32[256]{0:T(256)S(1)} %get-tuple-element.56) | copy-start | bytes 3076
  92.4 33.9 %all-to-all-start.3 = ((f32[128,1,640]{2,1,0:T(1,128)}), f32[128,1,640]{2,1,0:T(1,128)S(1)}, u32[]{:S(2)}, u32[]{:S(2)}) async-start(f32[128,1,640]{2,1,0:T(1,128)} %broadcast_in_dim.153), calls=%async_computation.3 | async-start | bytes 655360 | tf_op jit(solution)/shard_map/all_to_all | solution.py:19
  99.4 14.2 %collective-permute-start.2 = (bf16[448,512]{1,0:T(8,128)(2,1)S(1)}, bf16[448,512]{1,0:T(8,128)(2,1)S(1)}, u32[]{:S(2)}, u32[]{:S(2)}) collective-permute-start(bf16[448,512]{1,0:T(8,128)(2,1)S(1)} %pad_maximum_fusion.1), channel_id=1, source_target_pairs={{0,128},{128,256},{256,384},{384,0},{1,129},{129,257},{257,385},{3... | collective-permute-start | bytes 1376264 | tf_op jit(solution)/shard_map/ppermute | solution.py:245
  102.5 21.9 %collective-permute-start.3 = (bf16[448,512]{1,0:T(8,128)(2,1)S(1)}, bf16[448,512]{1,0:T(8,128)(2,1)S(1)}, u32[]{:S(2)}, u32[]{:S(2)}) collective-permute-start(bf16[448,512]{1,0:T(8,128)(2,1)S(1)} %pad_maximum_fusion.1), channel_id=1, source_target_pairs={{0,256},{128,384},{256,0},{384,128},{1,257},{129,385},{257,1},{385... | collective-permute-start | bytes 1376264 | tf_op jit(solution)/shard_map/ppermute | solution.py:245
  106.8 19.4 %collective-permute-start.4 = (bf16[448,512]{1,0:T(8,128)(2,1)S(1)}, bf16[448,512]{1,0:T(8,128)(2,1)S(1)}, u32[]{:S(2)}, u32[]{:S(2)}) collective-permute-start(bf16[448,512]{1,0:T(8,128)(2,1)S(1)} %pad_maximum_fusion.1), channel_id=1, source_target_pairs={{0,384},{128,0},{256,128},{384,256},{1,385},{129,1},{257,129},{385... | collective-permute-start | bytes 1376264 | tf_op jit(solution)/shard_map/ppermute | solution.py:245
  126.3 0.7 copy-start.2
  129.0 8.8 %all-to-all-start.4 = ((f32[4,1,384]{2,1,0:T(1,128)}), f32[4,1,384]{2,1,0:T(1,128)S(1)}, u32[]{:S(2)}, u32[]{:S(2)}) async-start(f32[4,1,384]{2,1,0:T(1,128)} %combine.1), calls=%async_computation.4 | async-start | bytes 12288 | tf_op jit(solution)/shard_map/all_to_all | solution.py:250
  139.7 27.2 %copy-start.7 = (s32[1,4]{1,0:T(1,128)S(1)}, s32[1,4]{1,0:T(1,128)}, u32[]{:S(2)}) copy-start(s32[1,4]{1,0:T(1,128)} %refs_0_.1) | copy-start | bytes 52
  140.3 9.7 %collective-permute-start.5 = (f32[256,512]{1,0:T(8,128)S(1)}, f32[256,512]{1,0:T(8,128)S(1)}, u32[]{:S(2)}, u32[]{:S(2)}) collective-permute-start(f32[256,512]{1,0:T(8,128)S(1)} %fusion.2), channel_id=1, source_target_pairs={{0,1},{1,0},{2,3},{3,2},{4,5},{5,4},{6,7},{7,6},{8,9},{9,8},{10,11... | collective-permute-start | bytes 1572872 | tf_op jit(solution)/shard_map/ppermute | solution.py:280
  145.8 3.1 %collective-permute-start.6 = (f32[8,128]{1,0:T(8,128)S(1)}, f32[8,128]{1,0:T(8,128)S(1)}, u32[]{:S(2)}, u32[]{:S(2)}) collective-permute-start(f32[8,128]{1,0:T(8,128)S(1)} %broadcast_in_dim.162), channel_id=1, source_target_pairs={{0,1},{1,0},{2,3},{3,2},{4,5},{5,4},{6,7},{7,6},{8,9},{9,8},{10,11... | collective-permute-start | bytes 12296 | tf_op jit(solution)/shard_map/ppermute | solution.py:281
  151.6 32.1 %all-to-all-start.5 = ((f32[64,4,640]{2,1,0:T(4,128)}), f32[64,4,640]{2,1,0:T(4,128)S(1)}, u32[]{:S(2)}, u32[]{:S(2)}) async-start(f32[64,4,640]{2,1,0:T(4,128)} %concatenate.15), calls=%async_computation.5 | async-start | bytes 1310720 | tf_op jit(solution)/shard_map/all_to_all | solution.py:285
Sparse Core Ops, SparseCore 0:
  34.3 40.4 all-gather.1

commit v6 on v5

--- a/solution.py
+++ b/solution.py
@@ -245,9 +245,10 @@
         lax.ppermute(shared, "member", [(i, (i + step) % members) for i in range(members)])
         for step in range(1, members)
     ]
-    every, *arrived = lax.optimization_barrier((every, *arrived))
     sent = combine(every, top, members)
-    factors = lax.all_to_all(sent, "member", 0, 0, tiled=True).reshape(members, -1)
+    factors = lax.all_to_all(sent, "member", 0, 0, tiled=True)
+    factors, *arrived = lax.optimization_barrier((factors, *arrived))
+    factors = factors.reshape(members, -1)
     log_total = factors[:, live_rows : live_rows + chunk].reshape(live_rows)
     factors = factors[:, :live_rows]
     ranks = jnp.arange(members, dtype=jnp.int32)[:, None]
@@ -270,23 +271,22 @@
     slope = (LOSS_SCALE * (jnp.exp(student_logits - log_total[:, None]) - mixture)).astype(BF16)
 
     def term(which_core):
-        chosen = jnp.take(places.reshape(chips, cores, cap), which_core, axis=1).reshape(-1, 1)
-        unpack = (chosen == packed_ids[None, :]).astype(BF16)
-        rows = jnp.dot(unpack, slope, preferred_element_type=F32).astype(BF16)
-        return lax.dot_general(
-            rows, student_head, (((1,), (1,)), ((), ())), preferred_element_type=F32
-        )
-
-    arrived = lax.ppermute(term(1 - core), "core", swap)
-    other_loss = lax.ppermute(jnp.full((8, 128), loss, F32), "core", swap)
-    grads = (term(core) + arrived).reshape(chips, cap, width)
-    chip_loss = jnp.broadcast_to(loss + other_loss[0, 0], (chips, cap, 128))
-    owned = jnp.sum(
-        lax.all_to_all(jnp.concatenate([grads, chip_loss], axis=2), CHIPS, 0, 0, tiled=True),
-        axis=0,
-    )
-    slot_grad = owned[:, :width]
-    mean_loss = owned[0, width] / jnp.sum(counts).astype(F32)
+        chosen = jnp.take(places.reshape(chips, cores, cap), which_core, axis=1)
+        parts = []
+        for slot in range(cap):
+            unpack = (chosen[:, slot : slot + 1] == packed_ids[None, :]).astype(BF16)
+            rows = jnp.dot(unpack, slope, preferred_element_type=F32).astype(BF16)
+            parts.append(
+                lax.dot_general(
+                    rows, student_head, (((1,), (1,)), ((), ())), preferred_element_type=F32
+                )
+            )
+        return jnp.concatenate(parts + [jnp.full((chips, 128), loss, F32)], axis=1)
+
+    grads = term(core) + lax.ppermute(term(1 - core), "core", swap)
+    owned = jnp.sum(lax.all_to_all(grads[:, None, :], CHIPS, 0, 0, tiled=True), axis=0)
+    slot_grad = owned[0, : cap * width].reshape(cap, width)
+    mean_loss = owned[0, cap * width] / jnp.sum(counts).astype(F32)
     live_here = slots < lax.dynamic_index_in_dim(counts, owner, keepdims=False)
     placed = (
         (jnp.arange(window, dtype=jnp.int32)[:, None] == slot_ids[None, :]) & live_here[None, :]

time: 197 us -> 182 us (0.924)
  the two profiles are of different devices: /device:TPU:1 before, /device:TPU:18 now
where the time goes in v6:
time: 182 us; the launch traced here: 181 us
  starting transfers between devices  50.6 us (28%)
  waiting for transfers between devices  41 us (23%)
  blocking collectives  35.5 us (20%)
  between operations  18.4 us (10%)
  matrix products  10.5 us (6%)
  Pallas kernels  10.2 us (6%)
  other arithmetic  7.76 us (4%)
  local copies, waits for them, and re-layouts  7.35 us (4%)
    all_to_all x1, blocking collectives, on_device(): group_rows = lax.all_to_all(sent, ('z', 'core'), 0, 0, tiled=True)  22.2 us
    all_to_all x1, waiting for transfers between devices, on_device(): lax.all_to_all(grads[:, None, :], CHIPS, 0, 0, tiled=True)  17.8 us
    all_to_all x2, starting transfers between devices, spread(): lax.all_to_all(jnp.broadcast_to(block[None], (size,) + block.shape), axes...  16.7 us
    all_to_all x2, waiting for transfers between devices, spread(): lax.all_to_all(jnp.broadcast_to(block[None], (size,) + block.shape), axes...  13.8 us
    all_to_all x1, blocking collectives, on_device(): lax.all_to_all(partial_logits.reshape(members, chunk, vocab), 'member', 0...  13.3 us
    all_to_all x1, starting transfers between devices, on_device(): lax.all_to_all(grads[:, None, :], CHIPS, 0, 0, tiled=True)  12.8 us
    ppermute x3, starting transfers between devices, on_device(): lax.ppermute(shared, 'member', [(i, (i + step) % members) for i in range(...  10.4 us
    dot_general x8, matrix products, both_halves(): jnp.dot(values[side], lax.dynamic_slice_in_dim(weights, first + side * pa...  7.32 us
  transfers between devices with their start and end apart: 11, of which 7 were waited for; matrix products, arithmetic and copies ran while one was open for 8% of the time, Pallas kernels for 2%

profile of v6, /device:TPU:18, one launch (start us, length us, event | category | flops | bytes accessed | tf_op | source)
XLA Modules:
  0.0 181.2 jit_solution(8703526971722194654)
XLA Ops:
  7.2 2.0 %own_rows.1 = bf16[128,1152]{1,0:T(8,128)(2,1)} custom-call(s32[1,4]{1,0:T(1,128)} %refs_0_.1, bf16[1,16,4096]{2,1,0:T(8,128)(2,1)} %refs_1_.1, f32[1,4096]{1,0:T(1,128)} %refs_2_.1, bf16[16,512]{1,0:T(8,128)(2,1)} %refs_3_.1), custom_call_target="tpu_custom_call" | custom-call | tf_op jit(solution)/shard_map/own_rows/pallas_call | solution.py:57
  9.2 22.2 %all_to_all.30 = bf16[16,8,1152]{2,1,0:T(8,128)(2,1)S(1)} all-to-all(bf16[16,8,1152]{2,1,0:T(8,128)(2,1)} %bitcast.92), channel_id=1, replica_groups=mesh['member'=4,'y'=8,'z'=8,'core'=2] {'z','core'}, dimensions={0} | all-to-all | bytes 589824 | tf_op jit(solution)/shard_map/all_to_all | solution.py:186
  31.4 0.7 slice.202
  32.2 0.8 select_reduce_fusion.1
  32.9 0.8 broadcast_in_dim.160
  33.7 7.4 %all-to-all-start.1 = ((bf16[8,128,128]{2,1,0:T(8,128)(2,1)}), bf16[8,128,128]{2,1,0:T(8,128)(2,1)S(1)}, u32[]{:S(2)}, u32[]{:S(2)}) async-start(bf16[8,128,128]{2,1,0:T(8,128)(2,1)} %broadcast_in_dim.160), calls=%async_computation.1 | async-start | bytes 524288 | tf_op jit(solution)/shard_map/all_to_all | solution.py:19
  41.1 0.8 add_select_fusion
  42.5 0.6 pad_add_fusion.places_ref
  43.1 10.0 %all-to-all-done.1 = bf16[8,128,128]{2,1,0:T(8,128)(2,1)S(1)} async-done(((bf16[8,128,128]{2,1,0:T(8,128)(2,1)}), bf16[8,128,128]{2,1,0:T(8,128)(2,1)S(1)}, u32[]{:S(2)}, u32[]{:S(2)}) %all-to-all-start.1) | async-done | bytes 262176 | tf_op jit(solution)/shard_map/all_to_all | solution.py:19
  53.1 0.7 copy-done.3
  53.8 2.4 %pack_student.1 = (bf16[2,256,128]{2,1,0:T(8,128)(2,1)}, bf16[2,256,1024]{2,1,0:T(8,128)(2,1)}) custom-call(s32[2,1024]{1,0:T(2,128)} %pad_add_fusion.places_ref, bf16[1024,128]{1,0:T(8,128)(2,1)} %bitcast.93), custom_call_target="tpu_custom_call" | custom-call | tf_op jit(solution)/shard_map/pack_student/pallas_call | solution.py:79
  56.2 1.9 %collective-permute-start = (bf16[2,256,128]{2,1,0:T(8,128)(2,1)}, bf16[2,256,128]{2,1,0:T(8,128)(2,1)S(1)}, u32[]{:S(2)}, u32[]{:S(2)}) collective-permute-start(bf16[2,256,128]{2,1,0:T(8,128)(2,1)} %get-tuple-element.14), channel_id=1, source_target_pairs={{0,1},{1,0},{2,3},{3,2},{4,5},{5,4},{6,7},{7,6},{8,9},{9,8},{10,11... | collective-permute-start | bytes 393224 | tf_op jit(solution)/shard_map/ppermute | solution.py:224
  58.1 1.1 fusion.19
  59.2 1.1 convolution_add_fusion.3
  60.7 13.3 %all_to_all.31 = f32[4,64,512]{2,1,0:T(8,128)S(1)} all-to-all(f32[4,64,512]{2,1,0:T(8,128)S(1)} %bitcast.89), channel_id=1, replica_groups=mesh['member'=4,'y'=8,'z'=8,'core'=2] {'member'}, dimensions={0} | all-to-all | bytes 1048576 | tf_op jit(solution)/shard_map/all_to_all | solution.py:226
  74.4 2.0 %all-gather.2.cloned.1.call-done.rows_ref = bf16[1024,1024]{1,0:T(8,128)(2,1)} async-done(((bf16[128,1024]{1,0:T(8,128)(2,1)}), bf16[1024,1024]{1,0:T(8,128)(2,1)}) %all-gather.2.cloned.1.call-update) | async-done | bytes 2097168 | tf_op jit(solution)/shard_map/all_gather | solution.py:188
  76.4 3.8 %pack_teacher.1 = bf16[2,256,1024]{2,1,0:T(8,128)(2,1)} custom-call(bf16[2,256,1024]{2,1,0:T(8,128)(2,1)} %get-tuple-element.13.one_ref, bf16[1024,1024]{1,0:T(8,128)(2,1)} %all-gather.2.cloned.1.call-done.rows_ref), custom_call_target="tpu_custom_call" | custom-call | tf_op jit(solution)/shard_map/pack_teacher/pallas_call | solution.py:100
  80.2 1.9 %collective-permute-start.1 = (bf16[2,256,1024]{2,1,0:T(8,128)(2,1)}, bf16[2,256,1024]{2,1,0:T(8,128)(2,1)S(1)}, u32[]{:S(2)}, u32[]{:S(2)}) collective-permute-start(bf16[2,256,1024]{2,1,0:T(8,128)(2,1)} %pack_teacher.1), channel_id=1, source_target_pairs={{0,1},{1,0},{2,3},{3,2},{4,5},{5,4},{6,7},{7,6},{8,9},{9,8},{10,11... | collective-permute-start | bytes 3145736 | tf_op jit(solution)/shard_map/ppermute | solution.py:238
  82.7 2.0 %fusion.6 = f32[256,512]{1,0:T(8,128)S(1)} fusion(bf16[1,4096,512]{2,1,0:T(8,128)(2,1)} %param.12, s32[]{:T(128)S(6)} %select_n.234, bf16[2,256,1024]{2,1,0:T(8,128)(2,1)} %pack_teacher.1), kind=kOutput, calls=%fused_computation.26 | convolution fusion | flops 268435456 | bytes 2097156 | tf_op jit(solution)/shard_map/dot_general | solution.py:214
  84.7 1.8 %convolution_add_fusion.1 = f32[256,512]{1,0:T(8,128)S(1)} fusion(f32[256,512]{1,0:T(8,128)S(1)} %fusion.6, bf16[1,4096,512]{2,1,0:T(8,128)(2,1)} %param.12, s32[]{:T(128)S(6)} %select_n.235, bf16[2,256,1024]{2,1,0:T(8,128)(2,1)} %pack_teacher.1), kind=kOutput, calls=%fused_computation.1 | convolution fusion | flops 268566528 | bytes 2621444 | tf_op jit(solution)/shard_map/dot_general | solution.py:214
  86.6 0.4 fusion.2
  87.0 0.5 fusion.55
  87.8 0.9 broadcast_in_dim.161
  88.7 9.3 %all-to-all-start.3 = ((f32[128,1,640]{2,1,0:T(1,128)}), f32[128,1,640]{2,1,0:T(1,128)S(1)}, u32[]{:S(2)}, u32[]{:S(2)}) async-start(f32[128,1,640]{2,1,0:T(1,128)} %broadcast_in_dim.161), calls=%async_computation.3 | async-start | bytes 655360 | tf_op jit(solution)/shard_map/all_to_all | solution.py:19
  98.1 3.4 %collective-permute-start.2 = (bf16[448,512]{1,0:T(8,128)(2,1)S(1)}, bf16[448,512]{1,0:T(8,128)(2,1)S(1)}, u32[]{:S(2)}, u32[]{:S(2)}) collective-permute-start(bf16[448,512]{1,0:T(8,128)(2,1)S(1)} %pad_maximum_fusion.1), channel_id=1, source_target_pairs={{0,128},{128,256},{256,384},{384,0},{1,129},{129,257},{257,385},{3... | collective-permute-start | bytes 1376264 | tf_op jit(solution)/shard_map/ppermute | solution.py:245
  101.5 3.1 %collective-permute-start.3 = (bf16[448,512]{1,0:T(8,128)(2,1)S(1)}, bf16[448,512]{1,0:T(8,128)(2,1)S(1)}, u32[]{:S(2)}, u32[]{:S(2)}) collective-permute-start(bf16[448,512]{1,0:T(8,128)(2,1)S(1)} %pad_maximum_fusion.1), channel_id=1, source_target_pairs={{0,256},{128,384},{256,0},{384,128},{1,257},{129,385},{257,1},{385... | collective-permute-start | bytes 1376264 | tf_op jit(solution)/shard_map/ppermute | solution.py:245
  104.6 4.0 %collective-permute-start.4 = (bf16[448,512]{1,0:T(8,128)(2,1)S(1)}, bf16[448,512]{1,0:T(8,128)(2,1)S(1)}, u32[]{:S(2)}, u32[]{:S(2)}) collective-permute-start(bf16[448,512]{1,0:T(8,128)(2,1)S(1)} %pad_maximum_fusion.1), channel_id=1, source_target_pairs={{0,384},{128,0},{256,128},{384,256},{1,385},{129,1},{257,129},{385... | collective-permute-start | bytes 1376264 | tf_op jit(solution)/shard_map/ppermute | solution.py:245
  108.7 3.8 %all-to-all-done.3.every_ref = f32[128,1,640]{2,1,0:T(1,128)S(1)} async-done(((f32[128,1,640]{2,1,0:T(1,128)}), f32[128,1,640]{2,1,0:T(1,128)S(1)}, u32[]{:S(2)}, u32[]{:S(2)}) %all-to-all-start.3) | async-done | bytes 327712 | tf_op jit(solution)/shard_map/all_to_all | solution.py:19
  112.5 0.7 copy-done.2
  113.2 2.0 %combine.1 = f32[4,1,384]{2,1,0:T(1,128)} custom-call(f32[128,1,640]{2,1,0:T(1,128)} %copy-done.2, f32[1,256]{1,0:T(1,128)} %bitcast.96), custom_call_target="tpu_custom_call" | custom-call | tf_op jit(solution)/shard_map/combine/pallas_call | solution.py:135
  115.3 4.8 %all-to-all-start.4 = ((f32[4,1,384]{2,1,0:T(1,128)}), f32[4,1,384]{2,1,0:T(1,128)S(1)}, u32[]{:S(2)}, u32[]{:S(2)}) async-start(f32[4,1,384]{2,1,0:T(1,128)} %combine.1), calls=%async_computation.4 | async-start | bytes 12288 | tf_op jit(solution)/shard_map/all_to_all | solution.py:249
  120.1 7.0 %collective-permute-done.4 = bf16[448,512]{1,0:T(8,128)(2,1)S(1)} collective-permute-done((bf16[448,512]{1,0:T(8,128)(2,1)S(1)}, bf16[448,512]{1,0:T(8,128)(2,1)S(1)}, u32[]{:S(2)}, u32[]{:S(2)}) %collective-permute-start.4) | collective-permute-done | bytes 458784 | tf_op jit(solution)/shard_map/ppermute | solution.py:245
  127.4 0.6 slice_reduce_fusion.1
  128.2 1.0 multiply_reduce_fusion
  129.8 0.4 convolution_dynamic-update-slice_fusion.2
  130.2 0.4 convolution_dynamic-update-slice_fusion.1
  132.4 1.9 %collective-permute-start.5 = (f32[64,2176]{1,0:T(8,128)S(1)}, f32[64,2176]{1,0:T(8,128)S(1)}, u32[]{:S(2)}, u32[]{:S(2)}) collective-permute-start(f32[64,2176]{1,0:T(8,128)S(1)} %constant_dynamic-update-slice_fusion.1), channel_id=1, source_target_pairs={{0,1},{1,0},{2,3},{3,2},{4,5},{5,4},{6,7},{7,6},{8,9},{9,8},{10,11... | collective-permute-start | bytes 1671176 | tf_op jit(solution)/shard_map/ppermute | solution.py:286
  134.7 0.4 convolution_dynamic-update-slice_fusion.6
  135.1 0.4 convolution_dynamic-update-slice_fusion.5
  135.5 0.4 convolution_dynamic-update-slice_fusion.4
  136.3 1.4 copy.19
  137.6 12.8 %all-to-all-start.5 = ((f32[64,1,2176]{2,1,0:T(1,128)}), f32[64,1,2176]{2,1,0:T(1,128)S(1)}, u32[]{:S(2)}, u32[]{:S(2)}) async-start(f32[64,1,2176]{2,1,0:T(1,128)} %copy.19), calls=%async_computation.5 | async-start | bytes 1114112 | tf_op jit(solution)/shard_map/all_to_all | solution.py:287
  150.5 0.6 reduce_sum.141
  151.1 0.6 dynamic_slice.48
  152.4 0.7 iota_compare_fusion.29
  153.1 17.8 %all-to-all-done.5 = f32[64,1,2176]{2,1,0:T(1,128)S(1)} async-done(((f32[64,1,2176]{2,1,0:T(1,128)}), f32[64,1,2176]{2,1,0:T(1,128)S(1)}, u32[]{:S(2)}, u32[]{:S(2)}) %all-to-all-start.5) | async-done | bytes 557088 | tf_op jit(solution)/shard_map/all_to_all | solution.py:287
  171.3 0.5 slice.223
  171.9 0.7 multiply_reduce_fusion.1
  (68 shorter events, 5.1 us)
Async XLA Ops:
  7.2 51.0 %copy-start = (bf16[512,512]{1,0:T(8,128)(2,1)S(1)}, bf16[512,512]{1,0:T(8,128)(2,1)}, u32[]{:S(2)}) copy-start(bf16[512,512]{1,0:T(8,128)(2,1)} %param.14) | copy-start | bytes 1572868
  7.2 69.2 %all-gather.2.cloned.1.call-start = ((), (), s32[]{:S(2)}) async-start(), calls=%async_computation.6 | async-start | bytes 2359296 | tf_op jit(solution)/shard_map/all_gather | solution.py:188
  33.7 19.4 %all-to-all-start.1 = ((bf16[8,128,128]{2,1,0:T(8,128)(2,1)}), bf16[8,128,128]{2,1,0:T(8,128)(2,1)S(1)}, u32[]{:S(2)}, u32[]{:S(2)}) async-start(bf16[8,128,128]{2,1,0:T(8,128)(2,1)} %broadcast_in_dim.160), calls=%async_computation.1 | async-start | bytes 524288 | tf_op jit(solution)/shard_map/all_to_all | solution.py:19
  53.1 0.7 copy-start.3
  56.2 4.1 %collective-permute-start = (bf16[2,256,128]{2,1,0:T(8,128)(2,1)}, bf16[2,256,128]{2,1,0:T(8,128)(2,1)S(1)}, u32[]{:S(2)}, u32[]{:S(2)}) collective-permute-start(bf16[2,256,128]{2,1,0:T(8,128)(2,1)} %get-tuple-element.14), channel_id=1, source_target_pairs={{0,1},{1,0},{2,3},{3,2},{4,5},{5,4},{6,7},{7,6},{8,9},{9,8},{10,11... | collective-permute-start | bytes 393224 | tf_op jit(solution)/shard_map/ppermute | solution.py:224
  60.5 21.9 %copy-start.5 = (s32[128]{0:T(128)S(1)}, s32[128]{0:T(128)}, u32[]{:S(2)}) copy-start(s32[128]{0:T(128)} %param.16) | copy-start | bytes 1540
  80.2 6.4 %collective-permute-start.1 = (bf16[2,256,1024]{2,1,0:T(8,128)(2,1)}, bf16[2,256,1024]{2,1,0:T(8,128)(2,1)S(1)}, u32[]{:S(2)}, u32[]{:S(2)}) collective-permute-start(bf16[2,256,1024]{2,1,0:T(8,128)(2,1)} %pack_teacher.1), channel_id=1, source_target_pairs={{0,1},{1,0},{2,3},{3,2},{4,5},{5,4},{6,7},{7,6},{8,9},{9,8},{10,11... | collective-permute-start | bytes 3145736 | tf_op jit(solution)/shard_map/ppermute | solution.py:238
  82.7 3.9 %copy-start.1 = (bf16[1,4096,512]{2,1,0:T(8,128)(2,1)S(1)}, bf16[1,4096,512]{2,1,0:T(8,128)(2,1)}, u32[]{:S(2)}) copy-start(bf16[1,4096,512]{2,1,0:T(8,128)(2,1)} %param.12) | copy-start | bytes 12582916
  86.5 22.0 %copy-start.6 = (s32[512]{0:T(512)S(1)}, s32[512]{0:T(512)}, u32[]{:S(2)}) copy-start(s32[512]{0:T(512)} %param.17) | copy-start | bytes 6148
  87.5 25.0 %copy-start.4 = (f32[256]{0:T(256)}, f32[256]{0:T(256)S(1)}, u32[]{:S(2)}) copy-start(f32[256]{0:T(256)S(1)} %get-tuple-element.64) | copy-start | bytes 3076
  88.7 23.8 %all-to-all-start.3 = ((f32[128,1,640]{2,1,0:T(1,128)}), f32[128,1,640]{2,1,0:T(1,128)S(1)}, u32[]{:S(2)}, u32[]{:S(2)}) async-start(f32[128,1,640]{2,1,0:T(1,128)} %broadcast_in_dim.161), calls=%async_computation.3 | async-start | bytes 655360 | tf_op jit(solution)/shard_map/all_to_all | solution.py:19
  98.1 22.0 %collective-permute-start.2 = (bf16[448,512]{1,0:T(8,128)(2,1)S(1)}, bf16[448,512]{1,0:T(8,128)(2,1)S(1)}, u32[]{:S(2)}, u32[]{:S(2)}) collective-permute-start(bf16[448,512]{1,0:T(8,128)(2,1)S(1)} %pad_maximum_fusion.1), channel_id=1, source_target_pairs={{0,128},{128,256},{256,384},{384,0},{1,129},{129,257},{257,385},{3... | collective-permute-start | bytes 1376264 | tf_op jit(solution)/shard_map/ppermute | solution.py:245
  101.5 18.6 %collective-permute-start.3 = (bf16[448,512]{1,0:T(8,128)(2,1)S(1)}, bf16[448,512]{1,0:T(8,128)(2,1)S(1)}, u32[]{:S(2)}, u32[]{:S(2)}) collective-permute-start(bf16[448,512]{1,0:T(8,128)(2,1)S(1)} %pad_maximum_fusion.1), channel_id=1, source_target_pairs={{0,256},{128,384},{256,0},{384,128},{1,257},{129,385},{257,1},{385... | collective-permute-start | bytes 1376264 | tf_op jit(solution)/shard_map/ppermute | solution.py:245
  104.6 22.5 %collective-permute-start.4 = (bf16[448,512]{1,0:T(8,128)(2,1)S(1)}, bf16[448,512]{1,0:T(8,128)(2,1)S(1)}, u32[]{:S(2)}, u32[]{:S(2)}) collective-permute-start(bf16[448,512]{1,0:T(8,128)(2,1)S(1)} %pad_maximum_fusion.1), channel_id=1, source_target_pairs={{0,384},{128,0},{256,128},{384,256},{1,385},{129,1},{257,129},{385... | collective-permute-start | bytes 1376264 | tf_op jit(solution)/shard_map/ppermute | solution.py:245
  112.5 0.7 copy-start.2
  115.3 11.8 %all-to-all-start.4 = ((f32[4,1,384]{2,1,0:T(1,128)}), f32[4,1,384]{2,1,0:T(1,128)S(1)}, u32[]{:S(2)}, u32[]{:S(2)}) async-start(f32[4,1,384]{2,1,0:T(1,128)} %combine.1), calls=%async_computation.4 | async-start | bytes 12288 | tf_op jit(solution)/shard_map/all_to_all | solution.py:249
  130.6 22.4 %copy-start.7 = (s32[1,4]{1,0:T(1,128)S(1)}, s32[1,4]{1,0:T(1,128)}, u32[]{:S(2)}) copy-start(s32[1,4]{1,0:T(1,128)} %refs_0_.1) | copy-start | bytes 52
  132.4 3.9 %collective-permute-start.5 = (f32[64,2176]{1,0:T(8,128)S(1)}, f32[64,2176]{1,0:T(8,128)S(1)}, u32[]{:S(2)}, u32[]{:S(2)}) collective-permute-start(f32[64,2176]{1,0:T(8,128)S(1)} %constant_dynamic-update-slice_fusion.1), channel_id=1, source_target_pairs={{0,1},{1,0},{2,3},{3,2},{4,5},{5,4},{6,7},{7,6},{8,9},{9,8},{10,11... | collective-permute-start | bytes 1671176 | tf_op jit(solution)/shard_map/ppermute | solution.py:286
  137.6 33.3 %all-to-all-start.5 = ((f32[64,1,2176]{2,1,0:T(1,128)}), f32[64,1,2176]{2,1,0:T(1,128)S(1)}, u32[]{:S(2)}, u32[]{:S(2)}) async-start(f32[64,1,2176]{2,1,0:T(1,128)} %copy.19), calls=%async_computation.5 | async-start | bytes 1114112 | tf_op jit(solution)/shard_map/all_to_all | solution.py:287
Sparse Core Ops, SparseCore 0:
  32.3 44.0 all-gather.1

commit v7 on v6

--- a/solution.py
+++ b/solution.py
@@ -64,17 +64,16 @@
     )(slot_ids, teacher_hidden, teacher_gain, student_hidden)
 
 
-def one_hot_kernel(places_ref, rows_ref, packed_ref, one_ref):
+def one_hot_kernel(places_ref, ring_places_ref, rows_ref, packed_ref, one_ref):
     live = packed_ref.shape[1]
     ids = lax.broadcasted_iota(jnp.int32, (live, places_ref.shape[1]), 0)
     for side in range(2):
-        one_ref[side] = (ids == places_ref[side : side + 1, :]).astype(BF16)
-        packed_ref[side] = jnp.dot(
-            one_ref[side], rows_ref[...], preferred_element_type=F32
-        ).astype(BF16)
-
-
-def pack_with_places(places, rows, live):
+        one = (ids == places_ref[side : side + 1, :]).astype(BF16)
+        packed_ref[side] = jnp.dot(one, rows_ref[...], preferred_element_type=F32).astype(BF16)
+        one_ref[side] = (ids == ring_places_ref[side : side + 1, :]).astype(BF16)
+
+
+def pack_with_places(places, ring_places, rows, live):
     total, features = rows.shape
     return pl.pallas_call(
         one_hot_kernel,
@@ -83,31 +82,48 @@
             jax.ShapeDtypeStruct((2, live, total), BF16),
         ),
         name="pack_student",
-    )(places, rows)
-
-
-def pack_kernel(one_ref, rows_ref, packed_ref):
+    )(places, ring_places, rows)
+
+
+def pack_kernel(one_ref, *refs):
+    blocks, packed_ref = refs[:-1], refs[-1]
+    rows = jnp.concatenate([block[...] for block in blocks], axis=0)
     for side in range(2):
-        packed_ref[side] = jnp.dot(
-            one_ref[side], rows_ref[...], preferred_element_type=F32
-        ).astype(BF16)
-
-
-def pack_rows(one, rows, parts):
-    total, features = rows.shape
+        packed_ref[side] = jnp.dot(one_ref[side], rows, preferred_element_type=F32).astype(BF16)
+
+
+def pack_rows(one, blocks, parts):
+    total = one.shape[2]
+    features = blocks[0].shape[1]
     live = one.shape[1]
     part = features // parts
     return pl.pallas_call(
         pack_kernel,
         grid=(parts,),
         out_shape=jax.ShapeDtypeStruct((2, live, features), BF16),
-        in_specs=[
-            pl.BlockSpec((2, live, total), lambda i: (0, 0, 0)),
-            pl.BlockSpec((total, part), lambda i: (0, i)),
-        ],
+        in_specs=[pl.BlockSpec((2, live, total), lambda i: (0, 0, 0))]
+        + [pl.BlockSpec((block.shape[0], part), lambda i: (0, i)) for block in blocks],
         out_specs=pl.BlockSpec((2, live, part), lambda i: (0, 0, i)),
         name="pack_teacher",
-    )(one, rows)
+    )(one, *blocks)
+
+
+def both_ways(block, axis, size):
+    ahead = [(i, (i + 1) % size) for i in range(size)]
+    back = [(i, (i - 1) % size) for i in range(size)]
+    result, offsets = [block], [0]
+    behind = front = block
+    for step in range(1, size // 2):
+        behind = lax.ppermute(behind, axis, ahead)
+        front = lax.ppermute(front, axis, back)
+        result += [behind, front]
+        offsets += [-step, step]
+    half = block.shape[0] // 2
+    result += [
+        lax.ppermute(behind[:half], axis, ahead),
+        lax.ppermute(front[half:], axis, back),
+    ]
+    return result, offsets + [size // 2]
 
 
 def combine_kernel(every_ref, top_ref, sent_ref):
@@ -185,7 +201,8 @@
     sent = sent.reshape(ring * cores, 2 * cap, -1)
     group_rows = lax.all_to_all(sent, ("z", "core"), 0, 0, tiled=True)
     group_rows = group_rows.reshape(ring * cores * 2 * cap, -1)
-    teacher_rows = lax.all_gather(group_rows[:, :quarter], "y", axis=0, tiled=True)
+    lengths = lax.axis_size("y")
+    blocks, offsets = both_ways(group_rows[:, :quarter], "y", lengths)
 
     before = (
         jnp.arange(owners, dtype=jnp.int32)[:, None] < jnp.arange(owners, dtype=jnp.int32)[None, :]
@@ -195,12 +212,17 @@
     places = jnp.where(slots[None, :] < counts[:, None], starts[:, None] + slots[None, :], -1)
     packed_ids = jnp.arange(live_rows, dtype=jnp.int32)
     sides = jnp.arange(2, dtype=jnp.int32)
-    side_places = jnp.stack(
-        [
-            jnp.where(sides[None, :, None] == side, places[:, None, :], -1).reshape(-1)
-            for side in range(2)
-        ]
-    )
+
+    def two_sides(held):
+        return jnp.stack(
+            [
+                jnp.where(sides[None, :, None] == side, held[:, None, :], -1).reshape(-1)
+                for side in range(2)
+            ]
+        )
+
+    sources = (lax.axis_index("y") + jnp.array(offsets, jnp.int32)) % lengths
+    ring_places = jnp.take(places.reshape(lengths, -1), sources, axis=0).reshape(owners, cap)
     live_targets = jnp.sum(
         jnp.where(packed_ids[:, None] == places.reshape(1, padded), targets[None, :], 0), axis=1
     )
@@ -220,7 +242,9 @@
 
     student_rows = spread(group_rows[:, quarter:], "y", lax.axis_size("y"))
     student_rows = student_rows.reshape(2 * padded, -1)
-    mine, one = pack_with_places(side_places, student_rows, live_rows)
+    mine, one = pack_with_places(
+        two_sides(places), two_sides(ring_places), student_rows, live_rows
+    )
     partial_logits = both_halves(mine, lax.ppermute(mine, "core", swap), student_head)
     logits_chunk = jnp.sum(
         lax.all_to_all(
@@ -231,10 +255,10 @@
     student_top, _, student_total = softmax_stats(logits_chunk)
     vocab_ids = owner * vocab + jnp.arange(vocab, dtype=jnp.int32)
     hit = vocab_ids[None, :] == live_targets[:, None]
-    teacher_rows, student_top, student_total = lax.optimization_barrier(
-        (teacher_rows, student_top, student_total)
-    )
-    mine = pack_rows(one, teacher_rows, 2)
+    student_top, student_total, *blocks = lax.optimization_barrier(
+        (student_top, student_total, *blocks)
+    )
+    mine = pack_rows(one, blocks, 2)
     teacher_logits = both_halves(mine, lax.ppermute(mine, "core", swap), teacher_head[0])
     top, shifted, total = softmax_stats(teacher_logits)
     every = spread(

time: 182 us -> 188 us (1.033)
  starting transfers between devices: 50.6 us -> 91.2 us
  blocking collectives: 35.5 us -> 0 us
  between operations: 18.4 us -> 5.16 us
  waiting for transfers between devices: 41 us -> 48 us
  local copies, waits for them, and re-layouts: 7.35 us -> 11.1 us
    all_to_all x2 -> x0, blocking collectives: 35.5 us -> none  [the longest x1 22.2 us: on_device(): group_rows = lax.all_to_all(sent, ('z', 'core'), 0, 0, tiled=True)]
    ppermute x0 -> x8, starting transfers between devices: none -> 23.3 us  [the longest x3 9.19 us: both_ways(): behind = lax.ppermute(behind, axis, ahead)]
    all_to_all x0 -> x2, starting transfers between devices: none -> 15.2 us  [the longest x1 10.4 us: on_device(): group_rows = lax.all_to_all(sent, ('z', 'core'), 0, 0, tiled=True)]
    ppermute x0 -> x8, waiting for transfers between devices: none -> 9.74 us  [the longest x1 5.35 us: both_ways(): lax.ppermute(front[half:], axis, back)]
    all_to_all x2, waiting for transfers between devices: 13.8 us -> 5.55 us  [spread(): lax.all_to_all(jnp.broadcast_to(block[None], (size,) + block.shape), axes...]
    all_to_all x0 -> x2, waiting for transfers between devices: none -> 7.51 us  [the longest x1 7.51 us: on_device(): group_rows = lax.all_to_all(sent, ('z', 'core'), 0, 0, tiled=True)]
    all_gather x1 -> x0, waiting for transfers between devices: 1.97 us -> none  [on_device(): lax.all_gather(group_rows[:, :quarter], 'y', axis=0, tiled=True)]
    all_to_all x2, starting transfers between devices: 16.7 us -> 18.6 us  [spread(): lax.all_to_all(jnp.broadcast_to(block[None], (size,) + block.shape), axes...]
  transfers between devices with their start and end apart: 11 -> 20, of which waited for: 7 -> 10; matrix products, arithmetic and copies ran while one was open for 8% -> 11% of each run, Pallas kernels for 2% -> 3%
where the time goes in v7:
time: 188 us; the launch traced here: 187 us
  starting transfers between devices  91.2 us (49%)
  waiting for transfers between devices  48 us (26%)
  matrix products  11.3 us (6%)
  local copies, waits for them, and re-layouts  11.1 us (6%)
  Pallas kernels  11 us (6%)
  other arithmetic  9.16 us (5%)
  between operations  5.16 us (3%)
    all_to_all x2, starting transfers between devices, spread(): lax.all_to_all(jnp.broadcast_to(block[None], (size,) + block.shape), axes...  18.6 us
    all_to_all x1, waiting for transfers between devices, on_device(): lax.all_to_all(grads[:, None, :], CHIPS, 0, 0, tiled=True)  18 us
    all_to_all x1, starting transfers between devices, on_device(): lax.all_to_all(grads[:, None, :], CHIPS, 0, 0, tiled=True)  12.9 us
    ppermute x3, starting transfers between devices, on_device(): lax.ppermute(shared, 'member', [(i, (i + step) % members) for i in range(...  10.4 us
    all_to_all x1, starting transfers between devices, on_device(): group_rows = lax.all_to_all(sent, ('z', 'core'), 0, 0, tiled=True)  10.4 us
    ppermute x3, starting transfers between devices, both_ways(): behind = lax.ppermute(behind, axis, ahead)  9.19 us
    ppermute x3, starting transfers between devices, both_ways(): front = lax.ppermute(front, axis, back)  8.31 us
    dot_general x8, matrix products, both_halves(): jnp.dot(values[side], lax.dynamic_slice_in_dim(weights, first + side * pa...  8.13 us
  transfers between devices with their start and end apart: 20, of which 10 were waited for; matrix products, arithmetic and copies ran while one was open for 11% of the time, Pallas kernels for 3%

profile of v7, /device:TPU:18, one launch (start us, length us, event | category | flops | bytes accessed | tf_op | source)
XLA Modules:
  0.0 186.8 jit_solution(5360131200009087670)
XLA Ops:
  0.6 2.0 %own_rows.1 = bf16[128,1152]{1,0:T(8,128)(2,1)} custom-call(s32[1,4]{1,0:T(1,128)} %refs_0_.1, bf16[1,16,4096]{2,1,0:T(8,128)(2,1)} %refs_1_.1, f32[1,4096]{1,0:T(1,128)} %refs_2_.1, bf16[16,512]{1,0:T(8,128)(2,1)} %refs_3_.1), custom_call_target="tpu_custom_call" | custom-call | tf_op jit(solution)/shard_map/own_rows/pallas_call | solution.py:57
  2.6 10.4 %all-to-all-start = ((bf16[16,8,1152]{2,1,0:T(8,128)(2,1)}), bf16[16,8,1152]{2,1,0:T(8,128)(2,1)S(1)}, u32[]{:S(2)}, u32[]{:S(2)}) async-start(bf16[16,8,1152]{2,1,0:T(8,128)(2,1)} %bitcast.93), calls=%async_computation | async-start | bytes 589824 | tf_op jit(solution)/shard_map/all_to_all | solution.py:202
  13.1 0.8 select_reduce_fusion.1
  13.8 0.7 lt.180
  16.6 0.8 add_select_fusion
  17.3 7.5 %all-to-all-done = bf16[16,8,1152]{2,1,0:T(8,128)(2,1)S(1)} async-done(((bf16[16,8,1152]{2,1,0:T(8,128)(2,1)}), bf16[16,8,1152]{2,1,0:T(8,128)(2,1)S(1)}, u32[]{:S(2)}, u32[]{:S(2)}) %all-to-all-start) | async-done | bytes 294944 | tf_op jit(solution)/shard_map/all_to_all | solution.py:202
  24.9 3.5 %collective-permute-start.1 = (bf16[128,1024]{1,0:T(8,128)(2,1)S(1)}, bf16[128,1024]{1,0:T(8,128)(2,1)S(1)}, u32[]{:S(2)}, u32[]{:S(2)}) collective-permute-start(bf16[128,1024]{1,0:T(8,128)(2,1)S(1)} %slice.214.refs_0_), channel_id=1, source_target_pairs={{0,16},{16,32},{32,48},{48,64},{64,80},{80,96},{96,112},{112,0},{1... | collective-permute-start | bytes 786440 | tf_op jit(solution)/shard_map/ppermute | solution.py:117
  28.4 2.4 %collective-permute-start.2 = (bf16[128,1024]{1,0:T(8,128)(2,1)S(1)}, bf16[128,1024]{1,0:T(8,128)(2,1)S(1)}, u32[]{:S(2)}, u32[]{:S(2)}) collective-permute-start(bf16[128,1024]{1,0:T(8,128)(2,1)S(1)} %slice.214.refs_0_), channel_id=1, source_target_pairs={{0,112},{16,0},{32,16},{48,32},{64,48},{80,64},{96,80},{112,96},{1... | collective-permute-start | bytes 786440 | tf_op jit(solution)/shard_map/ppermute | solution.py:118
  30.7 0.7 broadcast_in_dim.207
  31.5 8.6 %all-to-all-start.1 = ((bf16[8,128,128]{2,1,0:T(8,128)(2,1)}), bf16[8,128,128]{2,1,0:T(8,128)(2,1)S(1)}, u32[]{:S(2)}, u32[]{:S(2)}) async-start(bf16[8,128,128]{2,1,0:T(8,128)(2,1)} %broadcast_in_dim.207), calls=%async_computation.1 | async-start | bytes 524288 | tf_op jit(solution)/shard_map/all_to_all | solution.py:19
  42.4 3.4 %collective-permute-start.3 = (bf16[128,1024]{1,0:T(8,128)(2,1)S(1)}, bf16[128,1024]{1,0:T(8,128)(2,1)S(1)}, u32[]{:S(2)}, u32[]{:S(2)}) collective-permute-start(bf16[128,1024]{1,0:T(8,128)(2,1)S(1)} %collective-permute-done.1.refs_1_), channel_id=1, source_target_pairs={{0,16},{16,32},{32,48},{48,64},{64,80},{80,96},{96,112},{112,0},{1... | collective-permute-start | bytes 786440 | tf_op jit(solution)/shard_map/ppermute | solution.py:117
  45.8 2.5 %collective-permute-start.4 = (bf16[128,1024]{1,0:T(8,128)(2,1)S(1)}, bf16[128,1024]{1,0:T(8,128)(2,1)S(1)}, u32[]{:S(2)}, u32[]{:S(2)}) collective-permute-start(bf16[128,1024]{1,0:T(8,128)(2,1)S(1)} %collective-permute-done.2.refs_2_), channel_id=1, source_target_pairs={{0,112},{16,0},{32,16},{48,32},{64,48},{80,64},{96,80},{112,96},{1... | collective-permute-start | bytes 786440 | tf_op jit(solution)/shard_map/ppermute | solution.py:118
  48.3 1.7 all-to-all-done.1
  50.0 0.7 copy-done.4
  50.7 2.8 %pack_student.1 = (bf16[2,256,128]{2,1,0:T(8,128)(2,1)}, bf16[2,256,1024]{2,1,0:T(8,128)(2,1)}) custom-call(s32[2,1024]{1,0:T(2,128)} %pad_add_fusion.places_ref, s32[2,1024]{1,0:T(2,128)} %pad_add_fusion.1.ring_places_ref, bf16[1024,128]{1,0:T(8,128)(2,1)} %bitcast.94), custom_call_target="tpu_custom_call" | custom-call | tf_op jit(solution)/shard_map/pack_student/pallas_call | solution.py:78
  53.5 1.9 %collective-permute-start = (bf16[2,256,128]{2,1,0:T(8,128)(2,1)}, bf16[2,256,128]{2,1,0:T(8,128)(2,1)S(1)}, u32[]{:S(2)}, u32[]{:S(2)}) collective-permute-start(bf16[2,256,128]{2,1,0:T(8,128)(2,1)} %get-tuple-element.22), channel_id=1, source_target_pairs={{0,1},{1,0},{2,3},{3,2},{4,5},{5,4},{6,7},{7,6},{8,9},{9,8},{10,11... | collective-permute-start | bytes 393224 | tf_op jit(solution)/shard_map/ppermute | solution.py:248
  55.4 1.1 fusion.19
  56.5 1.1 convolution_add_fusion.3
  57.8 1.0 fusion.1
  58.8 4.8 %all-to-all-start.2 = ((f32[4,64,512]{2,1,0:T(8,128)}), f32[4,64,512]{2,1,0:T(8,128)S(1)}, u32[]{:S(2)}, u32[]{:S(2)}) async-start(f32[4,64,512]{2,1,0:T(8,128)} %bitcast.11), calls=%async_computation.2 | async-start | bytes 1048576 | tf_op jit(solution)/shard_map/all_to_all | solution.py:250
  63.7 2.3 %collective-permute-start.5 = (bf16[128,1024]{1,0:T(8,128)(2,1)S(1)}, bf16[128,1024]{1,0:T(8,128)(2,1)S(1)}, u32[]{:S(2)}, u32[]{:S(2)}) collective-permute-start(bf16[128,1024]{1,0:T(8,128)(2,1)S(1)} %collective-permute-done.3.refs_3_), channel_id=1, source_target_pairs={{0,16},{16,32},{32,48},{48,64},{64,80},{80,96},{96,112},{112,0},{1... | collective-permute-start | bytes 786440 | tf_op jit(solution)/shard_map/ppermute | solution.py:117
  66.0 3.5 %collective-permute-start.6 = (bf16[128,1024]{1,0:T(8,128)(2,1)S(1)}, bf16[128,1024]{1,0:T(8,128)(2,1)S(1)}, u32[]{:S(2)}, u32[]{:S(2)}) collective-permute-start(bf16[128,1024]{1,0:T(8,128)(2,1)S(1)} %collective-permute-done.4.refs_4_), channel_id=1, source_target_pairs={{0,112},{16,0},{32,16},{48,32},{64,48},{80,64},{96,80},{112,96},{1... | collective-permute-start | bytes 786440 | tf_op jit(solution)/shard_map/ppermute | solution.py:118
  69.5 4.2 %collective-permute-done.5.refs_5_ = bf16[128,1024]{1,0:T(8,128)(2,1)S(1)} collective-permute-done((bf16[128,1024]{1,0:T(8,128)(2,1)S(1)}, bf16[128,1024]{1,0:T(8,128)(2,1)S(1)}, u32[]{:S(2)}, u32[]{:S(2)}) %collective-permute-start.5) | collective-permute-done | bytes 262176 | tf_op jit(solution)/shard_map/ppermute | solution.py:117
  73.8 0.7 slice.215
  74.5 2.9 %collective-permute-start.7 = (bf16[64,1024]{1,0:T(8,128)(2,1)}, bf16[64,1024]{1,0:T(8,128)(2,1)S(1)}, u32[]{:S(2)}, u32[]{:S(2)}) collective-permute-start(bf16[64,1024]{1,0:T(8,128)(2,1)} %slice.215), channel_id=1, source_target_pairs={{0,16},{16,32},{32,48},{48,64},{64,80},{80,96},{96,112},{112,0},{1... | collective-permute-start | bytes 393224 | tf_op jit(solution)/shard_map/ppermute | solution.py:123
  77.5 0.7 slice.216
  78.2 2.9 %collective-permute-start.8 = (bf16[64,1024]{1,0:T(8,128)(2,1)}, bf16[64,1024]{1,0:T(8,128)(2,1)S(1)}, u32[]{:S(2)}, u32[]{:S(2)}) collective-permute-start(bf16[64,1024]{1,0:T(8,128)(2,1)} %slice.216), channel_id=1, source_target_pairs={{0,112},{16,0},{32,16},{48,32},{64,48},{80,64},{96,80},{112,96},{1... | collective-permute-start | bytes 393224 | tf_op jit(solution)/shard_map/ppermute | solution.py:124
  81.5 5.4 %collective-permute-done.8.refs_8_ = bf16[64,1024]{1,0:T(8,128)(2,1)S(1)} collective-permute-done((bf16[64,1024]{1,0:T(8,128)(2,1)}, bf16[64,1024]{1,0:T(8,128)(2,1)S(1)}, u32[]{:S(2)}, u32[]{:S(2)}) %collective-permute-start.8) | collective-permute-done | bytes 131104 | tf_op jit(solution)/shard_map/ppermute | solution.py:124
  87.5 4.2 %pack_teacher.1 = bf16[2,256,1024]{2,1,0:T(8,128)(2,1)} custom-call(bf16[2,256,1024]{2,1,0:T(8,128)(2,1)} %get-tuple-element.21.one_ref, bf16[128,1024]{1,0:T(8,128)(2,1)} %copy-done.3, bf16[128,1024]{1,0:T(8,128)(2,1)} %copy-done.7, bf16[128,1024]{1,0:T(8,128)(2,1)} %copy-done.8, bf16[128,1024]{1,0:T(8,128)(2,1)} %copy-done.9, ...), custom_call_target="tpu_custom_call" | custom-call | tf_op jit(solution)/shard_map/pack_teacher/pallas_call | solution.py:100
  91.7 1.9 %collective-permute-start.9 = (bf16[2,256,1024]{2,1,0:T(8,128)(2,1)}, bf16[2,256,1024]{2,1,0:T(8,128)(2,1)S(1)}, u32[]{:S(2)}, u32[]{:S(2)}) collective-permute-start(bf16[2,256,1024]{2,1,0:T(8,128)(2,1)} %pack_teacher.1), channel_id=1, source_target_pairs={{0,1},{1,0},{2,3},{3,2},{4,5},{5,4},{6,7},{7,6},{8,9},{9,8},{10,11... | collective-permute-start | bytes 3145736 | tf_op jit(solution)/shard_map/ppermute | solution.py:262
  94.3 2.0 %fusion.6 = f32[256,512]{1,0:T(8,128)S(1)} fusion(bf16[1,4096,512]{2,1,0:T(8,128)(2,1)} %param.13, s32[]{:T(128)S(6)} %select_n.290, bf16[2,256,1024]{2,1,0:T(8,128)(2,1)} %pack_teacher.1), kind=kOutput, calls=%fused_computation.27 | convolution fusion | flops 268435456 | bytes 2097156 | tf_op jit(solution)/shard_map/dot_general | solution.py:236
  96.3 1.8 convolution_add_fusion.1
  99.4 0.9 broadcast_in_dim.208
  100.3 10.0 %all-to-all-start.3 = ((f32[128,1,640]{2,1,0:T(1,128)}), f32[128,1,640]{2,1,0:T(1,128)S(1)}, u32[]{:S(2)}, u32[]{:S(2)}) async-start(f32[128,1,640]{2,1,0:T(1,128)} %broadcast_in_dim.208), calls=%async_computation.3 | async-start | bytes 655360 | tf_op jit(solution)/shard_map/all_to_all | solution.py:19
  110.4 3.4 %collective-permute-start.10 = (bf16[448,512]{1,0:T(8,128)(2,1)S(1)}, bf16[448,512]{1,0:T(8,128)(2,1)S(1)}, u32[]{:S(2)}, u32[]{:S(2)}) collective-permute-start(bf16[448,512]{1,0:T(8,128)(2,1)S(1)} %pad_maximum_fusion.1), channel_id=1, source_target_pairs={{0,128},{128,256},{256,384},{384,0},{1,129},{129,257},{257,385},{3... | collective-permute-start | bytes 1376264 | tf_op jit(solution)/shard_map/ppermute | solution.py:269
  113.8 2.8 %collective-permute-start.11 = (bf16[448,512]{1,0:T(8,128)(2,1)S(1)}, bf16[448,512]{1,0:T(8,128)(2,1)S(1)}, u32[]{:S(2)}, u32[]{:S(2)}) collective-permute-start(bf16[448,512]{1,0:T(8,128)(2,1)S(1)} %pad_maximum_fusion.1), channel_id=1, source_target_pairs={{0,256},{128,384},{256,0},{384,128},{1,257},{129,385},{257,1},{385... | collective-permute-start | bytes 1376264 | tf_op jit(solution)/shard_map/ppermute | solution.py:269
  116.6 4.3 %collective-permute-start.12 = (bf16[448,512]{1,0:T(8,128)(2,1)S(1)}, bf16[448,512]{1,0:T(8,128)(2,1)S(1)}, u32[]{:S(2)}, u32[]{:S(2)}) collective-permute-start(bf16[448,512]{1,0:T(8,128)(2,1)S(1)} %pad_maximum_fusion.1), channel_id=1, source_target_pairs={{0,384},{128,0},{256,128},{384,256},{1,385},{129,1},{257,129},{385... | collective-permute-start | bytes 1376264 | tf_op jit(solution)/shard_map/ppermute | solution.py:269
  121.0 3.8 %all-to-all-done.3.every_ref = f32[128,1,640]{2,1,0:T(1,128)S(1)} async-done(((f32[128,1,640]{2,1,0:T(1,128)}), f32[128,1,640]{2,1,0:T(1,128)S(1)}, u32[]{:S(2)}, u32[]{:S(2)}) %all-to-all-start.3) | async-done | bytes 327712 | tf_op jit(solution)/shard_map/all_to_all | solution.py:19
  124.8 0.7 copy-done.2
  125.5 2.0 %combine.1 = f32[4,1,384]{2,1,0:T(1,128)} custom-call(f32[128,1,640]{2,1,0:T(1,128)} %copy-done.2, f32[1,256]{1,0:T(1,128)} %bitcast.99), custom_call_target="tpu_custom_call" | custom-call | tf_op jit(solution)/shard_map/combine/pallas_call | solution.py:151
  127.6 4.8 %all-to-all-start.4 = ((f32[4,1,384]{2,1,0:T(1,128)}), f32[4,1,384]{2,1,0:T(1,128)S(1)}, u32[]{:S(2)}, u32[]{:S(2)}) async-start(f32[4,1,384]{2,1,0:T(1,128)} %combine.1), calls=%async_computation.4 | async-start | bytes 12288 | tf_op jit(solution)/shard_map/all_to_all | solution.py:273
  132.4 6.9 %collective-permute-done.12 = bf16[448,512]{1,0:T(8,128)(2,1)S(1)} collective-permute-done((bf16[448,512]{1,0:T(8,128)(2,1)S(1)}, bf16[448,512]{1,0:T(8,128)(2,1)S(1)}, u32[]{:S(2)}, u32[]{:S(2)}) %collective-permute-start.12) | collective-permute-done | bytes 458784 | tf_op jit(solution)/shard_map/ppermute | solution.py:269
  140.5 1.0 multiply_reduce_fusion
  144.6 2.1 %collective-permute-start.13 = (f32[64,2176]{1,0:T(8,128)S(1)}, f32[64,2176]{1,0:T(8,128)S(1)}, u32[]{:S(2)}, u32[]{:S(2)}) collective-permute-start(f32[64,2176]{1,0:T(8,128)S(1)} %constant_dynamic-update-slice_fusion.1), channel_id=1, source_target_pairs={{0,1},{1,0},{2,3},{3,2},{4,5},{5,4},{6,7},{7,6},{8,9},{9,8},{10,11... | collective-permute-start | bytes 1671176 | tf_op jit(solution)/shard_map/ppermute | solution.py:310
  148.6 1.4 copy.32
  149.9 12.9 %all-to-all-start.5 = ((f32[64,1,2176]{2,1,0:T(1,128)}), f32[64,1,2176]{2,1,0:T(1,128)S(1)}, u32[]{:S(2)}, u32[]{:S(2)}) async-start(f32[64,1,2176]{2,1,0:T(1,128)} %copy.32), calls=%async_computation.5 | async-start | bytes 1114112 | tf_op jit(solution)/shard_map/all_to_all | solution.py:311
  165.4 18.0 %all-to-all-done.5 = f32[64,1,2176]{2,1,0:T(1,128)S(1)} async-done(((f32[64,1,2176]{2,1,0:T(1,128)}), f32[64,1,2176]{2,1,0:T(1,128)S(1)}, u32[]{:S(2)}, u32[]{:S(2)}) %all-to-all-start.5) | async-done | bytes 557088 | tf_op jit(solution)/shard_map/all_to_all | solution.py:311
  184.3 0.7 multiply_reduce_fusion.1
  (123 shorter events, 15.1 us)
Async XLA Ops:
  0.6 54.8 %copy-start = (bf16[512,512]{1,0:T(8,128)(2,1)S(1)}, bf16[512,512]{1,0:T(8,128)(2,1)}, u32[]{:S(2)}) copy-start(bf16[512,512]{1,0:T(8,128)(2,1)} %param.15) | copy-start | bytes 1572868
  2.6 22.2 %all-to-all-start = ((bf16[16,8,1152]{2,1,0:T(8,128)(2,1)}), bf16[16,8,1152]{2,1,0:T(8,128)(2,1)S(1)}, u32[]{:S(2)}, u32[]{:S(2)}) async-start(bf16[16,8,1152]{2,1,0:T(8,128)(2,1)} %bitcast.93), calls=%async_computation | async-start | bytes 589824 | tf_op jit(solution)/shard_map/all_to_all | solution.py:202
  24.9 53.3 %copy-start.3 = (bf16[128,1024]{1,0:T(8,128)(2,1)}, bf16[128,1024]{1,0:T(8,128)(2,1)S(1)}, u32[]{:S(2)}) copy-start(bf16[128,1024]{1,0:T(8,128)(2,1)S(1)} %slice.214.refs_0_) | copy-start | bytes 786436
  24.9 17.5 %collective-permute-start.1 = (bf16[128,1024]{1,0:T(8,128)(2,1)S(1)}, bf16[128,1024]{1,0:T(8,128)(2,1)S(1)}, u32[]{:S(2)}, u32[]{:S(2)}) collective-permute-start(bf16[128,1024]{1,0:T(8,128)(2,1)S(1)} %slice.214.refs_0_), channel_id=1, source_target_pairs={{0,16},{16,32},{32,48},{48,64},{64,80},{80,96},{96,112},{112,0},{1... | collective-permute-start | bytes 786440 | tf_op jit(solution)/shard_map/ppermute | solution.py:117
  28.4 17.4 %collective-permute-start.2 = (bf16[128,1024]{1,0:T(8,128)(2,1)S(1)}, bf16[128,1024]{1,0:T(8,128)(2,1)S(1)}, u32[]{:S(2)}, u32[]{:S(2)}) collective-permute-start(bf16[128,1024]{1,0:T(8,128)(2,1)S(1)} %slice.214.refs_0_), channel_id=1, source_target_pairs={{0,112},{16,0},{32,16},{48,32},{64,48},{80,64},{96,80},{112,96},{1... | collective-permute-start | bytes 786440 | tf_op jit(solution)/shard_map/ppermute | solution.py:118
  31.5 18.5 %all-to-all-start.1 = ((bf16[8,128,128]{2,1,0:T(8,128)(2,1)}), bf16[8,128,128]{2,1,0:T(8,128)(2,1)S(1)}, u32[]{:S(2)}, u32[]{:S(2)}) async-start(bf16[8,128,128]{2,1,0:T(8,128)(2,1)} %broadcast_in_dim.207), calls=%async_computation.1 | async-start | bytes 524288 | tf_op jit(solution)/shard_map/all_to_all | solution.py:19
  42.4 44.5 %copy-start.7 = (bf16[128,1024]{1,0:T(8,128)(2,1)}, bf16[128,1024]{1,0:T(8,128)(2,1)S(1)}, u32[]{:S(2)}) copy-start(bf16[128,1024]{1,0:T(8,128)(2,1)S(1)} %collective-permute-done.1.refs_1_) | copy-start | bytes 786436
  42.4 21.3 %collective-permute-start.3 = (bf16[128,1024]{1,0:T(8,128)(2,1)S(1)}, bf16[128,1024]{1,0:T(8,128)(2,1)S(1)}, u32[]{:S(2)}, u32[]{:S(2)}) collective-permute-start(bf16[128,1024]{1,0:T(8,128)(2,1)S(1)} %collective-permute-done.1.refs_1_), channel_id=1, source_target_pairs={{0,16},{16,32},{32,48},{48,64},{64,80},{80,96},{96,112},{112,0},{1... | collective-permute-start | bytes 786440 | tf_op jit(solution)/shard_map/ppermute | solution.py:117
  45.8 41.1 %copy-start.8 = (bf16[128,1024]{1,0:T(8,128)(2,1)}, bf16[128,1024]{1,0:T(8,128)(2,1)S(1)}, u32[]{:S(2)}) copy-start(bf16[128,1024]{1,0:T(8,128)(2,1)S(1)} %collective-permute-done.2.refs_2_) | copy-start | bytes 786436
  45.8 20.2 %collective-permute-start.4 = (bf16[128,1024]{1,0:T(8,128)(2,1)S(1)}, bf16[128,1024]{1,0:T(8,128)(2,1)S(1)}, u32[]{:S(2)}, u32[]{:S(2)}) collective-permute-start(bf16[128,1024]{1,0:T(8,128)(2,1)S(1)} %collective-permute-done.2.refs_2_), channel_id=1, source_target_pairs={{0,112},{16,0},{32,16},{48,32},{64,48},{80,64},{96,80},{112,96},{1... | collective-permute-start | bytes 786440 | tf_op jit(solution)/shard_map/ppermute | solution.py:118
  50.0 0.7 copy-start.4
  53.5 4.1 %collective-permute-start = (bf16[2,256,128]{2,1,0:T(8,128)(2,1)}, bf16[2,256,128]{2,1,0:T(8,128)(2,1)S(1)}, u32[]{:S(2)}, u32[]{:S(2)}) collective-permute-start(bf16[2,256,128]{2,1,0:T(8,128)(2,1)} %get-tuple-element.22), channel_id=1, source_target_pairs={{0,1},{1,0},{2,3},{3,2},{4,5},{5,4},{6,7},{7,6},{8,9},{9,8},{10,11... | collective-permute-start | bytes 393224 | tf_op jit(solution)/shard_map/ppermute | solution.py:248
  57.8 36.2 %copy-start.14 = (s32[128]{0:T(128)S(1)}, s32[128]{0:T(128)}, u32[]{:S(2)}) copy-start(s32[128]{0:T(128)} %param.17) | copy-start | bytes 1540
  58.8 22.2 %all-to-all-start.2 = ((f32[4,64,512]{2,1,0:T(8,128)}), f32[4,64,512]{2,1,0:T(8,128)S(1)}, u32[]{:S(2)}, u32[]{:S(2)}) async-start(f32[4,64,512]{2,1,0:T(8,128)} %bitcast.11), calls=%async_computation.2 | async-start | bytes 1048576 | tf_op jit(solution)/shard_map/all_to_all | solution.py:250
  63.7 23.2 %copy-start.9 = (bf16[128,1024]{1,0:T(8,128)(2,1)}, bf16[128,1024]{1,0:T(8,128)(2,1)S(1)}, u32[]{:S(2)}) copy-start(bf16[128,1024]{1,0:T(8,128)(2,1)S(1)} %collective-permute-done.3.refs_3_) | copy-start | bytes 786436
  63.7 10.1 %collective-permute-start.5 = (bf16[128,1024]{1,0:T(8,128)(2,1)S(1)}, bf16[128,1024]{1,0:T(8,128)(2,1)S(1)}, u32[]{:S(2)}, u32[]{:S(2)}) collective-permute-start(bf16[128,1024]{1,0:T(8,128)(2,1)S(1)} %collective-permute-done.3.refs_3_), channel_id=1, source_target_pairs={{0,16},{16,32},{32,48},{48,64},{64,80},{80,96},{96,112},{112,0},{1... | collective-permute-start | bytes 786440 | tf_op jit(solution)/shard_map/ppermute | solution.py:117
  66.0 20.9 %copy-start.10 = (bf16[128,1024]{1,0:T(8,128)(2,1)}, bf16[128,1024]{1,0:T(8,128)(2,1)S(1)}, u32[]{:S(2)}) copy-start(bf16[128,1024]{1,0:T(8,128)(2,1)S(1)} %collective-permute-done.4.refs_4_) | copy-start | bytes 786436
  66.0 11.4 %collective-permute-start.6 = (bf16[128,1024]{1,0:T(8,128)(2,1)S(1)}, bf16[128,1024]{1,0:T(8,128)(2,1)S(1)}, u32[]{:S(2)}, u32[]{:S(2)}) collective-permute-start(bf16[128,1024]{1,0:T(8,128)(2,1)S(1)} %collective-permute-done.4.refs_4_), channel_id=1, source_target_pairs={{0,112},{16,0},{32,16},{48,32},{64,48},{80,64},{96,80},{112,96},{1... | collective-permute-start | bytes 786440 | tf_op jit(solution)/shard_map/ppermute | solution.py:118
  73.8 13.1 %copy-start.5 = (bf16[128,1024]{1,0:T(8,128)(2,1)}, bf16[128,1024]{1,0:T(8,128)(2,1)S(1)}, u32[]{:S(2)}) copy-start(bf16[128,1024]{1,0:T(8,128)(2,1)S(1)} %collective-permute-done.5.refs_5_) | copy-start | bytes 786436
  74.5 7.1 %collective-permute-start.7 = (bf16[64,1024]{1,0:T(8,128)(2,1)}, bf16[64,1024]{1,0:T(8,128)(2,1)S(1)}, u32[]{:S(2)}, u32[]{:S(2)}) collective-permute-start(bf16[64,1024]{1,0:T(8,128)(2,1)} %slice.215), channel_id=1, source_target_pairs={{0,16},{16,32},{32,48},{48,64},{64,80},{80,96},{96,112},{112,0},{1... | collective-permute-start | bytes 393224 | tf_op jit(solution)/shard_map/ppermute | solution.py:123
  77.4 9.5 %copy-start.6 = (bf16[128,1024]{1,0:T(8,128)(2,1)}, bf16[128,1024]{1,0:T(8,128)(2,1)S(1)}, u32[]{:S(2)}) copy-start(bf16[128,1024]{1,0:T(8,128)(2,1)S(1)} %collective-permute-done.6.refs_6_) | copy-start | bytes 786436
  78.2 8.7 %collective-permute-start.8 = (bf16[64,1024]{1,0:T(8,128)(2,1)}, bf16[64,1024]{1,0:T(8,128)(2,1)S(1)}, u32[]{:S(2)}, u32[]{:S(2)}) collective-permute-start(bf16[64,1024]{1,0:T(8,128)(2,1)} %slice.216), channel_id=1, source_target_pairs={{0,112},{16,0},{32,16},{48,32},{64,48},{80,64},{96,80},{112,96},{1... | collective-permute-start | bytes 393224 | tf_op jit(solution)/shard_map/ppermute | solution.py:124
  81.5 5.4 %copy-start.11 = (bf16[64,1024]{1,0:T(8,128)(2,1)}, bf16[64,1024]{1,0:T(8,128)(2,1)S(1)}, u32[]{:S(2)}) copy-start(bf16[64,1024]{1,0:T(8,128)(2,1)S(1)} %collective-permute-done.7.refs_7_) | copy-start | bytes 393220
  86.9 0.6 copy-start.12
  91.7 6.4 %collective-permute-start.9 = (bf16[2,256,1024]{2,1,0:T(8,128)(2,1)}, bf16[2,256,1024]{2,1,0:T(8,128)(2,1)S(1)}, u32[]{:S(2)}, u32[]{:S(2)}) collective-permute-start(bf16[2,256,1024]{2,1,0:T(8,128)(2,1)} %pack_teacher.1), channel_id=1, source_target_pairs={{0,1},{1,0},{2,3},{3,2},{4,5},{5,4},{6,7},{7,6},{8,9},{9,8},{10,11... | collective-permute-start | bytes 3145736 | tf_op jit(solution)/shard_map/ppermute | solution.py:262
  94.3 3.9 %copy-start.1 = (bf16[1,4096,512]{2,1,0:T(8,128)(2,1)S(1)}, bf16[1,4096,512]{2,1,0:T(8,128)(2,1)}, u32[]{:S(2)}) copy-start(bf16[1,4096,512]{2,1,0:T(8,128)(2,1)} %param.13) | copy-start | bytes 12582916
  98.1 22.7 %copy-start.15 = (s32[512]{0:T(512)S(1)}, s32[512]{0:T(512)}, u32[]{:S(2)}) copy-start(s32[512]{0:T(512)} %param.18) | copy-start | bytes 6148
  99.1 25.7 %copy-start.13 = (f32[256]{0:T(256)}, f32[256]{0:T(256)S(1)}, u32[]{:S(2)}) copy-start(f32[256]{0:T(256)S(1)} %get-tuple-element.86) | copy-start | bytes 3076
  100.3 24.5 %all-to-all-start.3 = ((f32[128,1,640]{2,1,0:T(1,128)}), f32[128,1,640]{2,1,0:T(1,128)S(1)}, u32[]{:S(2)}, u32[]{:S(2)}) async-start(f32[128,1,640]{2,1,0:T(1,128)} %broadcast_in_dim.208), calls=%async_computation.3 | async-start | bytes 655360 | tf_op jit(solution)/shard_map/all_to_all | solution.py:19
  110.4 22.0 %collective-permute-start.10 = (bf16[448,512]{1,0:T(8,128)(2,1)S(1)}, bf16[448,512]{1,0:T(8,128)(2,1)S(1)}, u32[]{:S(2)}, u32[]{:S(2)}) collective-permute-start(bf16[448,512]{1,0:T(8,128)(2,1)S(1)} %pad_maximum_fusion.1), channel_id=1, source_target_pairs={{0,128},{128,256},{256,384},{384,0},{1,129},{129,257},{257,385},{3... | collective-permute-start | bytes 1376264 | tf_op jit(solution)/shard_map/ppermute | solution.py:269
  113.8 18.6 %collective-permute-start.11 = (bf16[448,512]{1,0:T(8,128)(2,1)S(1)}, bf16[448,512]{1,0:T(8,128)(2,1)S(1)}, u32[]{:S(2)}, u32[]{:S(2)}) collective-permute-start(bf16[448,512]{1,0:T(8,128)(2,1)S(1)} %pad_maximum_fusion.1), channel_id=1, source_target_pairs={{0,256},{128,384},{256,0},{384,128},{1,257},{129,385},{257,1},{385... | collective-permute-start | bytes 1376264 | tf_op jit(solution)/shard_map/ppermute | solution.py:269
  116.6 22.7 %collective-permute-start.12 = (bf16[448,512]{1,0:T(8,128)(2,1)S(1)}, bf16[448,512]{1,0:T(8,128)(2,1)S(1)}, u32[]{:S(2)}, u32[]{:S(2)}) collective-permute-start(bf16[448,512]{1,0:T(8,128)(2,1)S(1)} %pad_maximum_fusion.1), channel_id=1, source_target_pairs={{0,384},{128,0},{256,128},{384,256},{1,385},{129,1},{257,129},{385... | collective-permute-start | bytes 1376264 | tf_op jit(solution)/shard_map/ppermute | solution.py:269
  124.8 0.7 copy-start.2
  127.6 11.8 %all-to-all-start.4 = ((f32[4,1,384]{2,1,0:T(1,128)}), f32[4,1,384]{2,1,0:T(1,128)S(1)}, u32[]{:S(2)}, u32[]{:S(2)}) async-start(f32[4,1,384]{2,1,0:T(1,128)} %combine.1), calls=%async_computation.4 | async-start | bytes 12288 | tf_op jit(solution)/shard_map/all_to_all | solution.py:273
  142.9 22.4 %copy-start.16 = (s32[1,4]{1,0:T(1,128)S(1)}, s32[1,4]{1,0:T(1,128)}, u32[]{:S(2)}) copy-start(s32[1,4]{1,0:T(1,128)} %refs_0_.1) | copy-start | bytes 52
  144.6 3.9 %collective-permute-start.13 = (f32[64,2176]{1,0:T(8,128)S(1)}, f32[64,2176]{1,0:T(8,128)S(1)}, u32[]{:S(2)}, u32[]{:S(2)}) collective-permute-start(f32[64,2176]{1,0:T(8,128)S(1)} %constant_dynamic-update-slice_fusion.1), channel_id=1, source_target_pairs={{0,1},{1,0},{2,3},{3,2},{4,5},{5,4},{6,7},{7,6},{8,9},{9,8},{10,11... | collective-permute-start | bytes 1671176 | tf_op jit(solution)/shard_map/ppermute | solution.py:310
  149.9 33.5 %all-to-all-start.5 = ((f32[64,1,2176]{2,1,0:T(1,128)}), f32[64,1,2176]{2,1,0:T(1,128)S(1)}, u32[]{:S(2)}, u32[]{:S(2)}) async-start(f32[64,1,2176]{2,1,0:T(1,128)} %copy.32), calls=%async_computation.5 | async-start | bytes 1114112 | tf_op jit(solution)/shard_map/all_to_all | solution.py:311

commit v8 on v6

--- a/solution.py
+++ b/solution.py
@@ -13,6 +13,9 @@
 OWNERS = ("y", "z", "core")
 BF16 = jnp.bfloat16
 F32 = jnp.float32
+F16 = jnp.float16
+GRAD_STEP = 2.0**11
+LOSS_STEP = 2.0**-7
 
 
 def spread(block, axes, size):
@@ -270,23 +273,34 @@
     loss = jnp.where(owner == 0, jnp.sum(log_total), 0.0) - jnp.sum(mixture * student_logits)
     slope = (LOSS_SCALE * (jnp.exp(student_logits - log_total[:, None]) - mixture)).astype(BF16)
 
+    half = width // 2
+
     def term(which_core):
         chosen = jnp.take(places.reshape(chips, cores, cap), which_core, axis=1)
-        parts = []
-        for slot in range(cap):
-            unpack = (chosen[:, slot : slot + 1] == packed_ids[None, :]).astype(BF16)
+        result = 0.0
+        for side in range(2):
+            at = jnp.where(sides[None, :, None] == side, chosen[:, None, :], -1).reshape(-1, 1)
+            unpack = (at == packed_ids[None, :]).astype(BF16)
             rows = jnp.dot(unpack, slope, preferred_element_type=F32).astype(BF16)
-            parts.append(
-                lax.dot_general(
-                    rows, student_head, (((1,), (1,)), ((), ())), preferred_element_type=F32
-                )
+            result = result + lax.dot_general(
+                rows,
+                student_head[side * half : (side + 1) * half],
+                (((1,), (1,)), ((), ())),
+                preferred_element_type=F32,
             )
-        return jnp.concatenate(parts + [jnp.full((chips, 128), loss, F32)], axis=1)
+        return jnp.concatenate([result, jnp.full((8, half), loss, F32)], axis=0)
 
     grads = term(core) + lax.ppermute(term(1 - core), "core", swap)
-    owned = jnp.sum(lax.all_to_all(grads[:, None, :], CHIPS, 0, 0, tiled=True), axis=0)
-    slot_grad = owned[0, : cap * width].reshape(cap, width)
-    mean_loss = owned[0, cap * width] / jnp.sum(counts).astype(F32)
+    chip_loss = grads[-1, 0] * LOSS_STEP
+    high = lax.reduce_precision(chip_loss, 5, 10)
+    middle = lax.reduce_precision(chip_loss - high, 5, 10)
+    parts = jnp.stack([high, middle, (chip_loss - high) - middle]).astype(F16)
+    grads = (grads[:-8] * GRAD_STEP).astype(F16).reshape(chips, 2 * cap, half)
+    parts = jnp.broadcast_to(jnp.pad(parts, (0, 125)), (chips, 2 * cap, 128))
+    owned = lax.all_to_all(jnp.concatenate([grads, parts], axis=2), CHIPS, 0, 0, tiled=True)
+    owned = jnp.sum(owned.astype(F32), axis=0)
+    slot_grad = jnp.concatenate([owned[:cap, :half], owned[cap:, :half]], axis=1) / GRAD_STEP
+    mean_loss = jnp.sum(owned[0, half : half + 3]) / LOSS_STEP / jnp.sum(counts).astype(F32)
     live_here = slots < lax.dynamic_index_in_dim(counts, owner, keepdims=False)
     placed = (
         (jnp.arange(window, dtype=jnp.int32)[:, None] == slot_ids[None, :]) & live_here[None, :]

time: 182 us -> 183 us (level)
  the two profiles are of different devices: /device:TPU:18 before, /device:TPU:1 now
where the time goes in v8:
time: 183 us; the launch traced here: 180 us
  starting transfers between devices  49.7 us (27%)
  blocking collectives  37.3 us (20%)
  waiting for transfers between devices  34.5 us (19%)
  between operations  22.7 us (12%)
  Pallas kernels  10.2 us (6%)
  other arithmetic  9.5 us (5%)
  matrix products  9.36 us (5%)
  local copies, waits for them, and re-layouts  6.35 us (3%)
    all_to_all x1, blocking collectives, on_device(): group_rows = lax.all_to_all(sent, ('z', 'core'), 0, 0, tiled=True)  24.2 us
    all_to_all x2, waiting for transfers between devices, spread(): lax.all_to_all(jnp.broadcast_to(block[None], (size,) + block.shape), axes...  17.2 us
    all_to_all x2, starting transfers between devices, spread(): lax.all_to_all(jnp.broadcast_to(block[None], (size,) + block.shape), axes...  13.5 us
    all_to_all x1, blocking collectives, on_device(): lax.all_to_all(partial_logits.reshape(members, chunk, vocab), 'member', 0...  13.1 us
    all_to_all x1, waiting for transfers between devices, on_device(): lax.all_to_all(jnp.concatenate([grads, parts], axis=2), CHIPS, 0, 0, tile...  12.3 us
    all_to_all x1, starting transfers between devices, on_device(): lax.all_to_all(jnp.concatenate([grads, parts], axis=2), CHIPS, 0, 0, tile...  11.8 us
    ppermute x3, starting transfers between devices, on_device(): lax.ppermute(shared, 'member', [(i, (i + step) % members) for i in range(...  10.5 us
    dot_general x8, matrix products, both_halves(): jnp.dot(values[side], lax.dynamic_slice_in_dim(weights, first + side * pa...  7.4 us
  transfers between devices with their start and end apart: 11, of which 6 were waited for; matrix products, arithmetic and copies ran while one was open for 8% of the time, Pallas kernels for 2%

profile of v8, /device:TPU:1, one launch (start us, length us, event | category | flops | bytes accessed | tf_op | source)
XLA Modules:
  0.0 179.6 jit_solution(1763430331913465680)
XLA Ops:
  7.2 2.0 %own_rows.1 = bf16[128,1152]{1,0:T(8,128)(2,1)} custom-call(s32[1,4]{1,0:T(1,128)} %refs_0_.1, bf16[1,16,4096]{2,1,0:T(8,128)(2,1)} %refs_1_.1, f32[1,4096]{1,0:T(1,128)} %refs_2_.1, bf16[16,512]{1,0:T(8,128)(2,1)} %refs_3_.1), custom_call_target="tpu_custom_call" | custom-call | tf_op jit(solution)/shard_map/own_rows/pallas_call | solution.py:60
  9.2 24.2 %all_to_all.30 = bf16[16,8,1152]{2,1,0:T(8,128)(2,1)S(1)} all-to-all(bf16[16,8,1152]{2,1,0:T(8,128)(2,1)} %bitcast.65), channel_id=1, replica_groups=mesh['member'=4,'y'=8,'z'=8,'core'=2] {'z','core'}, dimensions={0} | all-to-all | bytes 589824 | tf_op jit(solution)/shard_map/all_to_all | solution.py:189
  33.4 0.7 slice.192
  34.2 0.8 select_reduce_fusion.1
  34.9 0.8 broadcast_in_dim.212
  35.7 6.8 %all-to-all-start.1 = ((bf16[8,128,128]{2,1,0:T(8,128)(2,1)}), bf16[8,128,128]{2,1,0:T(8,128)(2,1)S(1)}, u32[]{:S(2)}, u32[]{:S(2)}) async-start(bf16[8,128,128]{2,1,0:T(8,128)(2,1)} %broadcast_in_dim.212), calls=%async_computation.1 | async-start | bytes 524288 | tf_op jit(solution)/shard_map/all_to_all | solution.py:22
  42.5 0.8 add_select_fusion
  43.8 0.6 pad_add_fusion.1.places_ref
  44.5 12.7 %all-to-all-done.1 = bf16[8,128,128]{2,1,0:T(8,128)(2,1)S(1)} async-done(((bf16[8,128,128]{2,1,0:T(8,128)(2,1)}), bf16[8,128,128]{2,1,0:T(8,128)(2,1)S(1)}, u32[]{:S(2)}, u32[]{:S(2)}) %all-to-all-start.1) | async-done | bytes 262176 | tf_op jit(solution)/shard_map/all_to_all | solution.py:22
  57.1 0.7 copy-done.3
  57.8 2.4 %pack_student.1 = (bf16[2,256,128]{2,1,0:T(8,128)(2,1)}, bf16[2,256,1024]{2,1,0:T(8,128)(2,1)}) custom-call(s32[2,1024]{1,0:T(2,128)} %pad_add_fusion.1.places_ref, bf16[1024,128]{1,0:T(8,128)(2,1)} %bitcast.66), custom_call_target="tpu_custom_call" | custom-call | tf_op jit(solution)/shard_map/pack_student/pallas_call | solution.py:82
  60.2 2.4 %collective-permute-start = (bf16[2,256,128]{2,1,0:T(8,128)(2,1)}, bf16[2,256,128]{2,1,0:T(8,128)(2,1)S(1)}, u32[]{:S(2)}, u32[]{:S(2)}) collective-permute-start(bf16[2,256,128]{2,1,0:T(8,128)(2,1)} %get-tuple-element.14), channel_id=1, source_target_pairs={{0,1},{1,0},{2,3},{3,2},{4,5},{5,4},{6,7},{7,6},{8,9},{9,8},{10,11... | collective-permute-start | bytes 393224 | tf_op jit(solution)/shard_map/ppermute | solution.py:227
  62.6 1.2 fusion.39
  63.8 1.1 convolution_add_fusion.3
  65.3 13.1 %all_to_all.31 = f32[4,64,512]{2,1,0:T(8,128)S(1)} all-to-all(f32[4,64,512]{2,1,0:T(8,128)S(1)} %bitcast.62), channel_id=1, replica_groups=mesh['member'=4,'y'=8,'z'=8,'core'=2] {'member'}, dimensions={0} | all-to-all | bytes 1048576 | tf_op jit(solution)/shard_map/all_to_all | solution.py:229
  78.8 3.8 %pack_teacher.1 = bf16[2,256,1024]{2,1,0:T(8,128)(2,1)} custom-call(bf16[2,256,1024]{2,1,0:T(8,128)(2,1)} %get-tuple-element.13.one_ref, bf16[1024,1024]{1,0:T(8,128)(2,1)} %all-gather.2.cloned.1.call-done.rows_ref), custom_call_target="tpu_custom_call" | custom-call | tf_op jit(solution)/shard_map/pack_teacher/pallas_call | solution.py:103
  82.6 3.1 %collective-permute-start.1 = (bf16[2,256,1024]{2,1,0:T(8,128)(2,1)}, bf16[2,256,1024]{2,1,0:T(8,128)(2,1)S(1)}, u32[]{:S(2)}, u32[]{:S(2)}) collective-permute-start(bf16[2,256,1024]{2,1,0:T(8,128)(2,1)} %pack_teacher.1), channel_id=1, source_target_pairs={{0,1},{1,0},{2,3},{3,2},{4,5},{5,4},{6,7},{7,6},{8,9},{9,8},{10,11... | collective-permute-start | bytes 3145736 | tf_op jit(solution)/shard_map/ppermute | solution.py:241
  86.4 2.0 %fusion.12 = f32[256,512]{1,0:T(8,128)S(1)} fusion(bf16[1,4096,512]{2,1,0:T(8,128)(2,1)} %param.12, s32[]{:T(128)S(6)} %select_n.277, bf16[2,256,1024]{2,1,0:T(8,128)(2,1)} %pack_teacher.1), kind=kOutput, calls=%fused_computation.20 | convolution fusion | flops 268435456 | bytes 2097156 | tf_op jit(solution)/shard_map/dot_general | solution.py:217
  88.4 1.8 %convolution_add_fusion.1 = f32[256,512]{1,0:T(8,128)S(1)} fusion(f32[256,512]{1,0:T(8,128)S(1)} %fusion.12, bf16[1,4096,512]{2,1,0:T(8,128)(2,1)} %param.12, s32[]{:T(128)S(6)} %select_n.278, bf16[2,256,1024]{2,1,0:T(8,128)(2,1)} %pack_teacher.1), kind=kOutput, calls=%fused_computation.5 | convolution fusion | flops 268566528 | bytes 2621444 | tf_op jit(solution)/shard_map/dot_general | solution.py:217
  90.2 0.4 fusion.8
  90.7 0.5 fusion.56
  91.5 0.9 broadcast_in_dim.213
  92.4 6.7 %all-to-all-start.3 = ((f32[128,1,640]{2,1,0:T(1,128)}), f32[128,1,640]{2,1,0:T(1,128)S(1)}, u32[]{:S(2)}, u32[]{:S(2)}) async-start(f32[128,1,640]{2,1,0:T(1,128)} %broadcast_in_dim.213), calls=%async_computation.3 | async-start | bytes 655360 | tf_op jit(solution)/shard_map/all_to_all | solution.py:22
  99.4 3.1 %collective-permute-start.2 = (bf16[448,512]{1,0:T(8,128)(2,1)S(1)}, bf16[448,512]{1,0:T(8,128)(2,1)S(1)}, u32[]{:S(2)}, u32[]{:S(2)}) collective-permute-start(bf16[448,512]{1,0:T(8,128)(2,1)S(1)} %pad_maximum_fusion.1), channel_id=1, source_target_pairs={{0,128},{128,256},{256,384},{384,0},{1,129},{129,257},{257,385},{3... | collective-permute-start | bytes 1376264 | tf_op jit(solution)/shard_map/ppermute | solution.py:248
  102.5 4.3 %collective-permute-start.3 = (bf16[448,512]{1,0:T(8,128)(2,1)S(1)}, bf16[448,512]{1,0:T(8,128)(2,1)S(1)}, u32[]{:S(2)}, u32[]{:S(2)}) collective-permute-start(bf16[448,512]{1,0:T(8,128)(2,1)S(1)} %pad_maximum_fusion.1), channel_id=1, source_target_pairs={{0,256},{128,384},{256,0},{384,128},{1,257},{129,385},{257,1},{385... | collective-permute-start | bytes 1376264 | tf_op jit(solution)/shard_map/ppermute | solution.py:248
  106.8 3.1 %collective-permute-start.4 = (bf16[448,512]{1,0:T(8,128)(2,1)S(1)}, bf16[448,512]{1,0:T(8,128)(2,1)S(1)}, u32[]{:S(2)}, u32[]{:S(2)}) collective-permute-start(bf16[448,512]{1,0:T(8,128)(2,1)S(1)} %pad_maximum_fusion.1), channel_id=1, source_target_pairs={{0,384},{128,0},{256,128},{384,256},{1,385},{129,1},{257,129},{385... | collective-permute-start | bytes 1376264 | tf_op jit(solution)/shard_map/ppermute | solution.py:248
  110.2 4.5 %all-to-all-done.3.every_ref = f32[128,1,640]{2,1,0:T(1,128)S(1)} async-done(((f32[128,1,640]{2,1,0:T(1,128)}), f32[128,1,640]{2,1,0:T(1,128)S(1)}, u32[]{:S(2)}, u32[]{:S(2)}) %all-to-all-start.3) | async-done | bytes 327712 | tf_op jit(solution)/shard_map/all_to_all | solution.py:22
  114.7 0.7 copy-done.2
  115.4 2.0 %combine.1 = f32[4,1,384]{2,1,0:T(1,128)} custom-call(f32[128,1,640]{2,1,0:T(1,128)} %copy-done.2, f32[1,256]{1,0:T(1,128)} %bitcast.71), custom_call_target="tpu_custom_call" | custom-call | tf_op jit(solution)/shard_map/combine/pallas_call | solution.py:138
  117.4 4.0 %all-to-all-start.4 = ((f32[4,1,384]{2,1,0:T(1,128)}), f32[4,1,384]{2,1,0:T(1,128)S(1)}, u32[]{:S(2)}, u32[]{:S(2)}) async-start(f32[4,1,384]{2,1,0:T(1,128)} %combine.1), calls=%async_computation.4 | async-start | bytes 12288 | tf_op jit(solution)/shard_map/all_to_all | solution.py:252
  121.7 2.7 %collective-permute-done.3 = bf16[448,512]{1,0:T(8,128)(2,1)S(1)} collective-permute-done((bf16[448,512]{1,0:T(8,128)(2,1)S(1)}, bf16[448,512]{1,0:T(8,128)(2,1)S(1)}, u32[]{:S(2)}, u32[]{:S(2)}) %collective-permute-start.3) | collective-permute-done | bytes 458784 | tf_op jit(solution)/shard_map/ppermute | solution.py:248
  124.4 1.9 %collective-permute-done.4 = bf16[448,512]{1,0:T(8,128)(2,1)S(1)} collective-permute-done((bf16[448,512]{1,0:T(8,128)(2,1)S(1)}, bf16[448,512]{1,0:T(8,128)(2,1)S(1)}, u32[]{:S(2)}, u32[]{:S(2)}) %collective-permute-start.4) | collective-permute-done | bytes 458784 | tf_op jit(solution)/shard_map/ppermute | solution.py:248
  126.6 0.6 slice_reduce_fusion.1
  127.4 1.0 multiply_reduce_fusion
  129.9 0.5 fusion.3
  130.4 0.5 fusion.6
  131.0 4.5 %collective-permute-start.5 = (f32[520,256]{1,0:T(8,128)S(1)}, f32[520,256]{1,0:T(8,128)S(1)}, u32[]{:S(2)}, u32[]{:S(2)}) collective-permute-start(f32[520,256]{1,0:T(8,128)S(1)} %concatenate.29), channel_id=1, source_target_pairs={{0,1},{1,0},{2,3},{3,2},{4,5},{5,4},{6,7},{7,6},{8,9},{9,8},{10,11... | collective-permute-start | bytes 1597448 | tf_op jit(solution)/shard_map/ppermute | solution.py:293
  135.7 0.5 fusion.1
  136.2 0.5 fusion.7
  137.0 0.5 slice.214
  142.0 0.8 pad_maximum_fusion.2
  142.8 11.8 %all-to-all-start.5 = ((f16[64,8,384]{2,1,0:T(8,128)(2,1)}), f16[64,8,384]{2,1,0:T(8,128)(2,1)S(1)}, u32[]{:S(2)}, u32[]{:S(2)}) async-start(f16[64,8,384]{2,1,0:T(8,128)(2,1)} %pad_maximum_fusion.2), calls=%async_computation.5 | async-start | bytes 786432 | tf_op jit(solution)/shard_map/all_to_all | solution.py:300
  154.6 0.6 reduce_sum.148
  155.3 0.6 dynamic_slice.48
  156.5 0.7 iota_compare_fusion.16
  157.2 12.3 %all-to-all-done.5 = f16[64,8,384]{2,1,0:T(8,128)(2,1)S(1)} async-done(((f16[64,8,384]{2,1,0:T(8,128)(2,1)}), f16[64,8,384]{2,1,0:T(8,128)(2,1)S(1)}, u32[]{:S(2)}, u32[]{:S(2)}) %all-to-all-start.5) | async-done | bytes 393248 | tf_op jit(solution)/shard_map/all_to_all | solution.py:300
  169.7 0.6 slice_reduce_fusion
  170.3 0.7 multiply_reduce_fusion.1
  (68 shorter events, 4.6 us)
Async XLA Ops:
  7.2 56.6 %copy-start.1 = (bf16[512,512]{1,0:T(8,128)(2,1)S(1)}, bf16[512,512]{1,0:T(8,128)(2,1)}, u32[]{:S(2)}) copy-start(bf16[512,512]{1,0:T(8,128)(2,1)} %param.14) | copy-start | bytes 1572868
  7.2 71.6 %all-gather.2.cloned.1.call-start = ((), (), s32[]{:S(2)}) async-start(), calls=%async_computation.6 | async-start | bytes 2359296 | tf_op jit(solution)/shard_map/all_gather | solution.py:191
  35.7 21.4 %all-to-all-start.1 = ((bf16[8,128,128]{2,1,0:T(8,128)(2,1)}), bf16[8,128,128]{2,1,0:T(8,128)(2,1)S(1)}, u32[]{:S(2)}, u32[]{:S(2)}) async-start(bf16[8,128,128]{2,1,0:T(8,128)(2,1)} %broadcast_in_dim.212), calls=%async_computation.1 | async-start | bytes 524288 | tf_op jit(solution)/shard_map/all_to_all | solution.py:22
  57.1 0.7 copy-start.3
  60.2 4.6 %collective-permute-start = (bf16[2,256,128]{2,1,0:T(8,128)(2,1)}, bf16[2,256,128]{2,1,0:T(8,128)(2,1)S(1)}, u32[]{:S(2)}, u32[]{:S(2)}) collective-permute-start(bf16[2,256,128]{2,1,0:T(8,128)(2,1)} %get-tuple-element.14), channel_id=1, source_target_pairs={{0,1},{1,0},{2,3},{3,2},{4,5},{5,4},{6,7},{7,6},{8,9},{9,8},{10,11... | collective-permute-start | bytes 393224 | tf_op jit(solution)/shard_map/ppermute | solution.py:227
  65.1 21.0 %copy-start.5 = (s32[128]{0:T(128)S(1)}, s32[128]{0:T(128)}, u32[]{:S(2)}) copy-start(s32[128]{0:T(128)} %param.16) | copy-start | bytes 1540
  65.1 21.2 %copy-start.6 = (s32[512]{0:T(512)S(1)}, s32[512]{0:T(512)}, u32[]{:S(2)}) copy-start(s32[512]{0:T(512)} %param.17) | copy-start | bytes 6148
  82.6 7.6 %collective-permute-start.1 = (bf16[2,256,1024]{2,1,0:T(8,128)(2,1)}, bf16[2,256,1024]{2,1,0:T(8,128)(2,1)S(1)}, u32[]{:S(2)}, u32[]{:S(2)}) collective-permute-start(bf16[2,256,1024]{2,1,0:T(8,128)(2,1)} %pack_teacher.1), channel_id=1, source_target_pairs={{0,1},{1,0},{2,3},{3,2},{4,5},{5,4},{6,7},{7,6},{8,9},{9,8},{10,11... | collective-permute-start | bytes 3145736 | tf_op jit(solution)/shard_map/ppermute | solution.py:241
  86.2 4.0 %copy-start = (bf16[1,4096,512]{2,1,0:T(8,128)(2,1)S(1)}, bf16[1,4096,512]{2,1,0:T(8,128)(2,1)}, u32[]{:S(2)}) copy-start(bf16[1,4096,512]{2,1,0:T(8,128)(2,1)} %param.12) | copy-start | bytes 12582916
  91.2 23.5 %copy-start.4 = (f32[256]{0:T(256)}, f32[256]{0:T(256)S(1)}, u32[]{:S(2)}) copy-start(f32[256]{0:T(256)S(1)} %get-tuple-element.64) | copy-start | bytes 3076
  92.4 22.3 %all-to-all-start.3 = ((f32[128,1,640]{2,1,0:T(1,128)}), f32[128,1,640]{2,1,0:T(1,128)S(1)}, u32[]{:S(2)}, u32[]{:S(2)}) async-start(f32[128,1,640]{2,1,0:T(1,128)} %broadcast_in_dim.213), calls=%async_computation.3 | async-start | bytes 655360 | tf_op jit(solution)/shard_map/all_to_all | solution.py:22
  99.4 22.3 %collective-permute-start.2 = (bf16[448,512]{1,0:T(8,128)(2,1)S(1)}, bf16[448,512]{1,0:T(8,128)(2,1)S(1)}, u32[]{:S(2)}, u32[]{:S(2)}) collective-permute-start(bf16[448,512]{1,0:T(8,128)(2,1)S(1)} %pad_maximum_fusion.1), channel_id=1, source_target_pairs={{0,128},{128,256},{256,384},{384,0},{1,129},{129,257},{257,385},{3... | collective-permute-start | bytes 1376264 | tf_op jit(solution)/shard_map/ppermute | solution.py:248
  102.5 21.9 %collective-permute-start.3 = (bf16[448,512]{1,0:T(8,128)(2,1)S(1)}, bf16[448,512]{1,0:T(8,128)(2,1)S(1)}, u32[]{:S(2)}, u32[]{:S(2)}) collective-permute-start(bf16[448,512]{1,0:T(8,128)(2,1)S(1)} %pad_maximum_fusion.1), channel_id=1, source_target_pairs={{0,256},{128,384},{256,0},{384,128},{1,257},{129,385},{257,1},{385... | collective-permute-start | bytes 1376264 | tf_op jit(solution)/shard_map/ppermute | solution.py:248
  106.8 19.5 %collective-permute-start.4 = (bf16[448,512]{1,0:T(8,128)(2,1)S(1)}, bf16[448,512]{1,0:T(8,128)(2,1)S(1)}, u32[]{:S(2)}, u32[]{:S(2)}) collective-permute-start(bf16[448,512]{1,0:T(8,128)(2,1)S(1)} %pad_maximum_fusion.1), channel_id=1, source_target_pairs={{0,384},{128,0},{256,128},{384,256},{1,385},{129,1},{257,129},{385... | collective-permute-start | bytes 1376264 | tf_op jit(solution)/shard_map/ppermute | solution.py:248
  114.7 0.7 copy-start.2
  117.4 8.9 %all-to-all-start.4 = ((f32[4,1,384]{2,1,0:T(1,128)}), f32[4,1,384]{2,1,0:T(1,128)S(1)}, u32[]{:S(2)}, u32[]{:S(2)}) async-start(f32[4,1,384]{2,1,0:T(1,128)} %combine.1), calls=%async_computation.4 | async-start | bytes 12288 | tf_op jit(solution)/shard_map/all_to_all | solution.py:252
  130.9 26.2 %copy-start.7 = (s32[1,4]{1,0:T(1,128)S(1)}, s32[1,4]{1,0:T(1,128)}, u32[]{:S(2)}) copy-start(s32[1,4]{1,0:T(1,128)} %refs_0_.1) | copy-start | bytes 52
  131.0 6.0 %collective-permute-start.5 = (f32[520,256]{1,0:T(8,128)S(1)}, f32[520,256]{1,0:T(8,128)S(1)}, u32[]{:S(2)}, u32[]{:S(2)}) collective-permute-start(f32[520,256]{1,0:T(8,128)S(1)} %concatenate.29), channel_id=1, source_target_pairs={{0,1},{1,0},{2,3},{3,2},{4,5},{5,4},{6,7},{7,6},{8,9},{9,8},{10,11... | collective-permute-start | bytes 1597448 | tf_op jit(solution)/shard_map/ppermute | solution.py:293
  142.8 26.7 %all-to-all-start.5 = ((f16[64,8,384]{2,1,0:T(8,128)(2,1)}), f16[64,8,384]{2,1,0:T(8,128)(2,1)S(1)}, u32[]{:S(2)}, u32[]{:S(2)}) async-start(f16[64,8,384]{2,1,0:T(8,128)(2,1)} %pad_maximum_fusion.2), calls=%async_computation.5 | async-start | bytes 786432 | tf_op jit(solution)/shard_map/all_to_all | solution.py:300
Sparse Core Ops, SparseCore 0:
  34.3 40.4 all-gather.1

commit v9 on v8

--- a/solution.py
+++ b/solution.py
@@ -85,6 +85,8 @@
             jax.ShapeDtypeStruct((2, live, features), BF16),
             jax.ShapeDtypeStruct((2, live, total), BF16),
         ),
+        in_specs=[pl.BlockSpec(memory_space=pltpu.VMEM)] * 2,
+        out_specs=(pl.BlockSpec(memory_space=pltpu.VMEM),) * 2,
         name="pack_student",
     )(places, rows)
 
@@ -138,6 +140,8 @@
     return pl.pallas_call(
         combine_kernel,
         out_shape=jax.ShapeDtypeStruct((copies, 1, live + 128), F32),
+        in_specs=[pl.BlockSpec(memory_space=pltpu.VMEM)] * 2,
+        out_specs=pl.BlockSpec(memory_space=pltpu.VMEM),
         name="combine",
     )(every, top[None])
 
@@ -291,16 +295,19 @@
         return jnp.concatenate([result, jnp.full((8, half), loss, F32)], axis=0)
 
     grads = term(core) + lax.ppermute(term(1 - core), "core", swap)
-    chip_loss = grads[-1, 0] * LOSS_STEP
+    chip_loss = grads[-8:] * LOSS_STEP
     high = lax.reduce_precision(chip_loss, 5, 10)
     middle = lax.reduce_precision(chip_loss - high, 5, 10)
-    parts = jnp.stack([high, middle, (chip_loss - high) - middle]).astype(F16)
+    low = (chip_loss - high) - middle
+    row = lax.broadcasted_iota(jnp.int32, chip_loss.shape, 0)
+    parts = jnp.where(row == 0, high, jnp.where(row == 1, middle, low)).astype(F16)
     grads = (grads[:-8] * GRAD_STEP).astype(F16).reshape(chips, 2 * cap, half)
-    parts = jnp.broadcast_to(jnp.pad(parts, (0, 125)), (chips, 2 * cap, 128))
-    owned = lax.all_to_all(jnp.concatenate([grads, parts], axis=2), CHIPS, 0, 0, tiled=True)
+    parts = jnp.broadcast_to(parts[None], (chips, 8, half))
+    owned = lax.all_to_all(jnp.concatenate([grads, parts], axis=1), CHIPS, 0, 0, tiled=True)
     owned = jnp.sum(owned.astype(F32), axis=0)
-    slot_grad = jnp.concatenate([owned[:cap, :half], owned[cap:, :half]], axis=1) / GRAD_STEP
-    mean_loss = jnp.sum(owned[0, half : half + 3]) / LOSS_STEP / jnp.sum(counts).astype(F32)
+    slot_grad = jnp.concatenate([owned[:cap], owned[cap : 2 * cap]], axis=1) / GRAD_STEP
+    mean_loss = jnp.sum(owned[2 * cap : 2 * cap + 3, 0]) / LOSS_STEP
+    mean_loss = mean_loss / jnp.sum(counts).astype(F32)
     live_here = slots < lax.dynamic_index_in_dim(counts, owner, keepdims=False)
     placed = (
         (jnp.arange(window, dtype=jnp.int32)[:, None] == slot_ids[None, :]) & live_here[None, :]

time: 183 us -> 181 us (0.989)
  the two profiles are of different devices: /device:TPU:1 before, /device:TPU:18 now
where the time goes in v9:
time: 181 us; the launch traced here: 180 us
  starting transfers between devices  50.6 us (28%)
  waiting for transfers between devices  40.1 us (22%)
  blocking collectives  35.5 us (20%)
  between operations  18.4 us (10%)
  Pallas kernels  10.2 us (6%)
  other arithmetic  9.62 us (5%)
  matrix products  9.35 us (5%)
  local copies, waits for them, and re-layouts  5.85 us (3%)
    all_to_all x1, blocking collectives, on_device(): group_rows = lax.all_to_all(sent, ('z', 'core'), 0, 0, tiled=True)  22.2 us
    all_to_all x1, waiting for transfers between devices, on_device(): lax.all_to_all(jnp.concatenate([grads, parts], axis=1), CHIPS, 0, 0, tile...  17.1 us
    all_to_all x2, starting transfers between devices, spread(): lax.all_to_all(jnp.broadcast_to(block[None], (size,) + block.shape), axes...  16.7 us
    all_to_all x2, waiting for transfers between devices, spread(): lax.all_to_all(jnp.broadcast_to(block[None], (size,) + block.shape), axes...  13.6 us
    all_to_all x1, blocking collectives, on_device(): lax.all_to_all(partial_logits.reshape(members, chunk, vocab), 'member', 0...  13.3 us
    all_to_all x1, starting transfers between devices, on_device(): lax.all_to_all(jnp.concatenate([grads, parts], axis=1), CHIPS, 0, 0, tile...  12.9 us
    ppermute x3, starting transfers between devices, on_device(): lax.ppermute(shared, 'member', [(i, (i + step) % members) for i in range(...  10.4 us
    dot_general x8, matrix products, both_halves(): jnp.dot(values[side], lax.dynamic_slice_in_dim(weights, first + side * pa...  7.4 us
  transfers between devices with their start and end apart: 11, of which 7 were waited for; matrix products, arithmetic and copies ran while one was open for 8% of the time, Pallas kernels for 2%

profile of v9, /device:TPU:18, one launch (start us, length us, event | category | flops | bytes accessed | tf_op | source)
XLA Modules:
  0.0 179.6 jit_solution(14329568824832143295)
XLA Ops:
  7.2 2.0 %own_rows.1 = bf16[128,1152]{1,0:T(8,128)(2,1)} custom-call(s32[1,4]{1,0:T(1,128)} %refs_0_.1, bf16[1,16,4096]{2,1,0:T(8,128)(2,1)} %refs_1_.1, f32[1,4096]{1,0:T(1,128)} %refs_2_.1, bf16[16,512]{1,0:T(8,128)(2,1)} %refs_3_.1), custom_call_target="tpu_custom_call" | custom-call | tf_op jit(solution)/shard_map/own_rows/pallas_call | solution.py:60
  9.2 22.2 %all_to_all.30 = bf16[16,8,1152]{2,1,0:T(8,128)(2,1)S(1)} all-to-all(bf16[16,8,1152]{2,1,0:T(8,128)(2,1)} %bitcast.61), channel_id=1, replica_groups=mesh['member'=4,'y'=8,'z'=8,'core'=2] {'z','core'}, dimensions={0} | all-to-all | bytes 589824 | tf_op jit(solution)/shard_map/all_to_all | solution.py:193
  31.4 0.7 slice.192
  32.2 0.8 select_reduce_fusion.1
  32.9 0.8 broadcast_in_dim.215
  33.7 7.4 %all-to-all-start.1 = ((bf16[8,128,128]{2,1,0:T(8,128)(2,1)}), bf16[8,128,128]{2,1,0:T(8,128)(2,1)S(1)}, u32[]{:S(2)}, u32[]{:S(2)}) async-start(bf16[8,128,128]{2,1,0:T(8,128)(2,1)} %broadcast_in_dim.215), calls=%async_computation.1 | async-start | bytes 524288 | tf_op jit(solution)/shard_map/all_to_all | solution.py:22
  41.1 0.8 add_select_fusion
  42.5 0.6 pad_add_fusion.1.places_ref
  43.1 10.0 %all-to-all-done.1 = bf16[8,128,128]{2,1,0:T(8,128)(2,1)S(1)} async-done(((bf16[8,128,128]{2,1,0:T(8,128)(2,1)}), bf16[8,128,128]{2,1,0:T(8,128)(2,1)S(1)}, u32[]{:S(2)}, u32[]{:S(2)}) %all-to-all-start.1) | async-done | bytes 262176 | tf_op jit(solution)/shard_map/all_to_all | solution.py:22
  53.1 0.7 copy-done.3
  53.8 2.4 %pack_student.1 = (bf16[2,256,128]{2,1,0:T(8,128)(2,1)}, bf16[2,256,1024]{2,1,0:T(8,128)(2,1)}) custom-call(s32[2,1024]{1,0:T(2,128)} %pad_add_fusion.1.places_ref, bf16[1024,128]{1,0:T(8,128)(2,1)} %bitcast.62), custom_call_target="tpu_custom_call" | custom-call | tf_op jit(solution)/shard_map/pack_student/pallas_call | solution.py:82
  56.2 1.9 %collective-permute-start = (bf16[2,256,128]{2,1,0:T(8,128)(2,1)}, bf16[2,256,128]{2,1,0:T(8,128)(2,1)S(1)}, u32[]{:S(2)}, u32[]{:S(2)}) collective-permute-start(bf16[2,256,128]{2,1,0:T(8,128)(2,1)} %get-tuple-element.14), channel_id=1, source_target_pairs={{0,1},{1,0},{2,3},{3,2},{4,5},{5,4},{6,7},{7,6},{8,9},{9,8},{10,11... | collective-permute-start | bytes 393224 | tf_op jit(solution)/shard_map/ppermute | solution.py:231
  58.1 1.2 fusion.39
  59.3 1.1 convolution_add_fusion.3
  60.8 13.3 %all_to_all.31 = f32[4,64,512]{2,1,0:T(8,128)S(1)} all-to-all(f32[4,64,512]{2,1,0:T(8,128)S(1)} %bitcast.58), channel_id=1, replica_groups=mesh['member'=4,'y'=8,'z'=8,'core'=2] {'member'}, dimensions={0} | all-to-all | bytes 1048576 | tf_op jit(solution)/shard_map/all_to_all | solution.py:233
  74.5 1.8 %all-gather.2.cloned.1.call-done.rows_ref = bf16[1024,1024]{1,0:T(8,128)(2,1)} async-done(((bf16[128,1024]{1,0:T(8,128)(2,1)}), bf16[1024,1024]{1,0:T(8,128)(2,1)}) %all-gather.2.cloned.1.call-update) | async-done | bytes 2097168 | tf_op jit(solution)/shard_map/all_gather | solution.py:195
  76.4 3.8 %pack_teacher.1 = bf16[2,256,1024]{2,1,0:T(8,128)(2,1)} custom-call(bf16[2,256,1024]{2,1,0:T(8,128)(2,1)} %get-tuple-element.13.one_ref, bf16[1024,1024]{1,0:T(8,128)(2,1)} %all-gather.2.cloned.1.call-done.rows_ref), custom_call_target="tpu_custom_call" | custom-call | tf_op jit(solution)/shard_map/pack_teacher/pallas_call | solution.py:105
  80.2 1.9 %collective-permute-start.1 = (bf16[2,256,1024]{2,1,0:T(8,128)(2,1)}, bf16[2,256,1024]{2,1,0:T(8,128)(2,1)S(1)}, u32[]{:S(2)}, u32[]{:S(2)}) collective-permute-start(bf16[2,256,1024]{2,1,0:T(8,128)(2,1)} %pack_teacher.1), channel_id=1, source_target_pairs={{0,1},{1,0},{2,3},{3,2},{4,5},{5,4},{6,7},{7,6},{8,9},{9,8},{10,11... | collective-permute-start | bytes 3145736 | tf_op jit(solution)/shard_map/ppermute | solution.py:245
  82.8 2.0 %fusion.12 = f32[256,512]{1,0:T(8,128)S(1)} fusion(bf16[1,4096,512]{2,1,0:T(8,128)(2,1)} %param.12, s32[]{:T(128)S(6)} %select_n.284, bf16[2,256,1024]{2,1,0:T(8,128)(2,1)} %pack_teacher.1), kind=kOutput, calls=%fused_computation.20 | convolution fusion | flops 268435456 | bytes 2097156 | tf_op jit(solution)/shard_map/dot_general | solution.py:221
  84.7 1.8 %convolution_add_fusion.1 = f32[256,512]{1,0:T(8,128)S(1)} fusion(f32[256,512]{1,0:T(8,128)S(1)} %fusion.12, bf16[1,4096,512]{2,1,0:T(8,128)(2,1)} %param.12, s32[]{:T(128)S(6)} %select_n.285, bf16[2,256,1024]{2,1,0:T(8,128)(2,1)} %pack_teacher.1), kind=kOutput, calls=%fused_computation.5 | convolution fusion | flops 268566528 | bytes 2621444 | tf_op jit(solution)/shard_map/dot_general | solution.py:221
  86.6 0.4 fusion.8
  87.0 0.5 fusion.57
  87.9 0.9 broadcast_in_dim.216
  88.8 9.3 %all-to-all-start.3 = ((f32[128,1,640]{2,1,0:T(1,128)}), f32[128,1,640]{2,1,0:T(1,128)S(1)}, u32[]{:S(2)}, u32[]{:S(2)}) async-start(f32[128,1,640]{2,1,0:T(1,128)} %broadcast_in_dim.216), calls=%async_computation.3 | async-start | bytes 655360 | tf_op jit(solution)/shard_map/all_to_all | solution.py:22
  98.3 3.4 %collective-permute-start.2 = (bf16[448,512]{1,0:T(8,128)(2,1)S(1)}, bf16[448,512]{1,0:T(8,128)(2,1)S(1)}, u32[]{:S(2)}, u32[]{:S(2)}) collective-permute-start(bf16[448,512]{1,0:T(8,128)(2,1)S(1)} %pad_maximum_fusion.2), channel_id=1, source_target_pairs={{0,128},{128,256},{256,384},{384,0},{1,129},{129,257},{257,385},{3... | collective-permute-start | bytes 1376264 | tf_op jit(solution)/shard_map/ppermute | solution.py:252
  101.7 3.1 %collective-permute-start.3 = (bf16[448,512]{1,0:T(8,128)(2,1)S(1)}, bf16[448,512]{1,0:T(8,128)(2,1)S(1)}, u32[]{:S(2)}, u32[]{:S(2)}) collective-permute-start(bf16[448,512]{1,0:T(8,128)(2,1)S(1)} %pad_maximum_fusion.2), channel_id=1, source_target_pairs={{0,256},{128,384},{256,0},{384,128},{1,257},{129,385},{257,1},{385... | collective-permute-start | bytes 1376264 | tf_op jit(solution)/shard_map/ppermute | solution.py:252
  104.8 4.0 %collective-permute-start.4 = (bf16[448,512]{1,0:T(8,128)(2,1)S(1)}, bf16[448,512]{1,0:T(8,128)(2,1)S(1)}, u32[]{:S(2)}, u32[]{:S(2)}) collective-permute-start(bf16[448,512]{1,0:T(8,128)(2,1)S(1)} %pad_maximum_fusion.2), channel_id=1, source_target_pairs={{0,384},{128,0},{256,128},{384,256},{1,385},{129,1},{257,129},{385... | collective-permute-start | bytes 1376264 | tf_op jit(solution)/shard_map/ppermute | solution.py:252
  109.0 3.6 %all-to-all-done.3.every_ref = f32[128,1,640]{2,1,0:T(1,128)S(1)} async-done(((f32[128,1,640]{2,1,0:T(1,128)}), f32[128,1,640]{2,1,0:T(1,128)S(1)}, u32[]{:S(2)}, u32[]{:S(2)}) %all-to-all-start.3) | async-done | bytes 327712 | tf_op jit(solution)/shard_map/all_to_all | solution.py:22
  112.5 0.7 copy-done.2
  113.3 2.0 %combine.1 = f32[4,1,384]{2,1,0:T(1,128)} custom-call(f32[128,1,640]{2,1,0:T(1,128)} %copy-done.2, f32[1,256]{1,0:T(1,128)} %bitcast.67), custom_call_target="tpu_custom_call" | custom-call | tf_op jit(solution)/shard_map/combine/pallas_call | solution.py:140
  115.3 4.8 %all-to-all-start.4 = ((f32[4,1,384]{2,1,0:T(1,128)}), f32[4,1,384]{2,1,0:T(1,128)S(1)}, u32[]{:S(2)}, u32[]{:S(2)}) async-start(f32[4,1,384]{2,1,0:T(1,128)} %combine.1), calls=%async_computation.4 | async-start | bytes 12288 | tf_op jit(solution)/shard_map/all_to_all | solution.py:256
  120.4 6.9 %collective-permute-done.4 = bf16[448,512]{1,0:T(8,128)(2,1)S(1)} collective-permute-done((bf16[448,512]{1,0:T(8,128)(2,1)S(1)}, bf16[448,512]{1,0:T(8,128)(2,1)S(1)}, u32[]{:S(2)}, u32[]{:S(2)}) %collective-permute-start.4) | collective-permute-done | bytes 458784 | tf_op jit(solution)/shard_map/ppermute | solution.py:252
  127.6 0.6 slice_reduce_fusion.1
  128.4 1.0 multiply_reduce_fusion
  130.9 0.5 fusion.3
  131.4 0.5 fusion.6
  132.0 1.9 %collective-permute-start.5 = (f32[520,256]{1,0:T(8,128)S(1)}, f32[520,256]{1,0:T(8,128)S(1)}, u32[]{:S(2)}, u32[]{:S(2)}) collective-permute-start(f32[520,256]{1,0:T(8,128)S(1)} %concatenate.29), channel_id=1, source_target_pairs={{0,1},{1,0},{2,3},{3,2},{4,5},{5,4},{6,7},{7,6},{8,9},{9,8},{10,11... | collective-permute-start | bytes 1597448 | tf_op jit(solution)/shard_map/ppermute | solution.py:297
  134.2 0.5 fusion.1
  134.7 0.5 fusion.7
  135.2 0.6 collective-permute-done.5
  136.0 0.9 pad_maximum_fusion.1
  137.0 12.9 %all-to-all-start.5 = ((f16[64,16,256]{2,1,0:T(8,128)(2,1)}), f16[64,16,256]{2,1,0:T(8,128)(2,1)S(1)}, u32[]{:S(2)}, u32[]{:S(2)}) async-start(f16[64,16,256]{2,1,0:T(8,128)(2,1)} %pad_maximum_fusion.1), calls=%async_computation.5 | async-start | bytes 1048576 | tf_op jit(solution)/shard_map/all_to_all | solution.py:306
  149.8 0.6 reduce_sum.148
  150.5 0.6 dynamic_slice.48
  151.7 0.7 iota_compare_fusion.16
  152.4 17.1 %all-to-all-done.5 = f16[64,16,256]{2,1,0:T(8,128)(2,1)S(1)} async-done(((f16[64,16,256]{2,1,0:T(8,128)(2,1)}), f16[64,16,256]{2,1,0:T(8,128)(2,1)S(1)}, u32[]{:S(2)}, u32[]{:S(2)}) %all-to-all-start.5) | async-done | bytes 524320 | tf_op jit(solution)/shard_map/all_to_all | solution.py:306
  169.6 0.6 slice_reduce_fusion
  170.3 0.7 multiply_reduce_fusion.1
  (68 shorter events, 4.4 us)
Async XLA Ops:
  7.2 52.1 %copy-start.1 = (bf16[512,512]{1,0:T(8,128)(2,1)S(1)}, bf16[512,512]{1,0:T(8,128)(2,1)}, u32[]{:S(2)}) copy-start(bf16[512,512]{1,0:T(8,128)(2,1)} %param.14) | copy-start | bytes 1572868
  7.2 69.2 %all-gather.2.cloned.1.call-start = ((), (), s32[]{:S(2)}) async-start(), calls=%async_computation.6 | async-start | bytes 2359296 | tf_op jit(solution)/shard_map/all_gather | solution.py:195
  33.7 19.4 %all-to-all-start.1 = ((bf16[8,128,128]{2,1,0:T(8,128)(2,1)}), bf16[8,128,128]{2,1,0:T(8,128)(2,1)S(1)}, u32[]{:S(2)}, u32[]{:S(2)}) async-start(bf16[8,128,128]{2,1,0:T(8,128)(2,1)} %broadcast_in_dim.215), calls=%async_computation.1 | async-start | bytes 524288 | tf_op jit(solution)/shard_map/all_to_all | solution.py:22
  53.1 0.7 copy-start.3
  56.2 4.2 %collective-permute-start = (bf16[2,256,128]{2,1,0:T(8,128)(2,1)}, bf16[2,256,128]{2,1,0:T(8,128)(2,1)S(1)}, u32[]{:S(2)}, u32[]{:S(2)}) collective-permute-start(bf16[2,256,128]{2,1,0:T(8,128)(2,1)} %get-tuple-element.14), channel_id=1, source_target_pairs={{0,1},{1,0},{2,3},{3,2},{4,5},{5,4},{6,7},{7,6},{8,9},{9,8},{10,11... | collective-permute-start | bytes 393224 | tf_op jit(solution)/shard_map/ppermute | solution.py:231
  60.6 21.8 %copy-start.5 = (s32[128]{0:T(128)S(1)}, s32[128]{0:T(128)}, u32[]{:S(2)}) copy-start(s32[128]{0:T(128)} %param.16) | copy-start | bytes 1540
  60.6 22.0 %copy-start.6 = (s32[512]{0:T(512)S(1)}, s32[512]{0:T(512)}, u32[]{:S(2)}) copy-start(s32[512]{0:T(512)} %param.17) | copy-start | bytes 6148
  80.2 6.4 %collective-permute-start.1 = (bf16[2,256,1024]{2,1,0:T(8,128)(2,1)}, bf16[2,256,1024]{2,1,0:T(8,128)(2,1)S(1)}, u32[]{:S(2)}, u32[]{:S(2)}) collective-permute-start(bf16[2,256,1024]{2,1,0:T(8,128)(2,1)} %pack_teacher.1), channel_id=1, source_target_pairs={{0,1},{1,0},{2,3},{3,2},{4,5},{5,4},{6,7},{7,6},{8,9},{9,8},{10,11... | collective-permute-start | bytes 3145736 | tf_op jit(solution)/shard_map/ppermute | solution.py:245
  82.6 4.0 %copy-start = (bf16[1,4096,512]{2,1,0:T(8,128)(2,1)S(1)}, bf16[1,4096,512]{2,1,0:T(8,128)(2,1)}, u32[]{:S(2)}) copy-start(bf16[1,4096,512]{2,1,0:T(8,128)(2,1)} %param.12) | copy-start | bytes 12582916
  87.6 25.0 %copy-start.4 = (f32[256]{0:T(256)}, f32[256]{0:T(256)S(1)}, u32[]{:S(2)}) copy-start(f32[256]{0:T(256)S(1)} %get-tuple-element.64) | copy-start | bytes 3076
  88.8 23.8 %all-to-all-start.3 = ((f32[128,1,640]{2,1,0:T(1,128)}), f32[128,1,640]{2,1,0:T(1,128)S(1)}, u32[]{:S(2)}, u32[]{:S(2)}) async-start(f32[128,1,640]{2,1,0:T(1,128)} %broadcast_in_dim.216), calls=%async_computation.3 | async-start | bytes 655360 | tf_op jit(solution)/shard_map/all_to_all | solution.py:22
  98.3 22.1 %collective-permute-start.2 = (bf16[448,512]{1,0:T(8,128)(2,1)S(1)}, bf16[448,512]{1,0:T(8,128)(2,1)S(1)}, u32[]{:S(2)}, u32[]{:S(2)}) collective-permute-start(bf16[448,512]{1,0:T(8,128)(2,1)S(1)} %pad_maximum_fusion.2), channel_id=1, source_target_pairs={{0,128},{128,256},{256,384},{384,0},{1,129},{129,257},{257,385},{3... | collective-permute-start | bytes 1376264 | tf_op jit(solution)/shard_map/ppermute | solution.py:252
  101.7 18.7 %collective-permute-start.3 = (bf16[448,512]{1,0:T(8,128)(2,1)S(1)}, bf16[448,512]{1,0:T(8,128)(2,1)S(1)}, u32[]{:S(2)}, u32[]{:S(2)}) collective-permute-start(bf16[448,512]{1,0:T(8,128)(2,1)S(1)} %pad_maximum_fusion.2), channel_id=1, source_target_pairs={{0,256},{128,384},{256,0},{384,128},{1,257},{129,385},{257,1},{385... | collective-permute-start | bytes 1376264 | tf_op jit(solution)/shard_map/ppermute | solution.py:252
  104.8 22.5 %collective-permute-start.4 = (bf16[448,512]{1,0:T(8,128)(2,1)S(1)}, bf16[448,512]{1,0:T(8,128)(2,1)S(1)}, u32[]{:S(2)}, u32[]{:S(2)}) collective-permute-start(bf16[448,512]{1,0:T(8,128)(2,1)S(1)} %pad_maximum_fusion.2), channel_id=1, source_target_pairs={{0,384},{128,0},{256,128},{384,256},{1,385},{129,1},{257,129},{385... | collective-permute-start | bytes 1376264 | tf_op jit(solution)/shard_map/ppermute | solution.py:252
  112.5 0.7 copy-start.2
  115.3 12.0 %all-to-all-start.4 = ((f32[4,1,384]{2,1,0:T(1,128)}), f32[4,1,384]{2,1,0:T(1,128)S(1)}, u32[]{:S(2)}, u32[]{:S(2)}) async-start(f32[4,1,384]{2,1,0:T(1,128)} %combine.1), calls=%async_computation.4 | async-start | bytes 12288 | tf_op jit(solution)/shard_map/all_to_all | solution.py:256
  131.9 20.4 %copy-start.7 = (s32[1,4]{1,0:T(1,128)S(1)}, s32[1,4]{1,0:T(1,128)}, u32[]{:S(2)}) copy-start(s32[1,4]{1,0:T(1,128)} %refs_0_.1) | copy-start | bytes 52
  132.0 3.8 %collective-permute-start.5 = (f32[520,256]{1,0:T(8,128)S(1)}, f32[520,256]{1,0:T(8,128)S(1)}, u32[]{:S(2)}, u32[]{:S(2)}) collective-permute-start(f32[520,256]{1,0:T(8,128)S(1)} %concatenate.29), channel_id=1, source_target_pairs={{0,1},{1,0},{2,3},{3,2},{4,5},{5,4},{6,7},{7,6},{8,9},{9,8},{10,11... | collective-permute-start | bytes 1597448 | tf_op jit(solution)/shard_map/ppermute | solution.py:297
  137.0 32.6 %all-to-all-start.5 = ((f16[64,16,256]{2,1,0:T(8,128)(2,1)}), f16[64,16,256]{2,1,0:T(8,128)(2,1)S(1)}, u32[]{:S(2)}, u32[]{:S(2)}) async-start(f16[64,16,256]{2,1,0:T(8,128)(2,1)} %pad_maximum_fusion.1), calls=%async_computation.5 | async-start | bytes 1048576 | tf_op jit(solution)/shard_map/all_to_all | solution.py:306
Sparse Core Ops, SparseCore 0:
  32.3 44.0 all-gather.1

commit v10 on v4

--- a/solution.py
+++ b/solution.py
@@ -13,6 +13,8 @@
 OWNERS = ("y", "z", "core")
 BF16 = jnp.bfloat16
 F32 = jnp.float32
+F16 = jnp.float16
+GRAD_STEP = 2.0**11
 
 
 def spread(block, axes, size):
@@ -106,8 +108,52 @@
             pl.BlockSpec((total, part), lambda i: (0, i)),
         ],
         out_specs=pl.BlockSpec((2, live, part), lambda i: (0, 0, i)),
+        cost_estimate=pl.CostEstimate(
+            flops=4 * live * total * features, bytes_accessed=8 << 20, transcendentals=0
+        ),
         name="pack_teacher",
     )(one, rows)
+
+
+def combine_kernel(every_ref, top_ref, sent_ref):
+    live = top_ref.shape[1]
+    chunk = (every_ref.shape[2] - 3 * live) // 4
+    copies = sent_ref.shape[0]
+
+    def scaled(first, count, sums):
+        tops = every_ref[:, :, first : first + count]
+        highest = jnp.max(tops, axis=0)
+        scales = jnp.exp(tops - highest[None])
+        starts = [first + (1 + index) * count for index in range(sums)]
+        return highest, [
+            jnp.sum(every_ref[:, :, start : start + count] * scales, axis=0) for start in starts
+        ]
+
+    highest, (total, cross) = scaled(0, live, 2)
+    factor = jnp.exp(top_ref[...] - highest) / total
+    crosses = jnp.sum(cross / total, axis=1, keepdims=True)
+    first = 3 * live
+    highest, (total,) = scaled(first, chunk, 1)
+    log_total = highest + jnp.log(total)
+    hits = jnp.sum(every_ref[:, :, first + 2 * chunk : first + 3 * chunk], axis=0)
+    loss = (
+        jnp.sum(log_total, axis=1, keepdims=True)
+        - BLEND * jnp.sum(hits, axis=1, keepdims=True)
+        - (1.0 - BLEND) / copies * crosses
+    )
+    tail = jnp.concatenate([log_total, jnp.broadcast_to(loss, (1, chunk))], axis=1)
+    for copy in range(copies):
+        sent_ref[copy, :, :live] = factor
+        sent_ref[copy, :, live:] = tail
+
+
+def combine(every, top, copies):
+    live = top.shape[0]
+    return pl.pallas_call(
+        combine_kernel,
+        out_shape=jax.ShapeDtypeStruct((copies, 1, live + 128), F32),
+        name="combine",
+    )(every, top[None])
 
 
 def softmax_stats(logits):
@@ -213,30 +259,11 @@
         for step in range(1, members)
     ]
     every = spread(jnp.concatenate([top, total, cross, student_stats])[None], OWNERS, owners)
-    every = every.reshape(owners, -1)
-    student_every = every[:, 3 * live_rows :]
-    student_tops = student_every[:, :chunk]
-    highest = jnp.max(student_tops, axis=0)
-    totals = jnp.sum(
-        student_every[:, chunk : 2 * chunk] * jnp.exp(student_tops - highest[None, :]), axis=0
-    )
-    log_chunk = highest + jnp.log(totals)
-    student_loss = jnp.sum(log_chunk) - BLEND * jnp.sum(
-        student_every[:, 2 * chunk : 3 * chunk]
-    )
-    tops = every[:, :live_rows]
-    highest = jnp.max(tops, axis=0)
-    scales = jnp.exp(tops - highest[None, :])
-    totals = jnp.sum(every[:, live_rows : 2 * live_rows] * scales, axis=0)
-    crosses = jnp.sum(every[:, 2 * live_rows : 3 * live_rows] * scales, axis=0)
-    factor = jnp.exp(top - highest) / totals
-    loss = student_loss - (1.0 - BLEND) / members * jnp.sum(crosses / totals)
-    factors = spread(
-        jnp.concatenate([factor, log_chunk, jnp.full((128 - chunk,), loss)]).reshape(-1, 128), "member", members
-    )
-    mean_loss = jnp.sum(factors[:, -1, chunk]) / jnp.sum(counts).astype(F32)
-    log_total = factors[:, -1, :chunk].reshape(live_rows)
-    factors = factors[:, :-1].reshape(members, live_rows)
+    factors = lax.all_to_all(combine(every, top, members), "member", 0, 0, tiled=True)
+    factors = factors.reshape(members, -1)
+    mean_loss = jnp.sum(factors[:, live_rows + chunk]) / jnp.sum(counts).astype(F32)
+    log_total = factors[:, live_rows : live_rows + chunk].reshape(live_rows)
+    factors = factors[:, :live_rows]
     ranks = jnp.arange(members, dtype=jnp.int32)[:, None]
     probs = 0.0
     for step in range(members):
@@ -264,9 +291,9 @@
         return result
 
     arrived = lax.ppermute(term(1 - core), "core", swap)
-    grads = (term(core) + arrived).astype(BF16).reshape(chips, 2 * cap, half)
+    grads = ((term(core) + arrived) * GRAD_STEP).astype(F16).reshape(chips, 2 * cap, half)
     owned = jnp.sum(lax.all_to_all(grads, CHIPS, 0, 0, tiled=True).astype(F32), axis=0)
-    slot_grad = jnp.concatenate([owned[:cap], owned[cap:]], axis=1)
+    slot_grad = jnp.concatenate([owned[:cap], owned[cap:]], axis=1) / GRAD_STEP
     live_here = slots < lax.dynamic_index_in_dim(counts, owner, keepdims=False)
     placed = (
         (jnp.arange(window, dtype=jnp.int32)[:, None] == slot_ids[None, :]) & live_here[None, :]

time: 178 us -> 176 us (0.989)
  Pallas kernels: 8.19 us -> 10.5 us
  other arithmetic: 9 us -> 6.89 us
  between operations: 19 us -> 17 us
    all_to_all x4 -> x3, waiting for transfers between devices: 31.5 us -> 27.6 us  [spread(): lax.all_to_all(jnp.broadcast_to(block[None], (size,) + block.shape), axes...]
    all_to_all x0 -> x1, waiting for transfers between devices: none -> 3.85 us  [on_device(): lax.all_to_all(combine(every, top, members), 'member', 0, 0, tiled=True)]
    all_to_all x4 -> x3, starting transfers between devices: 20.4 us -> 17.2 us  [spread(): lax.all_to_all(jnp.broadcast_to(block[None], (size,) + block.shape), axes...]
    all_to_all x0 -> x1, starting transfers between devices: none -> 3.25 us  [on_device(): lax.all_to_all(combine(every, top, members), 'member', 0, 0, tiled=True)]
    pallas_call x0 -> x1, Pallas kernels: none -> 2.36 us  [combine(): pl.pallas_call(combine_kernel, out_shape=jax.ShapeDtypeStruct((copies, 1,...]
  transfers between devices with their start and end apart: 13 -> 13, of which waited for: 7 -> 7; matrix products, arithmetic and copies ran while one was open for 12% -> 10% of each run, Pallas kernels for 1% -> 3%
where the time goes in v10:
time: 176 us; the launch traced here: 175 us
  waiting for transfers between devices  50.7 us (29%)
  starting transfers between devices  48.1 us (27%)
  blocking collectives  24.2 us (14%)
  between operations  17 us (10%)
  matrix products  10.8 us (6%)
  Pallas kernels  10.5 us (6%)
  local copies, waits for them, and re-layouts  6.97 us (4%)
  other arithmetic  6.89 us (4%)
    all_to_all x3, waiting for transfers between devices, spread(): lax.all_to_all(jnp.broadcast_to(block[None], (size,) + block.shape), axes...  27.6 us
    all_to_all x1, blocking collectives, on_device(): group_rows = lax.all_to_all(sent, ('z', 'core'), 0, 0, tiled=True)  24.2 us
    all_to_all x3, starting transfers between devices, spread(): lax.all_to_all(jnp.broadcast_to(block[None], (size,) + block.shape), axes...  17.2 us
    all_to_all x1, waiting for transfers between devices, on_device(): lax.all_to_all(grads, CHIPS, 0, 0, tiled=True).astype(F32)  9.48 us
    all_to_all x1, waiting for transfers between devices, on_device(): lax.all_to_all(partial_logits.reshape(members, chunk, vocab), 'member', 0...  8.93 us
    ppermute x3, starting transfers between devices, on_device(): lax.ppermute(shifted, 'member', [(i, (i + step) % members) for i in range...  8.41 us
    dot_general x8, matrix products, both_halves(): jnp.dot(values[side], lax.dynamic_slice_in_dim(weights, first + side * pa...  8.19 us
    ppermute x2, starting transfers between devices, on_device(): lax.ppermute(mine, 'core', swap)  5.41 us
  transfers between devices with their start and end apart: 13, of which 7 were waited for; matrix products, arithmetic and copies ran while one was open for 10% of the time, Pallas kernels for 3%

profile of v10, /device:TPU:1, one launch (start us, length us, event | category | flops | bytes accessed | tf_op | source)
XLA Modules:
  0.0 175.2 jit_solution(14893441961485777305)
XLA Ops:
  7.2 2.0 %own_rows.1 = bf16[128,1152]{1,0:T(8,128)(2,1)} custom-call(s32[1,4]{1,0:T(1,128)} %refs_0_.1, bf16[1,16,4096]{2,1,0:T(8,128)(2,1)} %refs_1_.1, f32[1,4096]{1,0:T(1,128)} %refs_2_.1, bf16[16,512]{1,0:T(8,128)(2,1)} %refs_3_.1), custom_call_target="tpu_custom_call" | custom-call | tf_op jit(solution)/shard_map/own_rows/pallas_call | solution.py:59
  9.2 24.2 %all_to_all.35 = bf16[16,8,1152]{2,1,0:T(8,128)(2,1)S(1)} all-to-all(bf16[16,8,1152]{2,1,0:T(8,128)(2,1)} %bitcast.75), channel_id=1, replica_groups=mesh['member'=4,'y'=8,'z'=8,'core'=2] {'z','core'}, dimensions={0} | all-to-all | bytes 589824 | tf_op jit(solution)/shard_map/all_to_all | solution.py:196
  33.4 0.7 slice.80
  34.1 0.8 select_reduce_fusion.2
  34.9 0.8 broadcast_in_dim.219
  35.7 6.8 %all-to-all-start.1 = ((bf16[8,128,128]{2,1,0:T(8,128)(2,1)}), bf16[8,128,128]{2,1,0:T(8,128)(2,1)S(1)}, u32[]{:S(2)}, u32[]{:S(2)}) async-start(bf16[8,128,128]{2,1,0:T(8,128)(2,1)} %broadcast_in_dim.219), calls=%async_computation.1 | async-start | bytes 524288 | tf_op jit(solution)/shard_map/all_to_all | solution.py:21
  42.5 0.8 add_select_fusion
  43.8 0.6 pad_add_fusion.places_ref
  44.4 12.7 %all-to-all-done.1 = bf16[8,128,128]{2,1,0:T(8,128)(2,1)S(1)} async-done(((bf16[8,128,128]{2,1,0:T(8,128)(2,1)}), bf16[8,128,128]{2,1,0:T(8,128)(2,1)S(1)}, u32[]{:S(2)}, u32[]{:S(2)}) %all-to-all-start.1) | async-done | bytes 262176 | tf_op jit(solution)/shard_map/all_to_all | solution.py:21
  57.1 0.7 copy-done.3
  57.8 2.4 %pack_student.1 = (bf16[2,256,128]{2,1,0:T(8,128)(2,1)}, bf16[2,256,1024]{2,1,0:T(8,128)(2,1)}) custom-call(s32[2,1024]{1,0:T(2,128)} %pad_add_fusion.places_ref, bf16[1024,128]{1,0:T(8,128)(2,1)} %bitcast.76), custom_call_target="tpu_custom_call" | custom-call | tf_op jit(solution)/shard_map/pack_student/pallas_call | solution.py:81
  60.2 2.4 %collective-permute-start = (bf16[2,256,128]{2,1,0:T(8,128)(2,1)}, bf16[2,256,128]{2,1,0:T(8,128)(2,1)S(1)}, u32[]{:S(2)}, u32[]{:S(2)}) collective-permute-start(bf16[2,256,128]{2,1,0:T(8,128)(2,1)} %get-tuple-element.8), channel_id=1, source_target_pairs={{0,1},{1,0},{2,3},{3,2},{4,5},{5,4},{6,7},{7,6},{8,9},{9,8},{10,11... | collective-permute-start | bytes 393224 | tf_op jit(solution)/shard_map/ppermute | solution.py:234
  62.6 1.2 fusion.46
  63.8 1.1 convolution_add_fusion.3
  65.1 1.0 fusion.5
  66.1 4.1 %all-to-all-start.2 = ((f32[4,64,512]{2,1,0:T(8,128)}), f32[4,64,512]{2,1,0:T(8,128)S(1)}, u32[]{:S(2)}, u32[]{:S(2)}) async-start(f32[4,64,512]{2,1,0:T(8,128)} %bitcast.7), calls=%async_computation.2 | async-start | bytes 1048576 | tf_op jit(solution)/shard_map/all_to_all | solution.py:236
  70.5 8.9 %all-to-all-done.2 = f32[4,64,512]{2,1,0:T(8,128)S(1)} async-done(((f32[4,64,512]{2,1,0:T(8,128)}), f32[4,64,512]{2,1,0:T(8,128)S(1)}, u32[]{:S(2)}, u32[]{:S(2)}) %all-to-all-start.2) | async-done | bytes 524320 | tf_op jit(solution)/shard_map/all_to_all | solution.py:236
  79.9 3.8 %pack_teacher.1 = bf16[2,256,1024]{2,1,0:T(8,128)(2,1)} custom-call(bf16[2,256,1024]{2,1,0:T(8,128)(2,1)} %get-tuple-element.7.one_ref, bf16[1024,1024]{1,0:T(8,128)(2,1)} %all-gather.2.cloned.1.call-done.rows_ref), custom_call_target="tpu_custom_call" | custom-call | flops 1073741824 | bytes 8388608 | tf_op jit(solution)/shard_map/pack_teacher/pallas_call | solution.py:102
  83.7 3.1 %collective-permute-start.1 = (bf16[2,256,1024]{2,1,0:T(8,128)(2,1)}, bf16[2,256,1024]{2,1,0:T(8,128)(2,1)S(1)}, u32[]{:S(2)}, u32[]{:S(2)}) collective-permute-start(bf16[2,256,1024]{2,1,0:T(8,128)(2,1)} %pack_teacher.1), channel_id=1, source_target_pairs={{0,1},{1,0},{2,3},{3,2},{4,5},{5,4},{6,7},{7,6},{8,9},{9,8},{10,11... | collective-permute-start | bytes 3145736 | tf_op jit(solution)/shard_map/ppermute | solution.py:253
  86.7 0.8 broadcast_in_dim.224
  87.6 3.5 %all-to-all-start.3 = ((f32[4,64,512]{2,1,0:T(8,128)}), f32[4,64,512]{2,1,0:T(8,128)S(1)}, u32[]{:S(2)}, u32[]{:S(2)}) async-start(f32[4,64,512]{2,1,0:T(8,128)} %broadcast_in_dim.224), calls=%async_computation.3 | async-start | bytes 1048576 | tf_op jit(solution)/shard_map/all_to_all | solution.py:21
  91.1 2.0 %fusion.16 = f32[256,512]{1,0:T(8,128)S(1)} fusion(bf16[1,4096,512]{2,1,0:T(8,128)(2,1)} %param.12, s32[]{:T(128)S(6)} %select_n.181, bf16[2,256,1024]{2,1,0:T(8,128)(2,1)} %pack_teacher.1), kind=kOutput, calls=%fused_computation.24 | convolution fusion | flops 268435456 | bytes 2097156 | tf_op jit(solution)/shard_map/dot_general | solution.py:224
  93.1 1.8 %convolution_add_fusion.1 = f32[256,512]{1,0:T(8,128)S(1)} fusion(f32[256,512]{1,0:T(8,128)S(1)} %fusion.16, bf16[1,4096,512]{2,1,0:T(8,128)(2,1)} %param.12, s32[]{:T(128)S(6)} %select_n.182, bf16[2,256,1024]{2,1,0:T(8,128)(2,1)} %pack_teacher.1), kind=kOutput, calls=%fused_computation.5 | convolution fusion | flops 268566528 | bytes 2621444 | tf_op jit(solution)/shard_map/dot_general | solution.py:224
  95.4 0.5 fusion.63
  95.9 4.8 %all-to-all-done.3 = f32[4,64,512]{2,1,0:T(8,128)S(1)} async-done(((f32[4,64,512]{2,1,0:T(8,128)}), f32[4,64,512]{2,1,0:T(8,128)S(1)}, u32[]{:S(2)}, u32[]{:S(2)}) %all-to-all-start.3) | async-done | bytes 524320 | tf_op jit(solution)/shard_map/all_to_all | solution.py:21
  101.0 1.1 broadcast_in_dim.225
  102.0 6.9 %all-to-all-start.4 = ((f32[128,1,1024]{2,1,0:T(1,128)}), f32[128,1,1024]{2,1,0:T(1,128)S(1)}, u32[]{:S(2)}, u32[]{:S(2)}) async-start(f32[128,1,1024]{2,1,0:T(1,128)} %broadcast_in_dim.225), calls=%async_computation.4 | async-start | bytes 1048576 | tf_op jit(solution)/shard_map/all_to_all | solution.py:21
  109.7 2.2 %collective-permute-start.2 = (bf16[256,512]{1,0:T(8,128)(2,1)S(1)}, bf16[256,512]{1,0:T(8,128)(2,1)S(1)}, u32[]{:S(2)}, u32[]{:S(2)}) collective-permute-start(bf16[256,512]{1,0:T(8,128)(2,1)S(1)} %get-tuple-element.30), channel_id=1, source_target_pairs={{0,128},{128,256},{256,384},{384,0},{1,129},{129,257},{257,385},{3... | collective-permute-start | bytes 786440 | tf_op jit(solution)/shard_map/ppermute | solution.py:258
  111.9 3.7 %collective-permute-start.3 = (bf16[256,512]{1,0:T(8,128)(2,1)S(1)}, bf16[256,512]{1,0:T(8,128)(2,1)S(1)}, u32[]{:S(2)}, u32[]{:S(2)}) collective-permute-start(bf16[256,512]{1,0:T(8,128)(2,1)S(1)} %get-tuple-element.30), channel_id=1, source_target_pairs={{0,256},{128,384},{256,0},{384,128},{1,257},{129,385},{257,1},{385... | collective-permute-start | bytes 786440 | tf_op jit(solution)/shard_map/ppermute | solution.py:258
  115.6 2.5 %collective-permute-start.4 = (bf16[256,512]{1,0:T(8,128)(2,1)S(1)}, bf16[256,512]{1,0:T(8,128)(2,1)S(1)}, u32[]{:S(2)}, u32[]{:S(2)}) collective-permute-start(bf16[256,512]{1,0:T(8,128)(2,1)S(1)} %get-tuple-element.30), channel_id=1, source_target_pairs={{0,384},{128,0},{256,128},{384,256},{1,385},{129,1},{257,129},{385... | collective-permute-start | bytes 786440 | tf_op jit(solution)/shard_map/ppermute | solution.py:258
  118.2 10.2 %all-to-all-done.4.every_ref = f32[128,1,1024]{2,1,0:T(1,128)S(1)} async-done(((f32[128,1,1024]{2,1,0:T(1,128)}), f32[128,1,1024]{2,1,0:T(1,128)S(1)}, u32[]{:S(2)}, u32[]{:S(2)}) %all-to-all-start.4) | async-done | bytes 524320 | tf_op jit(solution)/shard_map/all_to_all | solution.py:21
  128.4 0.8 copy-done.1
  129.2 2.4 %combine.1 = f32[4,1,384]{2,1,0:T(1,128)} custom-call(f32[128,1,1024]{2,1,0:T(1,128)} %copy-done.1, f32[1,256]{1,0:T(1,128)} %bitcast.82), custom_call_target="tpu_custom_call" | custom-call | tf_op jit(solution)/shard_map/combine/pallas_call | solution.py:152
  131.5 3.2 %all-to-all-start.5 = ((f32[4,1,384]{2,1,0:T(1,128)}), f32[4,1,384]{2,1,0:T(1,128)S(1)}, u32[]{:S(2)}, u32[]{:S(2)}) async-start(f32[4,1,384]{2,1,0:T(1,128)} %combine.1), calls=%async_computation.5 | async-start | bytes 12288 | tf_op jit(solution)/shard_map/all_to_all | solution.py:262
  135.1 3.8 %all-to-all-done.5 = f32[4,1,384]{2,1,0:T(1,128)S(1)} async-done(((f32[4,1,384]{2,1,0:T(1,128)}), f32[4,1,384]{2,1,0:T(1,128)S(1)}, u32[]{:S(2)}, u32[]{:S(2)}) %all-to-all-start.5) | async-done | bytes 6176 | tf_op jit(solution)/shard_map/all_to_all | solution.py:262
  139.6 0.5 fusion.3
  140.1 0.5 fusion.6
  140.6 5.1 %collective-permute-start.5 = (f32[512,256]{1,0:T(8,128)S(1)}, f32[512,256]{1,0:T(8,128)S(1)}, u32[]{:S(2)}, u32[]{:S(2)}) collective-permute-start(f32[512,256]{1,0:T(8,128)S(1)} %fusion.6), channel_id=1, source_target_pairs={{0,1},{1,0},{2,3},{3,2},{4,5},{5,4},{6,7},{7,6},{8,9},{9,8},{10,11... | collective-permute-start | bytes 1572872 | tf_op jit(solution)/shard_map/ppermute | solution.py:293
  145.9 0.5 fusion.1
  146.4 0.8 collective-permute-done.5
  147.2 1.2 fusion.11
  148.4 4.6 %all-to-all-start.6 = ((f16[64,8,256]{2,1,0:T(8,128)(2,1)}), f16[64,8,256]{2,1,0:T(8,128)(2,1)S(1)}, u32[]{:S(2)}, u32[]{:S(2)}) async-start(f16[64,8,256]{2,1,0:T(8,128)(2,1)} %fusion.11), calls=%async_computation.6 | async-start | bytes 524288 | tf_op jit(solution)/shard_map/all_to_all | solution.py:295
  153.0 0.6 reduce_sum.143
  153.6 0.6 dynamic_slice.52
  154.9 0.7 iota_compare_fusion.20
  155.6 0.7 slice_reduce_fusion
  156.9 9.5 %all-to-all-done.6 = f16[64,8,256]{2,1,0:T(8,128)(2,1)S(1)} async-done(((f16[64,8,256]{2,1,0:T(8,128)(2,1)}), f16[64,8,256]{2,1,0:T(8,128)(2,1)S(1)}, u32[]{:S(2)}, u32[]{:S(2)}) %all-to-all-start.6) | async-done | bytes 262176 | tf_op jit(solution)/shard_map/all_to_all | solution.py:295
  166.5 0.7 multiply_reduce_fusion
  (60 shorter events, 4.3 us)
Async XLA Ops:
  7.2 56.6 %copy-start.2 = (bf16[512,512]{1,0:T(8,128)(2,1)S(1)}, bf16[512,512]{1,0:T(8,128)(2,1)}, u32[]{:S(2)}) copy-start(bf16[512,512]{1,0:T(8,128)(2,1)} %param.14) | copy-start | bytes 1572868
  7.2 72.7 %all-gather.2.cloned.1.call-start = ((), (), s32[]{:S(2)}) async-start(), calls=%async_computation.7 | async-start | bytes 2359296 | tf_op jit(solution)/shard_map/all_gather | solution.py:198
  33.4 36.9 %copy-start.6 = (s32[512]{0:T(512)S(1)}, s32[512]{0:T(512)}, u32[]{:S(2)}) copy-start(s32[512]{0:T(512)} %param.17) | copy-start | bytes 6148
  35.7 21.4 %all-to-all-start.1 = ((bf16[8,128,128]{2,1,0:T(8,128)(2,1)}), bf16[8,128,128]{2,1,0:T(8,128)(2,1)S(1)}, u32[]{:S(2)}, u32[]{:S(2)}) async-start(bf16[8,128,128]{2,1,0:T(8,128)(2,1)} %broadcast_in_dim.219), calls=%async_computation.1 | async-start | bytes 524288 | tf_op jit(solution)/shard_map/all_to_all | solution.py:21
  57.1 0.7 copy-start.3
  60.2 4.6 %collective-permute-start = (bf16[2,256,128]{2,1,0:T(8,128)(2,1)}, bf16[2,256,128]{2,1,0:T(8,128)(2,1)S(1)}, u32[]{:S(2)}, u32[]{:S(2)}) collective-permute-start(bf16[2,256,128]{2,1,0:T(8,128)(2,1)} %get-tuple-element.8), channel_id=1, source_target_pairs={{0,1},{1,0},{2,3},{3,2},{4,5},{5,4},{6,7},{7,6},{8,9},{9,8},{10,11... | collective-permute-start | bytes 393224 | tf_op jit(solution)/shard_map/ppermute | solution.py:234
  66.1 13.3 %all-to-all-start.2 = ((f32[4,64,512]{2,1,0:T(8,128)}), f32[4,64,512]{2,1,0:T(8,128)S(1)}, u32[]{:S(2)}, u32[]{:S(2)}) async-start(f32[4,64,512]{2,1,0:T(8,128)} %bitcast.7), calls=%async_computation.2 | async-start | bytes 1048576 | tf_op jit(solution)/shard_map/all_to_all | solution.py:236
  83.7 11.2 %collective-permute-start.1 = (bf16[2,256,1024]{2,1,0:T(8,128)(2,1)}, bf16[2,256,1024]{2,1,0:T(8,128)(2,1)S(1)}, u32[]{:S(2)}, u32[]{:S(2)}) collective-permute-start(bf16[2,256,1024]{2,1,0:T(8,128)(2,1)} %pack_teacher.1), channel_id=1, source_target_pairs={{0,1},{1,0},{2,3},{3,2},{4,5},{5,4},{6,7},{7,6},{8,9},{9,8},{10,11... | collective-permute-start | bytes 3145736 | tf_op jit(solution)/shard_map/ppermute | solution.py:253
  87.6 13.1 %all-to-all-start.3 = ((f32[4,64,512]{2,1,0:T(8,128)}), f32[4,64,512]{2,1,0:T(8,128)S(1)}, u32[]{:S(2)}, u32[]{:S(2)}) async-start(f32[4,64,512]{2,1,0:T(8,128)} %broadcast_in_dim.224), calls=%async_computation.3 | async-start | bytes 1048576 | tf_op jit(solution)/shard_map/all_to_all | solution.py:21
  91.1 3.9 %copy-start = (bf16[1,4096,512]{2,1,0:T(8,128)(2,1)S(1)}, bf16[1,4096,512]{2,1,0:T(8,128)(2,1)}, u32[]{:S(2)}) copy-start(bf16[1,4096,512]{2,1,0:T(8,128)(2,1)} %param.12) | copy-start | bytes 12582916
  94.9 14.2 %copy-start.5 = (s32[128]{0:T(128)S(1)}, s32[128]{0:T(128)}, u32[]{:S(2)}) copy-start(s32[128]{0:T(128)} %param.16) | copy-start | bytes 1540
  95.9 32.5 %copy-start.4 = (f32[256]{0:T(256)}, f32[256]{0:T(256)S(1)}, u32[]{:S(2)}) copy-start(f32[256]{0:T(256)S(1)} %get-tuple-element.43) | copy-start | bytes 3076
  102.0 26.4 %all-to-all-start.4 = ((f32[128,1,1024]{2,1,0:T(1,128)}), f32[128,1,1024]{2,1,0:T(1,128)S(1)}, u32[]{:S(2)}, u32[]{:S(2)}) async-start(f32[128,1,1024]{2,1,0:T(1,128)} %broadcast_in_dim.225), calls=%async_computation.4 | async-start | bytes 1048576 | tf_op jit(solution)/shard_map/all_to_all | solution.py:21
  109.7 29.4 %collective-permute-start.2 = (bf16[256,512]{1,0:T(8,128)(2,1)S(1)}, bf16[256,512]{1,0:T(8,128)(2,1)S(1)}, u32[]{:S(2)}, u32[]{:S(2)}) collective-permute-start(bf16[256,512]{1,0:T(8,128)(2,1)S(1)} %get-tuple-element.30), channel_id=1, source_target_pairs={{0,128},{128,256},{256,384},{384,0},{1,129},{129,257},{257,385},{3... | collective-permute-start | bytes 786440 | tf_op jit(solution)/shard_map/ppermute | solution.py:258
  111.9 27.2 %collective-permute-start.3 = (bf16[256,512]{1,0:T(8,128)(2,1)S(1)}, bf16[256,512]{1,0:T(8,128)(2,1)S(1)}, u32[]{:S(2)}, u32[]{:S(2)}) collective-permute-start(bf16[256,512]{1,0:T(8,128)(2,1)S(1)} %get-tuple-element.30), channel_id=1, source_target_pairs={{0,256},{128,384},{256,0},{384,128},{1,257},{129,385},{257,1},{385... | collective-permute-start | bytes 786440 | tf_op jit(solution)/shard_map/ppermute | solution.py:258
  115.6 23.5 %collective-permute-start.4 = (bf16[256,512]{1,0:T(8,128)(2,1)S(1)}, bf16[256,512]{1,0:T(8,128)(2,1)S(1)}, u32[]{:S(2)}, u32[]{:S(2)}) collective-permute-start(bf16[256,512]{1,0:T(8,128)(2,1)S(1)} %get-tuple-element.30), channel_id=1, source_target_pairs={{0,384},{128,0},{256,128},{384,256},{1,385},{129,1},{257,129},{385... | collective-permute-start | bytes 786440 | tf_op jit(solution)/shard_map/ppermute | solution.py:258
  128.4 0.8 copy-start.1
  131.5 7.4 %all-to-all-start.5 = ((f32[4,1,384]{2,1,0:T(1,128)}), f32[4,1,384]{2,1,0:T(1,128)S(1)}, u32[]{:S(2)}, u32[]{:S(2)}) async-start(f32[4,1,384]{2,1,0:T(1,128)} %combine.1), calls=%async_computation.5 | async-start | bytes 12288 | tf_op jit(solution)/shard_map/all_to_all | solution.py:262
  139.1 16.4 %copy-start.7 = (s32[1,4]{1,0:T(1,128)S(1)}, s32[1,4]{1,0:T(1,128)}, u32[]{:S(2)}) copy-start(s32[1,4]{1,0:T(1,128)} %refs_0_.1) | copy-start | bytes 52
  140.6 6.6 %collective-permute-start.5 = (f32[512,256]{1,0:T(8,128)S(1)}, f32[512,256]{1,0:T(8,128)S(1)}, u32[]{:S(2)}, u32[]{:S(2)}) collective-permute-start(f32[512,256]{1,0:T(8,128)S(1)} %fusion.6), channel_id=1, source_target_pairs={{0,1},{1,0},{2,3},{3,2},{4,5},{5,4},{6,7},{7,6},{8,9},{9,8},{10,11... | collective-permute-start | bytes 1572872 | tf_op jit(solution)/shard_map/ppermute | solution.py:293
  148.4 18.0 %all-to-all-start.6 = ((f16[64,8,256]{2,1,0:T(8,128)(2,1)}), f16[64,8,256]{2,1,0:T(8,128)(2,1)S(1)}, u32[]{:S(2)}, u32[]{:S(2)}) async-start(f16[64,8,256]{2,1,0:T(8,128)(2,1)} %fusion.11), calls=%async_computation.6 | async-start | bytes 524288 | tf_op jit(solution)/shard_map/all_to_all | solution.py:295
Sparse Core Ops, SparseCore 0:
  34.3 40.4 all-gather.1

commit v11 on v10

--- a/solution.py
+++ b/solution.py
@@ -117,7 +117,7 @@
 
 def combine_kernel(every_ref, top_ref, sent_ref):
     live = top_ref.shape[1]
-    chunk = (every_ref.shape[2] - 3 * live) // 4
+    chunk = (every_ref.shape[2] - 3 * live) // 3
     copies = sent_ref.shape[0]
 
     def scaled(first, count, sums):
@@ -246,10 +246,10 @@
         live_targets, member * chunk, chunk
     )[:, None]
     target_part = jnp.sum(jnp.where(hit_chunk, logits_chunk, 0.0), axis=1)
-    student_stats = jnp.concatenate([top, total, target_part, jnp.zeros_like(top)])
+    student_stats = jnp.concatenate([top, total, target_part])
 
     teacher_rows, student_stats = lax.optimization_barrier((teacher_rows, student_stats))
-    mine = pack_rows(one, teacher_rows, 2)
+    mine = pack_rows(one, teacher_rows, 4)
     teacher_logits = both_halves(mine, lax.ppermute(mine, "core", swap), teacher_head[0])
     top, shifted, total = softmax_stats(teacher_logits)
     cross = jnp.sum(shifted * student_logits, axis=1)

time: 176 us -> 177 us (level)
  no operation moved by 1% of the time
where the time goes in v11:
time: 177 us; the launch traced here: 176 us
  waiting for transfers between devices  50.7 us (29%)
  starting transfers between devices  48.1 us (27%)
  blocking collectives  24.2 us (14%)
  between operations  17 us (10%)
  Pallas kernels  11.6 us (7%)
  matrix products  10.8 us (6%)
  local copies, waits for them, and re-layouts  6.96 us (4%)
  other arithmetic  6.89 us (4%)
    all_to_all x3, waiting for transfers between devices, spread(): lax.all_to_all(jnp.broadcast_to(block[None], (size,) + block.shape), axes...  27.6 us
    all_to_all x1, blocking collectives, on_device(): group_rows = lax.all_to_all(sent, ('z', 'core'), 0, 0, tiled=True)  24.2 us
    all_to_all x3, starting transfers between devices, spread(): lax.all_to_all(jnp.broadcast_to(block[None], (size,) + block.shape), axes...  17.2 us
    all_to_all x1, waiting for transfers between devices, on_device(): lax.all_to_all(grads, CHIPS, 0, 0, tiled=True).astype(F32)  9.49 us
    all_to_all x1, waiting for transfers between devices, on_device(): lax.all_to_all(partial_logits.reshape(members, chunk, vocab), 'member', 0...  8.93 us
    ppermute x3, starting transfers between devices, on_device(): lax.ppermute(shifted, 'member', [(i, (i + step) % members) for i in range...  8.41 us
    dot_general x8, matrix products, both_halves(): jnp.dot(values[side], lax.dynamic_slice_in_dim(weights, first + side * pa...  8.19 us
    ppermute x2, starting transfers between devices, on_device(): lax.ppermute(mine, 'core', swap)  5.41 us
  transfers between devices with their start and end apart: 13, of which 7 were waited for; matrix products, arithmetic and copies ran while one was open for 10% of the time, Pallas kernels for 3%

profile of v11, /device:TPU:1, one launch (start us, length us, event | category | flops | bytes accessed | tf_op | source)
XLA Modules:
  0.0 176.2 jit_solution(17473270875043332578)
XLA Ops:
  7.2 2.0 %own_rows.1 = bf16[128,1152]{1,0:T(8,128)(2,1)} custom-call(s32[1,4]{1,0:T(1,128)} %refs_0_.1, bf16[1,16,4096]{2,1,0:T(8,128)(2,1)} %refs_1_.1, f32[1,4096]{1,0:T(1,128)} %refs_2_.1, bf16[16,512]{1,0:T(8,128)(2,1)} %refs_3_.1), custom_call_target="tpu_custom_call" | custom-call | tf_op jit(solution)/shard_map/own_rows/pallas_call | solution.py:59
  9.2 24.2 %all_to_all.35 = bf16[16,8,1152]{2,1,0:T(8,128)(2,1)S(1)} all-to-all(bf16[16,8,1152]{2,1,0:T(8,128)(2,1)} %bitcast.75), channel_id=1, replica_groups=mesh['member'=4,'y'=8,'z'=8,'core'=2] {'z','core'}, dimensions={0} | all-to-all | bytes 589824 | tf_op jit(solution)/shard_map/all_to_all | solution.py:196
  33.4 0.7 slice.80
  34.1 0.8 select_reduce_fusion.2
  34.9 0.8 broadcast_in_dim.216
  35.7 6.8 %all-to-all-start.1 = ((bf16[8,128,128]{2,1,0:T(8,128)(2,1)}), bf16[8,128,128]{2,1,0:T(8,128)(2,1)S(1)}, u32[]{:S(2)}, u32[]{:S(2)}) async-start(bf16[8,128,128]{2,1,0:T(8,128)(2,1)} %broadcast_in_dim.216), calls=%async_computation.1 | async-start | bytes 524288 | tf_op jit(solution)/shard_map/all_to_all | solution.py:21
  42.5 0.8 add_select_fusion
  43.8 0.6 pad_add_fusion.places_ref
  44.4 12.7 %all-to-all-done.1 = bf16[8,128,128]{2,1,0:T(8,128)(2,1)S(1)} async-done(((bf16[8,128,128]{2,1,0:T(8,128)(2,1)}), bf16[8,128,128]{2,1,0:T(8,128)(2,1)S(1)}, u32[]{:S(2)}, u32[]{:S(2)}) %all-to-all-start.1) | async-done | bytes 262176 | tf_op jit(solution)/shard_map/all_to_all | solution.py:21
  57.1 0.7 copy-done.3
  57.8 2.4 %pack_student.1 = (bf16[2,256,128]{2,1,0:T(8,128)(2,1)}, bf16[2,256,1024]{2,1,0:T(8,128)(2,1)}) custom-call(s32[2,1024]{1,0:T(2,128)} %pad_add_fusion.places_ref, bf16[1024,128]{1,0:T(8,128)(2,1)} %bitcast.76), custom_call_target="tpu_custom_call" | custom-call | tf_op jit(solution)/shard_map/pack_student/pallas_call | solution.py:81
  60.2 2.4 %collective-permute-start = (bf16[2,256,128]{2,1,0:T(8,128)(2,1)}, bf16[2,256,128]{2,1,0:T(8,128)(2,1)S(1)}, u32[]{:S(2)}, u32[]{:S(2)}) collective-permute-start(bf16[2,256,128]{2,1,0:T(8,128)(2,1)} %get-tuple-element.8), channel_id=1, source_target_pairs={{0,1},{1,0},{2,3},{3,2},{4,5},{5,4},{6,7},{7,6},{8,9},{9,8},{10,11... | collective-permute-start | bytes 393224 | tf_op jit(solution)/shard_map/ppermute | solution.py:234
  62.6 1.2 fusion.46
  63.8 1.1 convolution_add_fusion.3
  65.1 1.0 fusion.5
  66.1 4.1 %all-to-all-start.2 = ((f32[4,64,512]{2,1,0:T(8,128)}), f32[4,64,512]{2,1,0:T(8,128)S(1)}, u32[]{:S(2)}, u32[]{:S(2)}) async-start(f32[4,64,512]{2,1,0:T(8,128)} %bitcast.7), calls=%async_computation.2 | async-start | bytes 1048576 | tf_op jit(solution)/shard_map/all_to_all | solution.py:236
  70.5 8.9 %all-to-all-done.2 = f32[4,64,512]{2,1,0:T(8,128)S(1)} async-done(((f32[4,64,512]{2,1,0:T(8,128)}), f32[4,64,512]{2,1,0:T(8,128)S(1)}, u32[]{:S(2)}, u32[]{:S(2)}) %all-to-all-start.2) | async-done | bytes 524320 | tf_op jit(solution)/shard_map/all_to_all | solution.py:236
  79.9 4.8 %pack_teacher.1 = bf16[2,256,1024]{2,1,0:T(8,128)(2,1)} custom-call(bf16[2,256,1024]{2,1,0:T(8,128)(2,1)} %get-tuple-element.7.one_ref, bf16[1024,1024]{1,0:T(8,128)(2,1)} %all-gather.2.cloned.1.call-done.rows_ref), custom_call_target="tpu_custom_call" | custom-call | flops 1073741824 | bytes 8388608 | tf_op jit(solution)/shard_map/pack_teacher/pallas_call | solution.py:102
  84.7 3.1 %collective-permute-start.1 = (bf16[2,256,1024]{2,1,0:T(8,128)(2,1)}, bf16[2,256,1024]{2,1,0:T(8,128)(2,1)S(1)}, u32[]{:S(2)}, u32[]{:S(2)}) collective-permute-start(bf16[2,256,1024]{2,1,0:T(8,128)(2,1)} %pack_teacher.1), channel_id=1, source_target_pairs={{0,1},{1,0},{2,3},{3,2},{4,5},{5,4},{6,7},{7,6},{8,9},{9,8},{10,11... | collective-permute-start | bytes 3145736 | tf_op jit(solution)/shard_map/ppermute | solution.py:253
  87.7 0.8 broadcast_in_dim.220
  88.6 3.5 %all-to-all-start.3 = ((f32[4,64,512]{2,1,0:T(8,128)}), f32[4,64,512]{2,1,0:T(8,128)S(1)}, u32[]{:S(2)}, u32[]{:S(2)}) async-start(f32[4,64,512]{2,1,0:T(8,128)} %broadcast_in_dim.220), calls=%async_computation.3 | async-start | bytes 1048576 | tf_op jit(solution)/shard_map/all_to_all | solution.py:21
  92.1 2.0 %fusion.16 = f32[256,512]{1,0:T(8,128)S(1)} fusion(bf16[1,4096,512]{2,1,0:T(8,128)(2,1)} %param.12, s32[]{:T(128)S(6)} %select_n.181, bf16[2,256,1024]{2,1,0:T(8,128)(2,1)} %pack_teacher.1), kind=kOutput, calls=%fused_computation.24 | convolution fusion | flops 268435456 | bytes 2097156 | tf_op jit(solution)/shard_map/dot_general | solution.py:224
  94.1 1.8 %convolution_add_fusion.1 = f32[256,512]{1,0:T(8,128)S(1)} fusion(f32[256,512]{1,0:T(8,128)S(1)} %fusion.16, bf16[1,4096,512]{2,1,0:T(8,128)(2,1)} %param.12, s32[]{:T(128)S(6)} %select_n.182, bf16[2,256,1024]{2,1,0:T(8,128)(2,1)} %pack_teacher.1), kind=kOutput, calls=%fused_computation.5 | convolution fusion | flops 268566528 | bytes 2621444 | tf_op jit(solution)/shard_map/dot_general | solution.py:224
  96.4 0.5 fusion.63
  96.9 4.8 %all-to-all-done.3 = f32[4,64,512]{2,1,0:T(8,128)S(1)} async-done(((f32[4,64,512]{2,1,0:T(8,128)}), f32[4,64,512]{2,1,0:T(8,128)S(1)}, u32[]{:S(2)}, u32[]{:S(2)}) %all-to-all-start.3) | async-done | bytes 524320 | tf_op jit(solution)/shard_map/all_to_all | solution.py:21
  102.0 1.1 broadcast_in_dim.221
  103.0 6.9 %all-to-all-start.4 = ((f32[128,1,960]{2,1,0:T(1,128)}), f32[128,1,960]{2,1,0:T(1,128)S(1)}, u32[]{:S(2)}, u32[]{:S(2)}) async-start(f32[128,1,960]{2,1,0:T(1,128)} %broadcast_in_dim.221), calls=%async_computation.4 | async-start | bytes 1048576 | tf_op jit(solution)/shard_map/all_to_all | solution.py:21
  110.7 2.2 %collective-permute-start.2 = (bf16[256,512]{1,0:T(8,128)(2,1)S(1)}, bf16[256,512]{1,0:T(8,128)(2,1)S(1)}, u32[]{:S(2)}, u32[]{:S(2)}) collective-permute-start(bf16[256,512]{1,0:T(8,128)(2,1)S(1)} %get-tuple-element.30), channel_id=1, source_target_pairs={{0,128},{128,256},{256,384},{384,0},{1,129},{129,257},{257,385},{3... | collective-permute-start | bytes 786440 | tf_op jit(solution)/shard_map/ppermute | solution.py:258
  112.9 3.7 %collective-permute-start.3 = (bf16[256,512]{1,0:T(8,128)(2,1)S(1)}, bf16[256,512]{1,0:T(8,128)(2,1)S(1)}, u32[]{:S(2)}, u32[]{:S(2)}) collective-permute-start(bf16[256,512]{1,0:T(8,128)(2,1)S(1)} %get-tuple-element.30), channel_id=1, source_target_pairs={{0,256},{128,384},{256,0},{384,128},{1,257},{129,385},{257,1},{385... | collective-permute-start | bytes 786440 | tf_op jit(solution)/shard_map/ppermute | solution.py:258
  116.6 2.5 %collective-permute-start.4 = (bf16[256,512]{1,0:T(8,128)(2,1)S(1)}, bf16[256,512]{1,0:T(8,128)(2,1)S(1)}, u32[]{:S(2)}, u32[]{:S(2)}) collective-permute-start(bf16[256,512]{1,0:T(8,128)(2,1)S(1)} %get-tuple-element.30), channel_id=1, source_target_pairs={{0,384},{128,0},{256,128},{384,256},{1,385},{129,1},{257,129},{385... | collective-permute-start | bytes 786440 | tf_op jit(solution)/shard_map/ppermute | solution.py:258
  119.2 10.2 %all-to-all-done.4.every_ref = f32[128,1,960]{2,1,0:T(1,128)S(1)} async-done(((f32[128,1,960]{2,1,0:T(1,128)}), f32[128,1,960]{2,1,0:T(1,128)S(1)}, u32[]{:S(2)}, u32[]{:S(2)}) %all-to-all-start.4) | async-done | bytes 491552 | tf_op jit(solution)/shard_map/all_to_all | solution.py:21
  129.4 0.8 copy-done.1
  130.2 2.4 %combine.1 = f32[4,1,384]{2,1,0:T(1,128)} custom-call(f32[128,1,960]{2,1,0:T(1,128)} %copy-done.1, f32[1,256]{1,0:T(1,128)} %bitcast.82), custom_call_target="tpu_custom_call" | custom-call | tf_op jit(solution)/shard_map/combine/pallas_call | solution.py:152
  132.5 3.2 %all-to-all-start.5 = ((f32[4,1,384]{2,1,0:T(1,128)}), f32[4,1,384]{2,1,0:T(1,128)S(1)}, u32[]{:S(2)}, u32[]{:S(2)}) async-start(f32[4,1,384]{2,1,0:T(1,128)} %combine.1), calls=%async_computation.5 | async-start | bytes 12288 | tf_op jit(solution)/shard_map/all_to_all | solution.py:262
  136.1 3.8 %all-to-all-done.5 = f32[4,1,384]{2,1,0:T(1,128)S(1)} async-done(((f32[4,1,384]{2,1,0:T(1,128)}), f32[4,1,384]{2,1,0:T(1,128)S(1)}, u32[]{:S(2)}, u32[]{:S(2)}) %all-to-all-start.5) | async-done | bytes 6176 | tf_op jit(solution)/shard_map/all_to_all | solution.py:262
  140.6 0.5 fusion.3
  141.1 0.5 fusion.6
  141.6 5.1 %collective-permute-start.5 = (f32[512,256]{1,0:T(8,128)S(1)}, f32[512,256]{1,0:T(8,128)S(1)}, u32[]{:S(2)}, u32[]{:S(2)}) collective-permute-start(f32[512,256]{1,0:T(8,128)S(1)} %fusion.6), channel_id=1, source_target_pairs={{0,1},{1,0},{2,3},{3,2},{4,5},{5,4},{6,7},{7,6},{8,9},{9,8},{10,11... | collective-permute-start | bytes 1572872 | tf_op jit(solution)/shard_map/ppermute | solution.py:293
  146.9 0.5 fusion.1
  147.4 0.8 collective-permute-done.5
  148.2 1.2 fusion.11
  149.4 4.6 %all-to-all-start.6 = ((f16[64,8,256]{2,1,0:T(8,128)(2,1)}), f16[64,8,256]{2,1,0:T(8,128)(2,1)S(1)}, u32[]{:S(2)}, u32[]{:S(2)}) async-start(f16[64,8,256]{2,1,0:T(8,128)(2,1)} %fusion.11), calls=%async_computation.6 | async-start | bytes 524288 | tf_op jit(solution)/shard_map/all_to_all | solution.py:295
  154.0 0.6 reduce_sum.143
  154.6 0.6 dynamic_slice.52
  155.9 0.7 iota_compare_fusion.20
  156.6 0.7 slice_reduce_fusion
  158.0 9.5 %all-to-all-done.6 = f16[64,8,256]{2,1,0:T(8,128)(2,1)S(1)} async-done(((f16[64,8,256]{2,1,0:T(8,128)(2,1)}), f16[64,8,256]{2,1,0:T(8,128)(2,1)S(1)}, u32[]{:S(2)}, u32[]{:S(2)}) %all-to-all-start.6) | async-done | bytes 262176 | tf_op jit(solution)/shard_map/all_to_all | solution.py:295
  167.5 0.7 multiply_reduce_fusion
  (59 shorter events, 4.3 us)
Async XLA Ops:
  7.2 56.6 %copy-start.2 = (bf16[512,512]{1,0:T(8,128)(2,1)S(1)}, bf16[512,512]{1,0:T(8,128)(2,1)}, u32[]{:S(2)}) copy-start(bf16[512,512]{1,0:T(8,128)(2,1)} %param.14) | copy-start | bytes 1572868
  7.2 72.7 %all-gather.2.cloned.1.call-start = ((), (), s32[]{:S(2)}) async-start(), calls=%async_computation.7 | async-start | bytes 2359296 | tf_op jit(solution)/shard_map/all_gather | solution.py:198
  33.4 36.9 %copy-start.6 = (s32[512]{0:T(512)S(1)}, s32[512]{0:T(512)}, u32[]{:S(2)}) copy-start(s32[512]{0:T(512)} %param.17) | copy-start | bytes 6148
  35.7 21.4 %all-to-all-start.1 = ((bf16[8,128,128]{2,1,0:T(8,128)(2,1)}), bf16[8,128,128]{2,1,0:T(8,128)(2,1)S(1)}, u32[]{:S(2)}, u32[]{:S(2)}) async-start(bf16[8,128,128]{2,1,0:T(8,128)(2,1)} %broadcast_in_dim.216), calls=%async_computation.1 | async-start | bytes 524288 | tf_op jit(solution)/shard_map/all_to_all | solution.py:21
  57.1 0.7 copy-start.3
  60.2 4.6 %collective-permute-start = (bf16[2,256,128]{2,1,0:T(8,128)(2,1)}, bf16[2,256,128]{2,1,0:T(8,128)(2,1)S(1)}, u32[]{:S(2)}, u32[]{:S(2)}) collective-permute-start(bf16[2,256,128]{2,1,0:T(8,128)(2,1)} %get-tuple-element.8), channel_id=1, source_target_pairs={{0,1},{1,0},{2,3},{3,2},{4,5},{5,4},{6,7},{7,6},{8,9},{9,8},{10,11... | collective-permute-start | bytes 393224 | tf_op jit(solution)/shard_map/ppermute | solution.py:234
  66.1 13.3 %all-to-all-start.2 = ((f32[4,64,512]{2,1,0:T(8,128)}), f32[4,64,512]{2,1,0:T(8,128)S(1)}, u32[]{:S(2)}, u32[]{:S(2)}) async-start(f32[4,64,512]{2,1,0:T(8,128)} %bitcast.7), calls=%async_computation.2 | async-start | bytes 1048576 | tf_op jit(solution)/shard_map/all_to_all | solution.py:236
  84.7 11.2 %collective-permute-start.1 = (bf16[2,256,1024]{2,1,0:T(8,128)(2,1)}, bf16[2,256,1024]{2,1,0:T(8,128)(2,1)S(1)}, u32[]{:S(2)}, u32[]{:S(2)}) collective-permute-start(bf16[2,256,1024]{2,1,0:T(8,128)(2,1)} %pack_teacher.1), channel_id=1, source_target_pairs={{0,1},{1,0},{2,3},{3,2},{4,5},{5,4},{6,7},{7,6},{8,9},{9,8},{10,11... | collective-permute-start | bytes 3145736 | tf_op jit(solution)/shard_map/ppermute | solution.py:253
  88.6 13.1 %all-to-all-start.3 = ((f32[4,64,512]{2,1,0:T(8,128)}), f32[4,64,512]{2,1,0:T(8,128)S(1)}, u32[]{:S(2)}, u32[]{:S(2)}) async-start(f32[4,64,512]{2,1,0:T(8,128)} %broadcast_in_dim.220), calls=%async_computation.3 | async-start | bytes 1048576 | tf_op jit(solution)/shard_map/all_to_all | solution.py:21
  92.1 3.9 %copy-start = (bf16[1,4096,512]{2,1,0:T(8,128)(2,1)S(1)}, bf16[1,4096,512]{2,1,0:T(8,128)(2,1)}, u32[]{:S(2)}) copy-start(bf16[1,4096,512]{2,1,0:T(8,128)(2,1)} %param.12) | copy-start | bytes 12582916
  95.9 14.2 %copy-start.5 = (s32[128]{0:T(128)S(1)}, s32[128]{0:T(128)}, u32[]{:S(2)}) copy-start(s32[128]{0:T(128)} %param.16) | copy-start | bytes 1540
  96.9 32.5 %copy-start.4 = (f32[256]{0:T(256)}, f32[256]{0:T(256)S(1)}, u32[]{:S(2)}) copy-start(f32[256]{0:T(256)S(1)} %get-tuple-element.43) | copy-start | bytes 3076
  103.0 26.4 %all-to-all-start.4 = ((f32[128,1,960]{2,1,0:T(1,128)}), f32[128,1,960]{2,1,0:T(1,128)S(1)}, u32[]{:S(2)}, u32[]{:S(2)}) async-start(f32[128,1,960]{2,1,0:T(1,128)} %broadcast_in_dim.221), calls=%async_computation.4 | async-start | bytes 1048576 | tf_op jit(solution)/shard_map/all_to_all | solution.py:21
  110.7 29.4 %collective-permute-start.2 = (bf16[256,512]{1,0:T(8,128)(2,1)S(1)}, bf16[256,512]{1,0:T(8,128)(2,1)S(1)}, u32[]{:S(2)}, u32[]{:S(2)}) collective-permute-start(bf16[256,512]{1,0:T(8,128)(2,1)S(1)} %get-tuple-element.30), channel_id=1, source_target_pairs={{0,128},{128,256},{256,384},{384,0},{1,129},{129,257},{257,385},{3... | collective-permute-start | bytes 786440 | tf_op jit(solution)/shard_map/ppermute | solution.py:258
  112.9 27.2 %collective-permute-start.3 = (bf16[256,512]{1,0:T(8,128)(2,1)S(1)}, bf16[256,512]{1,0:T(8,128)(2,1)S(1)}, u32[]{:S(2)}, u32[]{:S(2)}) collective-permute-start(bf16[256,512]{1,0:T(8,128)(2,1)S(1)} %get-tuple-element.30), channel_id=1, source_target_pairs={{0,256},{128,384},{256,0},{384,128},{1,257},{129,385},{257,1},{385... | collective-permute-start | bytes 786440 | tf_op jit(solution)/shard_map/ppermute | solution.py:258
  116.6 23.5 %collective-permute-start.4 = (bf16[256,512]{1,0:T(8,128)(2,1)S(1)}, bf16[256,512]{1,0:T(8,128)(2,1)S(1)}, u32[]{:S(2)}, u32[]{:S(2)}) collective-permute-start(bf16[256,512]{1,0:T(8,128)(2,1)S(1)} %get-tuple-element.30), channel_id=1, source_target_pairs={{0,384},{128,0},{256,128},{384,256},{1,385},{129,1},{257,129},{385... | collective-permute-start | bytes 786440 | tf_op jit(solution)/shard_map/ppermute | solution.py:258
  129.4 0.8 copy-start.1
  132.5 7.4 %all-to-all-start.5 = ((f32[4,1,384]{2,1,0:T(1,128)}), f32[4,1,384]{2,1,0:T(1,128)S(1)}, u32[]{:S(2)}, u32[]{:S(2)}) async-start(f32[4,1,384]{2,1,0:T(1,128)} %combine.1), calls=%async_computation.5 | async-start | bytes 12288 | tf_op jit(solution)/shard_map/all_to_all | solution.py:262
  140.1 16.4 %copy-start.7 = (s32[1,4]{1,0:T(1,128)S(1)}, s32[1,4]{1,0:T(1,128)}, u32[]{:S(2)}) copy-start(s32[1,4]{1,0:T(1,128)} %refs_0_.1) | copy-start | bytes 52
  141.6 6.6 %collective-permute-start.5 = (f32[512,256]{1,0:T(8,128)S(1)}, f32[512,256]{1,0:T(8,128)S(1)}, u32[]{:S(2)}, u32[]{:S(2)}) collective-permute-start(f32[512,256]{1,0:T(8,128)S(1)} %fusion.6), channel_id=1, source_target_pairs={{0,1},{1,0},{2,3},{3,2},{4,5},{5,4},{6,7},{7,6},{8,9},{9,8},{10,11... | collective-permute-start | bytes 1572872 | tf_op jit(solution)/shard_map/ppermute | solution.py:293
  149.4 18.1 %all-to-all-start.6 = ((f16[64,8,256]{2,1,0:T(8,128)(2,1)}), f16[64,8,256]{2,1,0:T(8,128)(2,1)S(1)}, u32[]{:S(2)}, u32[]{:S(2)}) async-start(f16[64,8,256]{2,1,0:T(8,128)(2,1)} %fusion.11), calls=%async_computation.6 | async-start | bytes 524288 | tf_op jit(solution)/shard_map/all_to_all | solution.py:295
Sparse Core Ops, SparseCore 0:
  34.3 40.4 all-gather.1
